TPU v7x, 32 devices: a whole 2x2x4 slice. The times are simulated.
32 devices in a mesh: groups: 2 (over y), hid: 8 (over z, x), row: 2 (over core).
Axes of the slice: x: 2, y: 2, z: 4, core: 2. Of those that a mesh axis runs over, the one named last changes fastest.
Arguments:
- gate_proj: bfloat16 [32, 32768], P(('groups', 'row'), 'hid'), parts along dimension 0, may hold values from -6 to 6
- up_proj: bfloat16 [32, 32768], P(('groups', 'row'), 'hid'), parts along dimension 0, may hold values from -6 to 6
- hadamard_signs: int32 [32768], P('hid'), may hold values from 0 to 1
- down_codes: bfloat16 [32768, 8192], P('hid', 'row'), may hold values from -127 to 127, as said below
- down_scales: int32 [8192], P('row'), may hold values from 128 to 1279
- residual: bfloat16 [32, 8192], P(('groups', 'hid'), 'row'), parts along dimension 0, may hold values from -16 to 16
- norm_gain: bfloat16 [8192], P('row'), may hold values from 0.099609375 to 1.8984375
- qkv_codes: bfloat16 [8192, 18432], P('row', 'hid'), may hold values from -127 to 127, as said below
- qkv_scales: int32 [18432], P('hid'), may hold values from 128 to 1279
Outputs:
- new_stream: bfloat16 [32, 8192], P(('groups', 'hid'), 'row'), parts along dimension 0
- joined_qkv: bfloat16 [32, 18432], P(('groups', 'row'), 'hid'), parts along dimension 0
There are 2 independent parts, one for each index of `groups`. A program takes and returns all parts, laid end to end along the dimension named above; an argument that names none is the same for every part. Nothing has to cross between parts.
Inputs may be any that keep to these rules, and one draw needn't show every extreme that they name: `down_codes`: every entry is a whole number. `qkv_codes`: every entry is a whole number.
All inputs are finite; a program needn't handle non-finite values.
Results may differ from a plain program's by a relative error of at most 0.0062.
Values may be sent and summed in bfloat16 or wider, within the bound.
No kernel may reach another device: no remote copies, remote signals or barrier semaphores. Data moves between devices by JAX's collectives and lax.ppermute only.
A program may use at most 128 MiB of HBM per device.

v0:
```python
import math

import jax
import jax.numpy as jnp
from jax import lax
from jax.sharding import PartitionSpec as P

epsilon = 1e-05


def partner_2(block, axis, bit):
    count = lax.axis_size(axis)
    route = []
    for low in range(count):
        high = low | 1 << bit
        if high != low and high < count:
            route += [(low, high), (high, low)]
    return lax.ppermute(block, axis, route)


def sylvester(order_size):
    row_index = lax.broadcasted_iota(jnp.int32, (order_size, order_size), 0)
    column_index = lax.broadcasted_iota(jnp.int32, (order_size, order_size), 1)
    result = jnp.ones((order_size, order_size), jnp.float32)
    for bit_number in range(order_size.bit_length() - 1):
        both_set = row_index // 2**bit_number % 2 * (column_index // 2**bit_number % 2)
        result = result * (1.0 - 2.0 * both_set.astype(jnp.float32))
    return result


def factor_list(length):
    factors = []
    remain = length
    while remain > 1:
        factor = min(remain, 128)
        factors.append(factor)
        remain = remain // factor
    return factors


def transform_axis(values, order_size, axis_place):
    product_moved = jnp.tensordot(
        values, sylvester(order_size), axes=([axis_place], [0]), precision=lax.Precision.HIGHEST
    )
    return jnp.moveaxis(product_moved, -1, axis_place)


def transform_last(values):
    factors = factor_list(values.shape[-1])
    leading = values.shape[:-1]
    shaped = values.reshape(leading + tuple(factors))
    for offset, order_size in enumerate(factors):
        shaped = transform_axis(shaped, order_size, len(leading) + offset)
    return shaped.reshape(values.shape)


def body(
    gate_proj,
    up_proj,
    hadamard_signs,
    down_codes,
    down_scales,
    residual,
    norm_gain,
    qkv_codes,
    qkv_scales,
):
    hidden = (jax.nn.silu(gate_proj.astype(jnp.float32)) * up_proj.astype(jnp.float32)).astype(
        jnp.bfloat16
    )
    flips = (1 - 2 * hadamard_signs).astype(jnp.bfloat16)
    signed = hidden * flips[None, :]
    groups = lax.axis_size("hid")
    local_rows, local_width = signed.shape
    norm_factor = 1.0 / math.sqrt(local_width * groups)
    mixed = transform_last(signed.astype(jnp.float32))
    position = lax.axis_index("hid")
    for bit_number in range(groups.bit_length() - 1):
        partner = partner_2(mixed, "hid", bit_number)
        upper_half = position // 2**bit_number % 2 == 1
        mixed = jnp.where(upper_half, partner - mixed, mixed + partner)
    rotated = (mixed * norm_factor).astype(jnp.bfloat16)
    partial_value = jnp.dot(
        lax.all_gather(rotated, "row", axis=0, tiled=True),
        down_codes,
        preferred_element_type=jnp.float32,
    )
    column_scale = (down_scales.astype(jnp.float32) * 2.0 ** (-23))[None, :]
    own_rows = residual.shape[0]
    every_residual = lax.all_gather(residual, "hid", axis=0, tiled=True)
    summed = lax.psum(partial_value, "hid")
    stream_all = (every_residual.astype(jnp.float32) + summed * column_scale).astype(jnp.bfloat16)
    new_stream = lax.dynamic_slice_in_dim(stream_all, lax.axis_index("hid") * own_rows, own_rows, 0)
    stream_wide = stream_all.astype(jnp.float32)
    scaled_rows = (stream_wide * norm_gain.astype(jnp.float32)[None, :]).astype(jnp.bfloat16)
    squares = jnp.sum(stream_wide * stream_wide, axis=1)
    out_rows = stream_all.shape[0] // lax.axis_size("row")
    full_width = stream_all.shape[1] * lax.axis_size("row")
    projected = lax.psum_scatter(
        jnp.dot(scaled_rows, qkv_codes, preferred_element_type=jnp.float32),
        "row",
        scatter_dimension=0,
        tiled=True,
    )
    all_squares = lax.psum(squares, "row")
    row_squares = lax.dynamic_slice_in_dim(
        all_squares, lax.axis_index("row") * out_rows, out_rows, 0
    )
    inverse = lax.rsqrt(row_squares / full_width + epsilon)
    output_scale = (qkv_scales.astype(jnp.float32) * 2.0 ** (-22))[None, :]
    joined_qkv = (projected * inverse[:, None] * output_scale).astype(jnp.bfloat16)
    return (new_stream, joined_qkv)


def solution(mesh):
    return jax.shard_map(
        body,
        mesh=mesh,
        in_specs=(
            P(("groups", "row"), "hid"),
            P(("groups", "row"), "hid"),
            P("hid"),
            P("hid", "row"),
            P("row"),
            P(("groups", "hid"), "row"),
            P("row"),
            P("row", "hid"),
            P("hid"),
        ),
        out_specs=(P(("groups", "hid"), "row"), P(("groups", "row"), "hid")),
        check_vma=False,
    )
```

profile of v0, /device:TPU:0, one launch (start us, length us, event | category | flops | bytes accessed | tf_op | source)
XLA Modules:
  0.0 144.0 jit_solution(14292946847741064035)
XLA Ops:
  7.2 0.0 copy-start
  7.2 0.0 copy-start.2
  7.2 0.0 copy-start.1
  7.2 0.0 all-reduce.2.cloned.1.call-start
  7.4 0.7 subtract_convert_fusion
  8.1 0.9 fusion.68
  9.1 0.2 reshape.15
  9.3 0.7 convolution_bitcast_fusion
  10.0 1.1 fusion.161
  11.0 0.2 reshape.16
  11.3 3.0 %collective-permute-start = (f32[8,4096]{1,0:T(8,128)S(1)}, f32[8,4096]{1,0:T(8,128)S(1)}, u32[]{:S(2)}, u32[]{:S(2)}) collective-permute-start(f32[8,4096]{1,0:T(8,128)S(1)} %reshape.16), channel_id=1, source_target_pairs={{0,2},{2,0},{4,6},{6,4},{8,10},{10,8},{12,14},{14,12},{1,3},{3,1},... | collective-permute-start | bytes 393224 | tf_op jit(solution)/shard_map/ppermute | solution.py:18
  14.3 3.5 %collective-permute-done = f32[8,4096]{1,0:T(8,128)S(1)} collective-permute-done((f32[8,4096]{1,0:T(8,128)S(1)}, f32[8,4096]{1,0:T(8,128)S(1)}, u32[]{:S(2)}, u32[]{:S(2)}) %collective-permute-start) | collective-permute-done | bytes 131104 | tf_op jit(solution)/shard_map/ppermute | solution.py:18
  17.8 1.9 %collective-permute-start.1 = (f32[8,4096]{1,0:T(8,128)S(1)}, f32[8,4096]{1,0:T(8,128)S(1)}, u32[]{:S(2)}, u32[]{:S(2)}) collective-permute-start(f32[8,4096]{1,0:T(8,128)S(1)} %add_select_fusion.1), channel_id=1, source_target_pairs={{0,4},{4,0},{2,6},{6,2},{8,12},{12,8},{10,14},{14,10},{1,5},{5,1},... | collective-permute-start | bytes 393224 | tf_op jit(solution)/shard_map/ppermute | solution.py:18
  19.7 3.1 %collective-permute-done.1 = f32[8,4096]{1,0:T(8,128)S(1)} collective-permute-done((f32[8,4096]{1,0:T(8,128)S(1)}, f32[8,4096]{1,0:T(8,128)S(1)}, u32[]{:S(2)}, u32[]{:S(2)}) %collective-permute-start.1) | collective-permute-done | bytes 131104 | tf_op jit(solution)/shard_map/ppermute | solution.py:18
  22.9 2.9 %collective-permute-start.2 = (f32[8,4096]{1,0:T(8,128)S(1)}, f32[8,4096]{1,0:T(8,128)S(1)}, u32[]{:S(2)}, u32[]{:S(2)}) collective-permute-start(f32[8,4096]{1,0:T(8,128)S(1)} %add_select_fusion), channel_id=1, source_target_pairs={{0,8},{8,0},{2,10},{10,2},{4,12},{12,4},{6,14},{14,6},{1,9},{9,1},... | collective-permute-start | bytes 393224 | tf_op jit(solution)/shard_map/ppermute | solution.py:18
  25.8 0.7 convert_multiply_fusion.4
  26.5 3.7 %collective-permute-done.2 = f32[8,4096]{1,0:T(8,128)S(1)} collective-permute-done((f32[8,4096]{1,0:T(8,128)S(1)}, f32[8,4096]{1,0:T(8,128)S(1)}, u32[]{:S(2)}, u32[]{:S(2)}) %collective-permute-start.2) | collective-permute-done | bytes 131104 | tf_op jit(solution)/shard_map/ppermute | solution.py:18
  30.2 1.9 %all_gather.7 = bf16[16,4096]{1,0:T(8,128)(2,1)S(1)} all-gather(bf16[8,4096]{1,0:T(8,128)(2,1)S(1)} %multiply_convert_fusion), channel_id=1, replica_groups=mesh['groups'=2,'hid'=8,'row'=2] {'row'}, dimensions={0}, use_global_device_ids=true | all-gather | bytes 196608 | tf_op jit(solution)/shard_map/all_gather | solution.py:84
  32.1 13.5 %fusion.266 = f32[16,4096]{1,0:T(8,128)} fusion(bf16[16,4096]{1,0:T(8,128)(2,1)S(1)} %all_gather.7, bf16[4096,4096]{1,0:T(8,128)(2,1)} %param.12), kind=kOutput, calls=%fused_computation.410 | convolution fusion | flops 536870912 | bytes 33947648 | tf_op jit(solution)/shard_map/dot_general | solution.py:83
  45.6 0.0 all-reduce.2.cloned.1.call-update
  45.7 0.0 reduce-scatter.2.cloned.1.call-start
  45.7 0.0 copy-done
  45.7 31.0 %all-gather = bf16[8,2,4096]{2,1,0:T(2,128)(2,1)S(1)} all-gather(bf16[1,2,4096]{2,1,0:T(2,128)(2,1)S(1)} %bitcast.14), channel_id=1, replica_groups=mesh['groups'=2,'hid'=8,'row'=2] {'hid'}, dimensions={0}, use_global_device_ids=true | all-gather | bytes 147456 | tf_op jit(solution)/shard_map/all_gather | solution.py:90
  76.8 41.0 %all-reduce.2.cloned.1.call-done = f32[16,4096]{1,0:T(8,128)} async-done(((f32[16,4096]{1,0:T(8,128)}), f32[16,4096]{1,0:T(8,128)}) %all-reduce.2.cloned.1.call-update) | async-done | bytes 262160 | tf_op jit(solution)/shard_map/psum | solution.py:91
  117.9 1.1 fusion.1
  119.0 9.6 %fusion.6 = f32[16,2304]{1,0:T(8,128)} fusion(bf16[4096,2304]{1,0:T(8,128)(2,1)} %param.16, bf16[16,4096]{1,0:T(8,128)(2,1)S(1)} %get-tuple-element.3, f32[4096]{0:T(1024)S(1)} %convert_element_type.97), kind=kOutput, calls=%fused_computation.12 | convolution fusion | flops 302186496 | bytes 19169280 | tf_op jit(solution)/shard_map/dot_general | solution.py:100
  128.6 0.0 reduce-scatter.2.cloned.1.call-update
  128.6 2.5 %psum.15 = f32[16]{0:T(128)S(1)} all-reduce(f32[16]{0:T(128)S(1)} %get-tuple-element.2), channel_id=1, replica_groups=mesh['groups'=2,'hid'=8,'row'=2] {'row'}, use_global_device_ids=true, to_apply=%region_3.4 | all-reduce | flops 16 | bytes 128 | tf_op jit(solution)/shard_map/psum | solution.py:105
  131.1 0.1 add_rsqrt_fusion
  131.1 0.6 constant_dynamic-slice_fusion
  131.8 3.8 %reduce-scatter.2.cloned.1.call-done = f32[8,2304]{1,0:T(8,128)} async-done(((f32[16,2304]{1,0:T(8,128)}), f32[8,2304]{1,0:T(8,128)}) %reduce-scatter.2.cloned.1.call-update) | async-done | bytes 73744 | tf_op jit(solution)/shard_map/reduce_scatter | solution.py:99
  135.6 1.6 %multiply_convert_fusion.1 = bf16[8,2304]{1,0:T(8,128)(2,1)} fusion(f32[8,2304]{1,0:T(8,128)} %reduce-scatter.2.cloned.1.call-done, f32[2304]{0:T(1024)S(1)} %convert_multiply_fusion.4, f32[8]{0:T(128)S(1)} %add_rsqrt_fusion), kind=kLoop, calls=%fused_computation.80 | loop fusion | flops 55296 | bytes 119840 | tf_op jit(solution)/shard_map/convert_element_type | solution.py:111
  (23 shorter events, 0.2 us)
Async XLA Ops:
  7.2 38.6 %copy-start = (bf16[2,4096]{1,0:T(2,128)(2,1)S(1)}, bf16[2,4096]{1,0:T(2,128)(2,1)}, u32[]{:S(2)}) copy-start(bf16[2,4096]{1,0:T(2,128)(2,1)} %param.14) | copy-start | bytes 49156
  7.2 69.6 %copy-start.2 = (bf16[4096]{0:T(1024)(128)(2,1)S(1)}, bf16[4096]{0:T(1024)(128)(2,1)}, u32[]{:S(2)}) copy-start(bf16[4096]{0:T(1024)(128)(2,1)} %param.15) | copy-start | bytes 24580
  7.2 69.6 %copy-start.1 = (s32[4096]{0:T(1024)S(1)}, s32[4096]{0:T(1024)}, u32[]{:S(2)}) copy-start(s32[4096]{0:T(1024)} %param.13) | copy-start | bytes 49156
  7.2 110.7 %all-reduce.2.cloned.1.call-start = ((), (), s32[]{:S(2)}) async-start(), calls=%async_computation.1 | async-start | bytes 524288 | tf_op jit(solution)/shard_map/psum | solution.py:91
  11.3 6.5 %collective-permute-start = (f32[8,4096]{1,0:T(8,128)S(1)}, f32[8,4096]{1,0:T(8,128)S(1)}, u32[]{:S(2)}, u32[]{:S(2)}) collective-permute-start(f32[8,4096]{1,0:T(8,128)S(1)} %reshape.16), channel_id=1, source_target_pairs={{0,2},{2,0},{4,6},{6,4},{8,10},{10,8},{12,14},{14,12},{1,3},{3,1},... | collective-permute-start | bytes 393224 | tf_op jit(solution)/shard_map/ppermute | solution.py:18
  17.8 5.0 %collective-permute-start.1 = (f32[8,4096]{1,0:T(8,128)S(1)}, f32[8,4096]{1,0:T(8,128)S(1)}, u32[]{:S(2)}, u32[]{:S(2)}) collective-permute-start(f32[8,4096]{1,0:T(8,128)S(1)} %add_select_fusion.1), channel_id=1, source_target_pairs={{0,4},{4,0},{2,6},{6,2},{8,12},{12,8},{10,14},{14,10},{1,5},{5,1},... | collective-permute-start | bytes 393224 | tf_op jit(solution)/shard_map/ppermute | solution.py:18
  22.9 7.3 %collective-permute-start.2 = (f32[8,4096]{1,0:T(8,128)S(1)}, f32[8,4096]{1,0:T(8,128)S(1)}, u32[]{:S(2)}, u32[]{:S(2)}) collective-permute-start(f32[8,4096]{1,0:T(8,128)S(1)} %add_select_fusion), channel_id=1, source_target_pairs={{0,8},{8,0},{2,10},{10,2},{4,12},{12,4},{6,14},{14,6},{1,9},{9,1},... | collective-permute-start | bytes 393224 | tf_op jit(solution)/shard_map/ppermute | solution.py:18
  45.7 89.9 %reduce-scatter.2.cloned.1.call-start = ((), (), s32[]{:S(2)}) async-start(), calls=%async_computation.2 | async-start | bytes 221184 | tf_op jit(solution)/shard_map/reduce_scatter | solution.py:99
Sparse Core Ops, SparseCore 0:
  45.8 72.0 all-reduce.1
  128.7 6.8 reduce-scatter.1
where the time goes:
time: 144 us
  waiting for transfers between devices  55.2 us (38%)
  blocking collectives  35.4 us (25%)
  matrix products  24.9 us (17%)
  between operations  14.2 us (10%)
  starting transfers between devices  7.88 us (5%)
  other arithmetic  5.27 us (4%)
    psum x1, waiting for transfers between devices, body(): summed = lax.psum(partial_value, 'hid')  41 us
    all_gather x1, blocking collectives, body(): every_residual = lax.all_gather(residual, 'hid', axis=0, tiled=True)  31 us
    dot_general x1, matrix products, body(): jnp.dot(lax.all_gather(rotated, 'row', axis=0, tiled=True), down_codes, p...  13.5 us
    ppermute x3, waiting for transfers between devices, partner_2(): return lax.ppermute(block, axis, route)  10.4 us
    dot_general x1, matrix products, body(): jnp.dot(scaled_rows, qkv_codes, preferred_element_type=jnp.float32)  9.57 us
    ppermute x3, starting transfers between devices, partner_2(): return lax.ppermute(block, axis, route)  7.8 us
    reduce_scatter x1, waiting for transfers between devices, body(): lax.psum_scatter(jnp.dot(scaled_rows, qkv_codes, preferred_element_type=j...  3.8 us
  transfers between devices with their start and end apart: 5, of which 5 were waited for; matrix products, arithmetic and copies ran while one was open for 1% of the time, Pallas kernels for 0%

commit v1 on v0

v1 whole, which is shorter than its diff:
```python
import math

import jax
import jax.numpy as jnp
from jax import lax
from jax.experimental import pallas as pl
from jax.experimental.pallas import tpu as pltpu
from jax.sharding import PartitionSpec as P

epsilon = 1e-05
lanes = 128
VMEM = pl.BlockSpec(memory_space=pltpu.VMEM)
f32, bf16 = jnp.float32, jnp.bfloat16


def exchange(block, axis, distance):
    count = lax.axis_size(axis)
    return lax.ppermute(block, axis, [(i, i ^ distance) for i in range(count)])


def bit_of(axis, distance):
    return lax.axis_index(axis) // distance % 2


def params(mib):
    return pltpu.CompilerParams(vmem_limit_bytes=mib << 20)


def cost(flops, nbytes):
    return pl.CostEstimate(flops=flops, bytes_accessed=nbytes, transcendentals=0)


def tile_of(width):
    return 256 if width % 256 == 0 else 128


def signed_kernel(gate_ref, up_ref, sign_ref, out_ref):
    gate = gate_ref[...].astype(f32)
    hidden = (gate / (1.0 + jnp.exp(-gate)) * up_ref[...].astype(f32)).astype(bf16)
    flips = (1 - 2 * sign_ref[...]).astype(f32)
    out_ref[...] = (hidden.astype(f32) * flips).astype(bf16)


def signed_units(gate, up, signs):
    return pl.pallas_call(
        signed_kernel,
        out_shape=jax.ShapeDtypeStruct(gate.shape, bf16),
        in_specs=[VMEM] * 3,
        out_specs=VMEM,
        compiler_params=params(4),
        cost_estimate=cost(0, 40 << 20),
        name="signed_units",
    )(gate, up, signs.reshape(1, -1))


def hadamard_128():
    both = lax.broadcasted_iota(jnp.int32, (lanes, lanes), 0) & lax.broadcasted_iota(
        jnp.int32, (lanes, lanes), 1
    )
    for shift in (4, 2, 1):
        both = both ^ (both >> shift)
    return (1 - 2 * (both & 1)).astype(f32).astype(bf16)


def mix_kernel(own_ref, other_ref, wide_ref, send_ref):
    rows, width = own_ref.shape
    matrix = hadamard_128()
    upper = bit_of("hid", 1) == 1
    own, other = own_ref[...].astype(f32), other_ref[...].astype(f32)
    stacked = jnp.concatenate([other, own], axis=0).astype(bf16)
    blocks = []
    for j in range(width // lanes):
        product = jnp.dot(
            stacked[:, j * lanes : (j + 1) * lanes], matrix, preferred_element_type=f32
        )
        theirs, mine = product[:rows], product[rows:]
        blocks.append(theirs + jnp.where(upper, -mine, mine))
    step = 1
    while step < len(blocks):
        for j in range(len(blocks)):
            if not j & step:
                a, b = blocks[j], blocks[j | step]
                blocks[j], blocks[j | step] = a + b, a - b
        step *= 2
    for j, block in enumerate(blocks):
        wide_ref[:, j * lanes : (j + 1) * lanes] = block
        send_ref[:, j * lanes : (j + 1) * lanes] = block.astype(bf16)


def mix(own, other):
    return pl.pallas_call(
        mix_kernel,
        out_shape=(jax.ShapeDtypeStruct(own.shape, f32), jax.ShapeDtypeStruct(own.shape, bf16)),
        in_specs=[VMEM] * 2,
        out_specs=(VMEM, VMEM),
        compiler_params=params(4),
        name="mix",
    )(own, other)


def down_half(rows, weight, scale, placed, other_half):
    count, depth = rows.shape
    half = weight.shape[1] // 2
    bn = tile_of(half)

    def kernel(x_ref, w_ref, s_ref, p_ref, o_ref):
        side = bit_of("hid", 1)
        if other_half:
            side = 1 - side

        @pl.loop(0, half // bn)
        def _(n):
            at = pl.multiple_of(n * bn, bn)
            there = pl.ds(pl.multiple_of(side * half + at, bn), bn)
            total = jnp.dot(x_ref[...], w_ref[:, there], preferred_element_type=f32)
            o_ref[:, pl.ds(at, bn)] = total * (s_ref[:, there].astype(f32) * 2.0 ** (-23)) + p_ref[:, there]

    return pl.pallas_call(
        kernel,
        out_shape=jax.ShapeDtypeStruct((count, half), f32),
        in_specs=[VMEM] * 4,
        out_specs=VMEM,
        compiler_params=params(4),
        cost_estimate=cost(2 * count * depth * half, 2 * depth * half),
        name="down_other" if other_half else "down_own",
    )(rows, weight, scale, placed)


def qkv_half(stream, gain, weight, before, own_half):
    count, depth = stream.shape
    width = weight.shape[1]
    bn = tile_of(width)

    def kernel(x_ref, g_ref, w_ref, *refs):
        if own_half:
            o_ref, q_ref, scaled = refs
        else:
            before_ref, squares_ref, o_ref, q_ref, scaled = refs
        side = bit_of("hid", 1)
        if not own_half:
            side = 1 - side
        there = pl.ds(pl.multiple_of(side * depth, depth), depth)
        wide = x_ref[...].astype(f32)
        scaled[...] = (wide * g_ref[:, there].astype(f32)).astype(bf16)
        squares = jnp.broadcast_to(jnp.sum(wide * wide, axis=1, keepdims=True), q_ref.shape)
        if not own_half:
            squares = squares + squares_ref[...]
        q_ref[...] = squares

        @pl.loop(0, width // bn)
        def _(n):
            columns = pl.ds(pl.multiple_of(n * bn, bn), bn)
            total = jnp.dot(scaled[...], w_ref[there, columns], preferred_element_type=f32)
            if not own_half:
                total += before_ref[:, columns]
            o_ref[:, columns] = total

    return pl.pallas_call(
        kernel,
        out_shape=(
            jax.ShapeDtypeStruct((count, width), f32),
            jax.ShapeDtypeStruct((count, lanes), f32),
        ),
        in_specs=[VMEM] * (3 + len(before)),
        out_specs=(VMEM, VMEM),
        scratch_shapes=[pltpu.VMEM((count, depth), bf16)],
        compiler_params=params(4),
        cost_estimate=cost(2 * count * depth * width, 2 * depth * width),
        name="qkv_own" if own_half else "qkv_other",
    )(stream, gain, weight, *before)


def body(
    gate_proj,
    up_proj,
    hadamard_signs,
    down_codes,
    down_scales,
    residual,
    norm_gain,
    qkv_codes,
    qkv_scales,
):
    hid, n_row = lax.axis_size("hid"), lax.axis_size("row")
    me_hid, me_row = lax.axis_index("hid"), lax.axis_index("row")
    own_rows, depth = gate_proj.shape
    all_rows = own_rows * n_row
    res_rows, features = residual.shape
    half = features // 2
    distances = [1 << b for b in range(hid.bit_length() - 1)]

    def natural(block):
        return block ^ me_row

    spot = lax.broadcasted_iota(jnp.int32, (all_rows, 1), 0)
    spot = natural(spot // own_rows) * own_rows + spot % own_rows - me_hid * res_rows
    placed = jnp.zeros((all_rows, features), f32)
    for r in range(res_rows):
        placed = jnp.where(spot == r, residual[r : r + 1].astype(f32), placed)

    down_codes = pltpu.with_memory_space_constraint(down_codes, pltpu.VMEM)
    qkv_codes = pltpu.with_memory_space_constraint(qkv_codes, pltpu.VMEM)

    signed = signed_units(gate_proj, up_proj, hadamard_signs)
    send = signed
    for k, distance in enumerate(distances):
        other = exchange(send, "hid", distance)
        if k == 0:
            wide, send = mix(signed, other)
        else:
            upper = bit_of("hid", distance) == 1
            wide = other.astype(f32) + jnp.where(upper, -wide, wide)
            send = wide.astype(bf16)
    rotated = (wide * (1.0 / math.sqrt(depth * hid))).astype(bf16)
    rows = [rotated] + [exchange(rotated, "row", j) for j in range(1, n_row)]
    rows = jnp.concatenate(rows, axis=0)

    scale = down_scales.reshape(1, -1)
    theirs = down_half(rows, down_codes, scale, placed, True)
    arrived = exchange(theirs, "hid", 1)
    total = down_half(rows, down_codes, scale, placed, False) + arrived
    for distance in distances[1:]:
        total = total + exchange(total.astype(bf16), "hid", distance).astype(f32)
    stream = total.astype(bf16)
    stream_other = exchange(stream, "hid", 1)

    gain = norm_gain.reshape(1, -1)
    part = qkv_half(stream, gain, qkv_codes, (), True)
    projected, squares = qkv_half(stream_other, gain, qkv_codes, part, False)
    both = jnp.concatenate([projected, squares], axis=1)
    mine = both[:own_rows]
    for j in range(1, n_row):
        mine = mine + exchange(both[j * own_rows : (j + 1) * own_rows], "row", j)
    width = projected.shape[1]
    inverse = lax.rsqrt(mine[:, width : width + 1] / (features * n_row) + epsilon)
    joined_qkv = (mine[:, :width] * inverse * (qkv_scales.astype(f32) * 2.0 ** (-22))[None, :]).astype(bf16)

    lower = bit_of("hid", 1) == 0
    full = jnp.concatenate(
        [jnp.where(lower, stream, stream_other), jnp.where(lower, stream_other, stream)], axis=1
    )
    first = me_hid * res_rows
    first = natural(first // own_rows) * own_rows + first % own_rows
    new_stream = lax.dynamic_slice_in_dim(full, first, res_rows, 0)
    return (new_stream, joined_qkv)


def solution(mesh):
    return jax.shard_map(
        body,
        mesh=mesh,
        in_specs=(
            P(("groups", "row"), "hid"),
            P(("groups", "row"), "hid"),
            P("hid"),
            P("hid", "row"),
            P("row"),
            P(("groups", "hid"), "row"),
            P("row"),
            P("row", "hid"),
            P("hid"),
        ),
        out_specs=(P(("groups", "hid"), "row"), P(("groups", "row"), "hid")),
        check_vma=False,
    )
```

time: 144 us -> 71.8 us (0.50)
  waiting for transfers between devices: 55.2 us -> 12.8 us
  blocking collectives: 35.4 us -> 0 us
  local copies, waits for them, and re-layouts: 1.1 us -> 26.4 us
  matrix products: 24.9 us -> 0 us
  between operations: 14.2 us -> 0.84 us
  Pallas kernels: 0 us -> 11.7 us
  starting transfers between devices: 7.88 us -> 16.9 us
  other arithmetic: 5.27 us -> 2.65 us
    psum x1 -> x0, waiting for transfers between devices: 41 us -> none  [body(): summed = lax.psum(partial_value, 'hid')]
    all_gather x2 -> x0, blocking collectives: 32.9 us -> none  [the longest x1 31 us: body(): every_residual = lax.all_gather(residual, 'hid', axis=0, tiled=True)]
    unnamed x6 -> x19, local copies, waits for them, and re-layouts: 0.01 us -> 26.4 us
    dot_general x4 -> x0, matrix products: 24.9 us -> none  [the longest x1 13.5 us: body(): jnp.dot(lax.all_gather(rotated, 'row', axis=0, tiled=True), down_codes, p...]
    pallas_call x0 -> x6, Pallas kernels: none -> 11.7 us  [the longest x2 6.38 us: down_half(): pl.pallas_call(kernel, out_shape=jax.ShapeDtypeStruct((count, half), f32)...]
    ppermute x3 -> x9, starting transfers between devices: 7.8 us -> 16.9 us  [exchange(): return lax.ppermute(block, axis, [(i, i ^ distance) for i in range(count)])]
    reduce_scatter x1 -> x0, waiting for transfers between devices: 3.8 us -> none  [body(): lax.psum_scatter(jnp.dot(scaled_rows, qkv_codes, preferred_element_type=j...]
    psum x1 -> x0, blocking collectives: 2.47 us -> none  [body(): all_squares = lax.psum(squares, 'row')]
  transfers between devices with their start and end apart: 5 -> 9, of which waited for: 5 -> 8; matrix products, arithmetic and copies ran while one was open for 1% -> 2% of each run, Pallas kernels for 0% -> 8%
where the time goes in v1:
time: 71.8 us; the launch traced here: 71.3 us
  local copies, waits for them, and re-layouts  26.4 us (37%)
  starting transfers between devices  16.9 us (24%)
  waiting for transfers between devices  12.8 us (18%)
  Pallas kernels  11.7 us (16%)
  other arithmetic  2.65 us (4%)
  between operations  0.84 us (1%)
    unnamed x19, local copies, waits for them, and re-layouts  26.4 us
    ppermute x9, starting transfers between devices, exchange(): return lax.ppermute(block, axis, [(i, i ^ distance) for i in range(count)])  16.9 us
    ppermute x9, waiting for transfers between devices, exchange(): return lax.ppermute(block, axis, [(i, i ^ distance) for i in range(count)])  12.8 us
    pallas_call x2, Pallas kernels, down_half(): pl.pallas_call(kernel, out_shape=jax.ShapeDtypeStruct((count, half), f32)...  6.38 us
    pallas_call x2, Pallas kernels, qkv_half(): pl.pallas_call(kernel, out_shape=(jax.ShapeDtypeStruct((count, width), f3...  4.8 us
  transfers between devices with their start and end apart: 9, of which 8 were waited for; matrix products, arithmetic and copies ran while one was open for 2% of the time, Pallas kernels for 8%

profile of v1, /device:TPU:0, one launch (start us, length us, event | category | flops | bytes accessed | tf_op | source)
XLA Modules:
  0.0 71.3 jit_solution(7079786837840569523)
XLA Ops:
  0.6 0.8 %copy-done.4 = bf16[8,4096]{1,0:T(8,128)(2,1)S(1)} copy-done((bf16[8,4096]{1,0:T(8,128)(2,1)S(1)}, bf16[8,4096]{1,0:T(8,128)(2,1)}, u32[]{:S(2)}) %copy-start.4) | copy-done | bytes 65560
  1.5 0.8 %copy-done.5 = bf16[8,4096]{1,0:T(8,128)(2,1)S(1)} copy-done((bf16[8,4096]{1,0:T(8,128)(2,1)S(1)}, bf16[8,4096]{1,0:T(8,128)(2,1)}, u32[]{:S(2)}) %copy-start.5) | copy-done | bytes 65560
  2.3 0.7 %copy-done.6 = s32[4096]{0:T(1024)S(1)} copy-done((s32[4096]{0:T(1024)S(1)}, s32[4096]{0:T(1024)}, u32[]{:S(2)}) %copy-start.6) | copy-done | bytes 16408
  3.1 3.0 %collective-permute-start = (bf16[8,4096]{1,0:T(8,128)(2,1)S(1)}, bf16[8,4096]{1,0:T(8,128)(2,1)S(1)}, u32[]{:S(2)}, u32[]{:S(2)}) collective-permute-start(bf16[8,4096]{1,0:T(8,128)(2,1)S(1)} %signed_units.1.own_ref), channel_id=1, source_target_pairs={{0,2},{2,0},{4,6},{6,4},{8,10},{10,8},{12,14},{14,12},{1,3},{3,1},... | collective-permute-start | bytes 196616 | tf_op jit(solution)/shard_map/ppermute | solution.py:18
  6.1 2.2 %collective-permute-done.other_ref = bf16[8,4096]{1,0:T(8,128)(2,1)S(1)} collective-permute-done((bf16[8,4096]{1,0:T(8,128)(2,1)S(1)}, bf16[8,4096]{1,0:T(8,128)(2,1)S(1)}, u32[]{:S(2)}, u32[]{:S(2)}) %collective-permute-start) | collective-permute-done | bytes 65568 | tf_op jit(solution)/shard_map/ppermute | solution.py:18
  8.4 0.4 mix.1
  8.8 2.2 %collective-permute-start.1 = (bf16[8,4096]{1,0:T(8,128)(2,1)S(1)}, bf16[8,4096]{1,0:T(8,128)(2,1)S(1)}, u32[]{:S(2)}, u32[]{:S(2)}) collective-permute-start(bf16[8,4096]{1,0:T(8,128)(2,1)S(1)} %get-tuple-element.8), channel_id=1, source_target_pairs={{0,4},{2,6},{4,0},{6,2},{8,12},{10,14},{12,8},{14,10},{1,5},{3,7},... | collective-permute-start | bytes 196616 | tf_op jit(solution)/shard_map/ppermute | solution.py:18
  11.0 0.8 %slice_convert_fusion.1 = (f32[1,4096]{1,0:T(1,128)S(1)}, f32[1,4096]{1,0:T(1,128)S(1)}) fusion(bf16[2,4096]{1,0:T(2,128)(2,1)} %param.14), kind=kLoop, calls=%fused_computation.22 | loop fusion | flops 8192 | bytes 49152 | tf_op jit(solution)/shard_map/jit(_where)/broadcast_in_dim | solution.py:199
  11.8 1.4 %collective-permute-done.1 = bf16[8,4096]{1,0:T(8,128)(2,1)S(1)} collective-permute-done((bf16[8,4096]{1,0:T(8,128)(2,1)S(1)}, bf16[8,4096]{1,0:T(8,128)(2,1)S(1)}, u32[]{:S(2)}, u32[]{:S(2)}) %collective-permute-start.1) | collective-permute-done | bytes 65568 | tf_op jit(solution)/shard_map/ppermute | solution.py:18
  13.2 3.1 %collective-permute-start.2 = (bf16[8,4096]{1,0:T(8,128)(2,1)S(1)}, bf16[8,4096]{1,0:T(8,128)(2,1)S(1)}, u32[]{:S(2)}, u32[]{:S(2)}) collective-permute-start(bf16[8,4096]{1,0:T(8,128)(2,1)S(1)} %fusion.5), channel_id=1, source_target_pairs={{0,8},{2,10},{4,12},{6,14},{8,0},{10,2},{12,4},{14,6},{1,9},{3,11}... | collective-permute-start | bytes 196616 | tf_op jit(solution)/shard_map/ppermute | solution.py:18
  16.3 2.2 %collective-permute-done.2 = bf16[8,4096]{1,0:T(8,128)(2,1)S(1)} collective-permute-done((bf16[8,4096]{1,0:T(8,128)(2,1)S(1)}, bf16[8,4096]{1,0:T(8,128)(2,1)S(1)}, u32[]{:S(2)}, u32[]{:S(2)}) %collective-permute-start.2) | collective-permute-done | bytes 65568 | tf_op jit(solution)/shard_map/ppermute | solution.py:18
  18.7 0.1 select_select_fusion.p_ref
  18.8 1.1 %collective-permute-done.3 = bf16[8,4096]{1,0:T(8,128)(2,1)S(1)} collective-permute-done((bf16[8,4096]{1,0:T(8,128)(2,1)S(1)}, bf16[8,4096]{1,0:T(8,128)(2,1)S(1)}, u32[]{:S(2)}, u32[]{:S(2)}) %collective-permute-start.3) | collective-permute-done | bytes 65568 | tf_op jit(solution)/shard_map/ppermute | solution.py:18
  20.0 10.5 %copy-done = bf16[4096,4096]{1,0:T(8,128)(2,1)S(1)} copy-done((bf16[4096,4096]{1,0:T(8,128)(2,1)S(1)}, bf16[4096,4096]{1,0:T(8,128)(2,1)}, u32[]{:S(2)}) %copy-start) | copy-done | bytes 33554456
  30.5 0.7 %copy-done.3 = s32[4096]{0:T(1024)S(1)} copy-done((s32[4096]{0:T(1024)S(1)}, s32[4096]{0:T(1024)}, u32[]{:S(2)}) %copy-start.3) | copy-done | bytes 16408
  31.2 3.2 %down_other.1 = f32[16,2048]{1,0:T(8,128)S(1)} custom-call(bf16[16,4096]{1,0:T(8,128)(2,1)S(1)} %pad_maximum_fusion.x_ref, bf16[4096,4096]{1,0:T(8,128)(2,1)S(1)} %copy-done, s32[1,4096]{1,0:T(1,128)S(1)} %bitcast.4, f32[16,4096]{1,0:T(8,128)S(1)} %select_select_fusion.p_ref), custom_call_target="tpu_custom_call" | custom-call | flops 268435456 | bytes 16777216 | tf_op jit(solution)/shard_map/down_other/pallas_call | solution.py:118
  34.4 1.8 %collective-permute-start.4 = (f32[16,2048]{1,0:T(8,128)S(1)}, f32[16,2048]{1,0:T(8,128)S(1)}, u32[]{:S(2)}, u32[]{:S(2)}) collective-permute-start(f32[16,2048]{1,0:T(8,128)S(1)} %down_other.1), channel_id=1, source_target_pairs={{0,2},{2,0},{4,6},{6,4},{8,10},{10,8},{12,14},{14,12},{1,3},{3,1},... | collective-permute-start | bytes 393224 | tf_op jit(solution)/shard_map/ppermute | solution.py:18
  36.2 3.2 %down_own.1 = f32[16,2048]{1,0:T(8,128)S(1)} custom-call(bf16[16,4096]{1,0:T(8,128)(2,1)S(1)} %pad_maximum_fusion.x_ref, bf16[4096,4096]{1,0:T(8,128)(2,1)S(1)} %copy-done, s32[1,4096]{1,0:T(1,128)S(1)} %bitcast.5, f32[16,4096]{1,0:T(8,128)S(1)} %select_select_fusion.p_ref), custom_call_target="tpu_custom_call" | custom-call | flops 268435456 | bytes 16777216 | tf_op jit(solution)/shard_map/down_own/pallas_call | solution.py:118
  39.4 0.6 collective-permute-done.4
  40.1 1.9 %collective-permute-start.5 = (bf16[16,2048]{1,0:T(8,128)(2,1)S(1)}, bf16[16,2048]{1,0:T(8,128)(2,1)S(1)}, u32[]{:S(2)}, u32[]{:S(2)}) collective-permute-start(bf16[16,2048]{1,0:T(8,128)(2,1)S(1)} %get-tuple-element.14), channel_id=1, source_target_pairs={{0,4},{2,6},{4,0},{6,2},{8,12},{10,14},{12,8},{14,10},{1,5},{3,7},... | collective-permute-start | bytes 196616 | tf_op jit(solution)/shard_map/ppermute | solution.py:18
  42.0 2.4 %collective-permute-done.5 = bf16[16,2048]{1,0:T(8,128)(2,1)S(1)} collective-permute-done((bf16[16,2048]{1,0:T(8,128)(2,1)S(1)}, bf16[16,2048]{1,0:T(8,128)(2,1)S(1)}, u32[]{:S(2)}, u32[]{:S(2)}) %collective-permute-start.5) | collective-permute-done | bytes 65568 | tf_op jit(solution)/shard_map/ppermute | solution.py:18
  44.4 3.1 %collective-permute-start.6 = (bf16[16,2048]{1,0:T(8,128)(2,1)S(1)}, bf16[16,2048]{1,0:T(8,128)(2,1)S(1)}, u32[]{:S(2)}, u32[]{:S(2)}) collective-permute-start(bf16[16,2048]{1,0:T(8,128)(2,1)S(1)} %fusion.4), channel_id=1, source_target_pairs={{0,8},{2,10},{4,12},{6,14},{8,0},{10,2},{12,4},{14,6},{1,9},{3,11}... | collective-permute-start | bytes 196616 | tf_op jit(solution)/shard_map/ppermute | solution.py:18
  47.5 2.2 %collective-permute-done.6 = bf16[16,2048]{1,0:T(8,128)(2,1)S(1)} collective-permute-done((bf16[16,2048]{1,0:T(8,128)(2,1)S(1)}, bf16[16,2048]{1,0:T(8,128)(2,1)S(1)}, u32[]{:S(2)}, u32[]{:S(2)}) %collective-permute-start.6) | collective-permute-done | bytes 65568 | tf_op jit(solution)/shard_map/ppermute | solution.py:18
  49.8 1.7 %collective-permute-start.7 = (bf16[16,2048]{1,0:T(8,128)(2,1)S(1)}, bf16[16,2048]{1,0:T(8,128)(2,1)S(1)}, u32[]{:S(2)}, u32[]{:S(2)}) collective-permute-start(bf16[16,2048]{1,0:T(8,128)(2,1)S(1)} %add_convert_fusion.x_ref), channel_id=1, source_target_pairs={{0,2},{2,0},{4,6},{6,4},{8,10},{10,8},{12,14},{14,12},{1,3},{3,1},... | collective-permute-start | bytes 196616 | tf_op jit(solution)/shard_map/ppermute | solution.py:18
  51.5 6.4 %copy-done.1 = bf16[4096,2304]{1,0:T(8,128)(2,1)S(1)} copy-done((bf16[4096,2304]{1,0:T(8,128)(2,1)S(1)}, bf16[4096,2304]{1,0:T(8,128)(2,1)}, u32[]{:S(2)}) %copy-start.1) | copy-done | bytes 18874392
  57.9 2.4 %qkv_own.1 = (f32[16,2304]{1,0:T(8,128)S(1)}, f32[16,128]{1,0:T(8,128)S(1)}) custom-call(bf16[16,2048]{1,0:T(8,128)(2,1)S(1)} %add_convert_fusion.x_ref, bf16[1,4096]{1,0:T(2,128)(2,1)S(1)} %reshape.80.g_ref, bf16[4096,2304]{1,0:T(8,128)(2,1)S(1)} %copy-done.1), custom_call_target="tpu_custom_call" | custom-call | flops 150994944 | bytes 9437184 | tf_op jit(solution)/shard_map/qkv_own/pallas_call | solution.py:158
  60.3 6.4 %copy-done.2 = bf16[4096,2304]{1,0:T(8,128)(2,1)S(1)} copy-done((bf16[4096,2304]{1,0:T(8,128)(2,1)S(1)}, bf16[4096,2304]{1,0:T(8,128)(2,1)}, u32[]{:S(2)}) %copy-start.2) | copy-done | bytes 18874392
  66.7 2.4 %qkv_other.1 = (f32[16,2304]{1,0:T(8,128)S(1)}, f32[16,128]{1,0:T(8,128)S(1)}) custom-call(bf16[16,2048]{1,0:T(8,128)(2,1)S(1)} %collective-permute-done.7.x_ref, bf16[1,4096]{1,0:T(2,128)(2,1)S(1)} %reshape.80.g_ref, bf16[4096,2304]{1,0:T(8,128)(2,1)S(1)} %copy-done.2, f32[16,2304]{1,0:T(8,128)S(1)} %get-tuple-element.10.refs_0_, ...), custom_call_target="tpu_custom_call" | custom-call | flops 150994944 | bytes 9437184 | tf_op jit(solution)/shard_map/qkv_other/pallas_call | solution.py:158
  69.2 0.7 %fusion.8 = bf16[2,4096]{1,0:T(2,128)(2,1)} fusion(s32[]{:T(128)S(6)} %select_n.111, bf16[16,2048]{1,0:T(8,128)(2,1)S(1)} %get-tuple-element.17, bf16[16,2048]{1,0:T(8,128)(2,1)S(1)} %get-tuple-element.16), kind=kLoop, calls=%fused_computation.20 | loop fusion | flops 32768 | bytes 147460 | tf_op jit(solution)/shard_map/concatenate | solution.py:239
  70.0 0.5 collective-permute-done.8
  70.5 0.1 fusion.11
  70.6 0.7 fusion.7
  (29 shorter events, 0.5 us)
Async XLA Ops:
  0.6 0.8 %copy-start.4 = (bf16[8,4096]{1,0:T(8,128)(2,1)S(1)}, bf16[8,4096]{1,0:T(8,128)(2,1)}, u32[]{:S(2)}) copy-start(bf16[8,4096]{1,0:T(8,128)(2,1)} %gate_ref.1) | copy-start | bytes 196612
  1.5 0.8 %copy-start.5 = (bf16[8,4096]{1,0:T(8,128)(2,1)S(1)}, bf16[8,4096]{1,0:T(8,128)(2,1)}, u32[]{:S(2)}) copy-start(bf16[8,4096]{1,0:T(8,128)(2,1)} %up_ref.1) | copy-start | bytes 196612
  2.3 0.7 %copy-start.6 = (s32[4096]{0:T(1024)S(1)}, s32[4096]{0:T(1024)}, u32[]{:S(2)}) copy-start(s32[4096]{0:T(1024)} %param.11) | copy-start | bytes 49156
  3.1 5.2 %collective-permute-start = (bf16[8,4096]{1,0:T(8,128)(2,1)S(1)}, bf16[8,4096]{1,0:T(8,128)(2,1)S(1)}, u32[]{:S(2)}, u32[]{:S(2)}) collective-permute-start(bf16[8,4096]{1,0:T(8,128)(2,1)S(1)} %signed_units.1.own_ref), channel_id=1, source_target_pairs={{0,2},{2,0},{4,6},{6,4},{8,10},{10,8},{12,14},{14,12},{1,3},{3,1},... | collective-permute-start | bytes 196616 | tf_op jit(solution)/shard_map/ppermute | solution.py:18
  8.8 4.4 %collective-permute-start.1 = (bf16[8,4096]{1,0:T(8,128)(2,1)S(1)}, bf16[8,4096]{1,0:T(8,128)(2,1)S(1)}, u32[]{:S(2)}, u32[]{:S(2)}) collective-permute-start(bf16[8,4096]{1,0:T(8,128)(2,1)S(1)} %get-tuple-element.8), channel_id=1, source_target_pairs={{0,4},{2,6},{4,0},{6,2},{8,12},{10,14},{12,8},{14,10},{1,5},{3,7},... | collective-permute-start | bytes 196616 | tf_op jit(solution)/shard_map/ppermute | solution.py:18
  13.2 5.3 %collective-permute-start.2 = (bf16[8,4096]{1,0:T(8,128)(2,1)S(1)}, bf16[8,4096]{1,0:T(8,128)(2,1)S(1)}, u32[]{:S(2)}, u32[]{:S(2)}) collective-permute-start(bf16[8,4096]{1,0:T(8,128)(2,1)S(1)} %fusion.5), channel_id=1, source_target_pairs={{0,8},{2,10},{4,12},{6,14},{8,0},{10,2},{12,4},{14,6},{1,9},{3,11}... | collective-permute-start | bytes 196616 | tf_op jit(solution)/shard_map/ppermute | solution.py:18
  18.6 1.3 %collective-permute-start.3 = (bf16[8,4096]{1,0:T(8,128)(2,1)S(1)}, bf16[8,4096]{1,0:T(8,128)(2,1)S(1)}, u32[]{:S(2)}, u32[]{:S(2)}) collective-permute-start(bf16[8,4096]{1,0:T(8,128)(2,1)S(1)} %fusion.3), channel_id=1, source_target_pairs={{0,1},{1,0},{2,3},{3,2},{4,5},{5,4},{6,7},{7,6},{8,9},{9,8},{10,11... | collective-permute-start | bytes 196616 | tf_op jit(solution)/shard_map/ppermute | solution.py:18
  20.0 10.5 %copy-start = (bf16[4096,4096]{1,0:T(8,128)(2,1)S(1)}, bf16[4096,4096]{1,0:T(8,128)(2,1)}, u32[]{:S(2)}) copy-start(bf16[4096,4096]{1,0:T(8,128)(2,1)} %w_ref.5) | copy-start | bytes 100663296
  30.5 0.7 %copy-start.3 = (s32[4096]{0:T(1024)S(1)}, s32[4096]{0:T(1024)}, u32[]{:S(2)}) copy-start(s32[4096]{0:T(1024)} %param.13) | copy-start | bytes 49156
  31.2 20.3 %copy-start.7 = (s32[2304]{0:T(1024)S(1)}, s32[2304]{0:T(1024)}, u32[]{:S(2)}) copy-start(s32[2304]{0:T(1024)} %param.17) | copy-start | bytes 27652
  31.2 20.3 %copy-start.8 = (bf16[4096]{0:T(1024)(128)(2,1)S(1)}, bf16[4096]{0:T(1024)(128)(2,1)}, u32[]{:S(2)}) copy-start(bf16[4096]{0:T(1024)(128)(2,1)} %param.15) | copy-start | bytes 24580
  34.4 5.6 %collective-permute-start.4 = (f32[16,2048]{1,0:T(8,128)S(1)}, f32[16,2048]{1,0:T(8,128)S(1)}, u32[]{:S(2)}, u32[]{:S(2)}) collective-permute-start(f32[16,2048]{1,0:T(8,128)S(1)} %down_other.1), channel_id=1, source_target_pairs={{0,2},{2,0},{4,6},{6,4},{8,10},{10,8},{12,14},{14,12},{1,3},{3,1},... | collective-permute-start | bytes 393224 | tf_op jit(solution)/shard_map/ppermute | solution.py:18
  40.1 4.3 %collective-permute-start.5 = (bf16[16,2048]{1,0:T(8,128)(2,1)S(1)}, bf16[16,2048]{1,0:T(8,128)(2,1)S(1)}, u32[]{:S(2)}, u32[]{:S(2)}) collective-permute-start(bf16[16,2048]{1,0:T(8,128)(2,1)S(1)} %get-tuple-element.14), channel_id=1, source_target_pairs={{0,4},{2,6},{4,0},{6,2},{8,12},{10,14},{12,8},{14,10},{1,5},{3,7},... | collective-permute-start | bytes 196616 | tf_op jit(solution)/shard_map/ppermute | solution.py:18
  44.4 5.3 %collective-permute-start.6 = (bf16[16,2048]{1,0:T(8,128)(2,1)S(1)}, bf16[16,2048]{1,0:T(8,128)(2,1)S(1)}, u32[]{:S(2)}, u32[]{:S(2)}) collective-permute-start(bf16[16,2048]{1,0:T(8,128)(2,1)S(1)} %fusion.4), channel_id=1, source_target_pairs={{0,8},{2,10},{4,12},{6,14},{8,0},{10,2},{12,4},{14,6},{1,9},{3,11}... | collective-permute-start | bytes 196616 | tf_op jit(solution)/shard_map/ppermute | solution.py:18
  49.8 10.6 %collective-permute-start.7 = (bf16[16,2048]{1,0:T(8,128)(2,1)S(1)}, bf16[16,2048]{1,0:T(8,128)(2,1)S(1)}, u32[]{:S(2)}, u32[]{:S(2)}) collective-permute-start(bf16[16,2048]{1,0:T(8,128)(2,1)S(1)} %add_convert_fusion.x_ref), channel_id=1, source_target_pairs={{0,2},{2,0},{4,6},{6,4},{8,10},{10,8},{12,14},{14,12},{1,3},{3,1},... | collective-permute-start | bytes 196616 | tf_op jit(solution)/shard_map/ppermute | solution.py:18
  51.5 6.4 %copy-start.1 = (bf16[4096,2304]{1,0:T(8,128)(2,1)S(1)}, bf16[4096,2304]{1,0:T(8,128)(2,1)}, u32[]{:S(2)}) copy-start(bf16[4096,2304]{1,0:T(8,128)(2,1)} %w_ref.7) | copy-start | bytes 56623108
  60.3 6.4 %copy-start.2 = (bf16[4096,2304]{1,0:T(8,128)(2,1)S(1)}, bf16[4096,2304]{1,0:T(8,128)(2,1)}, u32[]{:S(2)}) copy-start(bf16[4096,2304]{1,0:T(8,128)(2,1)} %w_ref.7) | copy-start | bytes 56623108
  69.1 1.3 %collective-permute-start.8 = (f32[8,2432]{1,0:T(8,128)S(1)}, f32[8,2432]{1,0:T(8,128)S(1)}, u32[]{:S(2)}, u32[]{:S(2)}) collective-permute-start(f32[8,2432]{1,0:T(8,128)S(1)} %slice.25), channel_id=1, source_target_pairs={{0,1},{1,0},{2,3},{3,2},{4,5},{5,4},{6,7},{7,6},{8,9},{9,8},{10,11... | collective-permute-start | bytes 233480 | tf_op jit(solution)/shard_map/ppermute | solution.py:18

commit v2 on v1

v2 whole, which is shorter than its diff:
```python
import math

import jax
import jax.numpy as jnp
from jax import lax
from jax.experimental import pallas as pl
from jax.experimental.pallas import tpu as pltpu
from jax.sharding import PartitionSpec as P

epsilon = 1e-05
lanes = 128
VMEM = pl.BlockSpec(memory_space=pltpu.VMEM)
HBM = pl.BlockSpec(memory_space=pltpu.HBM)
f32, bf16 = jnp.float32, jnp.bfloat16


def exchange(block, axis, distance):
    count = lax.axis_size(axis)
    return lax.ppermute(block, axis, [(i, i ^ distance) for i in range(count)])


def bit_of(axis, distance):
    return lax.axis_index(axis) // distance % 2


def in_hbm(array):
    return pltpu.with_memory_space_constraint(array, pltpu.HBM)


def in_vmem(array):
    return pltpu.with_memory_space_constraint(array, pltpu.VMEM)


def params(mib):
    return pltpu.CompilerParams(vmem_limit_bytes=mib << 20)


def cost(flops, nbytes):
    return pl.CostEstimate(flops=flops, bytes_accessed=nbytes, transcendentals=0)


def tile_of(width):
    parts = next(p for p in (1, 2, 3, 4, 6, 8, 9, 12) if width // p <= 1152 and width % (p * lanes) == 0)
    return width // parts


def signed_kernel(gate_hbm, up_hbm, sign_hbm, out_ref, gate_ref, up_ref, sign_ref, sems):
    copies = [
        pltpu.make_async_copy(gate_hbm, gate_ref, sems.at[0]),
        pltpu.make_async_copy(up_hbm, up_ref, sems.at[1]),
        pltpu.make_async_copy(sign_hbm, sign_ref, sems.at[2]),
    ]
    for copy in copies:
        copy.start()
    for copy in copies:
        copy.wait()
    gate = gate_ref[...].astype(f32)
    hidden = (gate / (1.0 + jnp.exp(-gate)) * up_ref[...].astype(f32)).astype(bf16)
    flips = (1 - 2 * sign_ref[...]).astype(f32)
    out_ref[...] = (hidden.astype(f32) * flips).astype(bf16)


def signed_units(gate, up, signs):
    signs = signs.reshape(1, -1)
    return pl.pallas_call(
        signed_kernel,
        out_shape=jax.ShapeDtypeStruct(gate.shape, bf16),
        in_specs=[HBM] * 3,
        out_specs=VMEM,
        scratch_shapes=[
            pltpu.VMEM(gate.shape, bf16),
            pltpu.VMEM(gate.shape, bf16),
            pltpu.VMEM(signs.shape, jnp.int32),
            pltpu.SemaphoreType.DMA((3,)),
        ],
        compiler_params=params(4),
        name="signed_units",
    )(in_hbm(gate), in_hbm(up), in_hbm(signs))


def hadamard_128():
    both = lax.broadcasted_iota(jnp.int32, (lanes, lanes), 0) & lax.broadcasted_iota(
        jnp.int32, (lanes, lanes), 1
    )
    for shift in (4, 2, 1):
        both = both ^ (both >> shift)
    return (1 - 2 * (both & 1)).astype(f32).astype(bf16)


def mix_kernel(own_ref, other_ref, wide_ref, send_ref):
    rows, width = own_ref.shape
    matrix = hadamard_128()
    upper = bit_of("hid", 1) == 1
    own, other = own_ref[...].astype(f32), other_ref[...].astype(f32)
    stacked = jnp.concatenate([other, own], axis=0).astype(bf16)
    blocks = []
    for j in range(width // lanes):
        product = jnp.dot(
            stacked[:, j * lanes : (j + 1) * lanes], matrix, preferred_element_type=f32
        )
        theirs, mine = product[:rows], product[rows:]
        blocks.append(theirs + jnp.where(upper, -mine, mine))
    step = 1
    while step < len(blocks):
        for j in range(len(blocks)):
            if not j & step:
                a, b = blocks[j], blocks[j | step]
                blocks[j], blocks[j | step] = a + b, a - b
        step *= 2
    for j, block in enumerate(blocks):
        wide_ref[:, j * lanes : (j + 1) * lanes] = block
        send_ref[:, j * lanes : (j + 1) * lanes] = block.astype(bf16)


def mix(own, other):
    return pl.pallas_call(
        mix_kernel,
        out_shape=(jax.ShapeDtypeStruct(own.shape, f32), jax.ShapeDtypeStruct(own.shape, bf16)),
        in_specs=[VMEM] * 2,
        out_specs=(VMEM, VMEM),
        compiler_params=params(4),
        name="mix",
    )(own, other)


def combine(wide, other, distance, factor):
    def kernel(wide_ref, other_ref, *out_refs):
        own, theirs = wide_ref[...], other_ref[...].astype(f32)
        mixed = theirs + jnp.where(bit_of("hid", distance) == 1, -own, own)
        if factor is None:
            out_refs[0][...] = mixed
            out_refs[1][...] = mixed.astype(bf16)
        else:
            out_refs[0][...] = (mixed * factor).astype(bf16)

    types = (f32, bf16) if factor is None else (bf16,)
    return pl.pallas_call(
        kernel,
        out_shape=tuple(jax.ShapeDtypeStruct(wide.shape, t) for t in types),
        in_specs=[VMEM] * 2,
        out_specs=(VMEM,) * len(types),
        compiler_params=params(4),
        name="combine",
    )(wide, other)


def add(total, arrived, last, first):
    def kernel(total_ref, arrived_ref, *out_refs):
        value = total_ref[...] + arrived_ref[...].astype(f32)
        if not last:
            out_refs[0][...] = value
        out_refs[-1][...] = value.astype(bf16)

    types = (bf16,) if last else (f32, bf16)
    return pl.pallas_call(
        kernel,
        out_shape=tuple(jax.ShapeDtypeStruct(total.shape, t) for t in types),
        in_specs=[VMEM] * 2,
        out_specs=(VMEM,) * len(types),
        compiler_params=params(4),
        cost_estimate=cost(40_000_000_000, 0) if not last else None,
        name="add",
    )(total, arrived)


def places(res_rows, own_rows):
    first, me_row = lax.axis_index("hid") * res_rows, lax.axis_index("row")
    found = []
    for r in range(res_rows):
        row = first + r
        found.append(((row // own_rows) ^ me_row) * own_rows + row % own_rows)
    return found


def half_columns(weight_ref, start, count, other_half):
    half = weight_ref.shape[1] // 2
    side = bit_of("hid", 1)
    if other_half:
        side = 1 - side
    return weight_ref.at[pl.ds(start, count), pl.ds(pl.multiple_of(side * half, half), half)]


def load_rows(weight, start, count, other_half, after):
    def kernel(after_ref, weight_ref, out_ref, sem):
        copy = pltpu.make_async_copy(half_columns(weight_ref, start, count, other_half), out_ref, sem)
        copy.start()
        copy.wait()

    return pl.pallas_call(
        kernel,
        out_shape=pltpu.VMEM((count, weight.shape[1] // 2), weight.dtype),
        in_specs=[VMEM, HBM],
        out_specs=VMEM,
        scratch_shapes=[pltpu.SemaphoreType.DMA],
        compiler_params=params(2),
        cost_estimate=cost(0, count * weight.shape[1]),
        name="load_rows",
    )(after, in_hbm(weight))


def tie(first, second):
    return lax.optimization_barrier((first, second))


def down_half(rows, chunks, weight, scale, residual, own_rows, other_half, ahead):
    count, depth = rows.shape
    half = weight.shape[1] // 2
    bn = tile_of(half)
    n_chunks = len(chunks)
    starts = [sum(c.shape[0] for c in chunks[:i]) for i in range(n_chunks + 1)]
    loaded = starts[-1]
    rest = depth - loaded
    pieces = max(p for p in (1, 2, 3, 4, 5, 6) if rest % (p * lanes) == 0) if rest else 0
    piece = rest // max(pieces, 1)
    first, few = ahead

    def kernel(x_ref, *refs):
        refs = list(refs)
        chunk_refs = [refs.pop(0) for _ in range(n_chunks)]
        w_ref, s_ref, r_ref, o_ref = (refs.pop(0) for _ in range(4))
        if few:
            ahead_ref = refs.pop(0)
        if rest:
            buf = refs.pop(0)
        sems = refs.pop(0)
        copies = [
            pltpu.make_async_copy(
                half_columns(w_ref, loaded + i * piece, piece, other_half),
                buf.at[pl.ds(i * piece, piece)],
                sems.at[i],
            )
            for i in range(pieces)
        ]
        if few:
            copies.append(
                pltpu.make_async_copy(
                    half_columns(w_ref, first, few, not other_half), ahead_ref, sems.at[pieces]
                )
            )
        for copy in copies:
            copy.start()
        side = bit_of("hid", 1)
        if other_half:
            side = 1 - side
        where = places(r_ref.shape[0], own_rows)
        index = lax.broadcasted_iota(jnp.int32, (count, bn), 0)
        parts = [(refs_at, start, ref.shape[0]) for refs_at, (start, ref) in enumerate(zip(starts, chunk_refs))]
        steps = [[(chunk_refs[i], start, 0, size) for i, start, size in parts]] if parts else []
        for i in range(pieces):
            steps.append([(buf, loaded + i * piece, i * piece, piece)])

        for i, step in enumerate(steps):
            if parts and i > 0:
                copies[i - 1].wait()
            elif not parts:
                copies[i].wait()

            @pl.loop(0, half // bn)
            def _(n):
                here = pl.ds(pl.multiple_of(n * bn, lanes), bn)
                total = jnp.zeros((count, bn), f32) if i == 0 else o_ref[:, here]
                for ref, x_at, at, size in step:
                    total += jnp.dot(
                        x_ref[:, x_at : x_at + size],
                        ref[at : at + size, here],
                        preferred_element_type=f32,
                    )
                if i == len(steps) - 1:
                    there = pl.ds(pl.multiple_of(side * half + n * bn, lanes), bn)
                    total = total * (s_ref[:, there].astype(f32) * 2.0 ** (-23))
                    residual_rows = r_ref[:, there].astype(f32)
                    for r, place in enumerate(where):
                        total = total + jnp.where(index == place, residual_rows[r : r + 1], 0.0)
                o_ref[:, here] = total

        if few:
            copies[-1].wait()

    out_shape = [jax.ShapeDtypeStruct((count, half), f32)]
    scratch = [pltpu.SemaphoreType.DMA((pieces + 1,))]
    if few:
        out_shape.append(pltpu.VMEM((few, half), weight.dtype))
    if rest:
        scratch.insert(0, pltpu.VMEM((rest, half), bf16))
    return pl.pallas_call(
        kernel,
        out_shape=tuple(out_shape),
        in_specs=[VMEM] * (1 + n_chunks) + [HBM, VMEM, VMEM],
        out_specs=(VMEM,) * len(out_shape),
        scratch_shapes=scratch,
        compiler_params=params(14),
        cost_estimate=cost(2 * count * depth * half, 2 * depth * half),
        name="down_other" if other_half else "down_own",
    )(rows, *map(in_vmem, chunks), in_hbm(weight), scale, residual)


def qkv_half(stream, gain, weight, before, own_rows):
    count, depth = stream.shape
    width = weight.shape[1]
    bn = tile_of(width)
    own_half = before is None
    first_rows = [(0, count)] if own_half else [(0, own_rows), (own_rows, count - own_rows)]

    def kernel(x_ref, g_ref, w_ref, *refs):
        before_ref = None if own_half else refs[0]
        out_refs, scaled = refs[-1 - len(first_rows) : -1], refs[-1]
        side = bit_of("hid", 1)
        if not own_half:
            side = 1 - side
        there = pl.ds(pl.multiple_of(side * depth, depth), depth)
        wide = x_ref[...].astype(f32)
        scaled[...] = (wide * g_ref[:, there].astype(f32)).astype(bf16)
        squares = jnp.broadcast_to(jnp.sum(wide * wide, axis=1, keepdims=True), (count, lanes))

        def put(columns, value):
            if not own_half:
                value = value + before_ref[:, columns]
            for ref, (start, size) in zip(out_refs, first_rows):
                ref[:, columns] = value[start : start + size]

        put(pl.ds(width, lanes), squares)

        for n in range(width // bn):
            columns = pl.ds(n * bn, bn)
            put(columns, jnp.dot(scaled[...], w_ref[there, columns], preferred_element_type=f32))

    operands = (stream, gain, weight) + (() if own_half else (before,))
    return pl.pallas_call(
        kernel,
        out_shape=tuple(jax.ShapeDtypeStruct((size, width + lanes), f32) for _, size in first_rows),
        in_specs=[VMEM] * len(operands),
        out_specs=(VMEM,) * len(first_rows),
        scratch_shapes=[pltpu.VMEM((count, depth), bf16)],
        compiler_params=params(4),
        cost_estimate=cost(2 * count * depth * width, 2 * depth * width),
        name="qkv_own" if own_half else "qkv_other",
    )(*operands)


def take_rows(stream, stream_other, res_rows, own_rows):
    count, half = stream.shape

    def kernel(own_ref, other_ref, out_ref):
        index = lax.broadcasted_iota(jnp.int32, (count, half), 0)
        side = bit_of("hid", 1)
        for ref, at in ((own_ref, side), (other_ref, 1 - side)):
            wide = ref[...].astype(f32)
            taken = [
                jnp.sum(jnp.where(index == place, wide, 0.0), axis=0, keepdims=True)
                for place in places(res_rows, own_rows)
            ]
            there = pl.ds(pl.multiple_of(at * half, half), half)
            out_ref[:, there] = jnp.concatenate(taken, axis=0).astype(bf16)

    return pl.pallas_call(
        kernel,
        out_shape=jax.ShapeDtypeStruct((res_rows, 2 * half), bf16),
        in_specs=[VMEM] * 2,
        out_specs=VMEM,
        compiler_params=params(4),
        name="take_rows",
    )(stream, stream_other)


def body(
    gate_proj,
    up_proj,
    hadamard_signs,
    down_codes,
    down_scales,
    residual,
    norm_gain,
    qkv_codes,
    qkv_scales,
):
    hid, n_row = lax.axis_size("hid"), lax.axis_size("row")
    own_rows, depth = gate_proj.shape
    res_rows, features = residual.shape
    distances = [1 << b for b in range(hid.bit_length() - 1)]

    send = signed_units(gate_proj, up_proj, hadamard_signs)
    chunks, loaded = [], 0
    share = -(-depth // len(distances) // lanes) * lanes
    for k, distance in enumerate(distances):
        other = exchange(send, "hid", distance)
        count = min(share, depth - loaded)
        chunk = load_rows(down_codes, loaded, count, True, send)
        other, chunk = tie(other, chunk)
        chunks.append(chunk)
        loaded += count
        last = k == len(distances) - 1
        if k == 0:
            wide, send = mix(send, other)
        elif not last:
            wide, send = combine(wide, other, distance, None)
        else:
            (rotated,) = combine(wide, other, distance, 1.0 / math.sqrt(depth * hid))
    rows = [rotated] + [exchange(rotated, "row", j) for j in range(1, n_row)]
    early = depth * 3 // 32 // lanes * lanes
    own_chunk = load_rows(down_codes, 0, early, False, rotated)
    rows[-1], own_chunk = tie(rows[-1], own_chunk)
    rows = jnp.concatenate(rows, axis=0)

    scale = down_scales.reshape(1, -1)
    ahead = (early, depth * 11 // 32 // lanes * lanes)
    theirs, next_chunk = down_half(rows, chunks, down_codes, scale, residual, own_rows, True, ahead)
    arrived = exchange(theirs, "hid", 1)
    own_chunks = [own_chunk, next_chunk]
    (total,) = down_half(rows, own_chunks, down_codes, scale, residual, own_rows, False, (0, 0))
    for distance in distances[1:]:
        total, send = add(total, arrived, False, distance == 2)
        arrived = exchange(send, "hid", distance)
    (stream,) = add(total, arrived, True, False)
    stream_other = exchange(stream, "hid", 1)

    gain = norm_gain.reshape(1, -1)
    (part,) = qkv_half(stream, gain, qkv_codes, None, own_rows)
    mine, rest = qkv_half(stream_other, gain, qkv_codes, part, own_rows)
    for j in range(1, n_row):
        mine = mine + exchange(rest[(j - 1) * own_rows : j * own_rows], "row", j)
    width = qkv_codes.shape[1]
    inverse = lax.rsqrt(mine[:, width : width + 1] / (features * n_row) + epsilon)
    joined_qkv = (mine[:, :width] * inverse * (qkv_scales.astype(f32) * 2.0 ** (-22))[None, :]).astype(bf16)
    return (take_rows(stream, stream_other, res_rows, own_rows), joined_qkv)


def solution(mesh):
    return jax.shard_map(
        body,
        mesh=mesh,
        in_specs=(
            P(("groups", "row"), "hid"),
            P(("groups", "row"), "hid"),
            P("hid"),
            P("hid", "row"),
            P("row"),
            P(("groups", "hid"), "row"),
            P("row"),
            P("row", "hid"),
            P("hid"),
        ),
        out_specs=(P(("groups", "hid"), "row"), P(("groups", "row"), "hid")),
        check_vma=False,
    )
```

time: 71.8 us -> 45.7 us (0.64)
  local copies, waits for them, and re-layouts: 26.4 us -> 0.05 us
  Pallas kernels: 11.7 us -> 21.1 us
  waiting for transfers between devices: 12.8 us -> 7.46 us
  other arithmetic: 2.65 us -> 0.85 us
  starting transfers between devices: 16.9 us -> 15.1 us
    unnamed x19 -> x18, local copies, waits for them, and re-layouts: 26.4 us -> 0.04 us
    pallas_call x4 -> x14, Pallas kernels: 11.2 us -> 19.7 us  [the longest x4 9.21 us: load_rows(): pl.pallas_call(kernel, out_shape=pltpu.VMEM((count, weight.shape[1] // 2)...]
    ppermute x9, waiting for transfers between devices: 12.8 us -> 7.46 us  [exchange(): return lax.ppermute(block, axis, [(i, i ^ distance) for i in range(count)])]
    ppermute x9, starting transfers between devices: 16.9 us -> 15.1 us  [exchange(): return lax.ppermute(block, axis, [(i, i ^ distance) for i in range(count)])]
    pallas_call x1, Pallas kernels: 0.07 us -> 0.97 us  [signed_units(): pl.pallas_call(signed_kernel, out_shape=jax.ShapeDtypeStruct(gate.shape,...]
    broadcast_in_dim x1 -> x0, other arithmetic: 0.82 us -> none  [body(): placed = jnp.where(spot == r, residual[r:r + 1].astype(f32), placed)]
    concatenate x1 -> x0, other arithmetic: 0.74 us -> none  [body(): jnp.concatenate([jnp.where(lower, stream, stream_other), jnp.where(lower,...]
  transfers between devices with their start and end apart: 9 -> 9, of which waited for: 8 -> 6; matrix products, arithmetic and copies ran while one was open for 2% -> 0% of each run, Pallas kernels for 8% -> 34%
where the time goes in v2:
time: 45.7 us; the launch traced here: 45.4 us
  Pallas kernels  21.1 us (46%)
  starting transfers between devices  15.1 us (33%)
  waiting for transfers between devices  7.46 us (16%)
  between operations  0.9 us (2%)
  other arithmetic  0.85 us (2%)
    ppermute x9, starting transfers between devices, exchange(): return lax.ppermute(block, axis, [(i, i ^ distance) for i in range(count)])  15.1 us
    pallas_call x4, Pallas kernels, load_rows(): pl.pallas_call(kernel, out_shape=pltpu.VMEM((count, weight.shape[1] // 2)...  9.21 us
    ppermute x9, waiting for transfers between devices, exchange(): return lax.ppermute(block, axis, [(i, i ^ distance) for i in range(count)])  7.46 us
    pallas_call x2, Pallas kernels, down_half(): pl.pallas_call(kernel, out_shape=tuple(out_shape), in_specs=[VMEM] * (1 +...  6.91 us
    pallas_call x2, Pallas kernels, qkv_half(): pl.pallas_call(kernel, out_shape=tuple((jax.ShapeDtypeStruct((size, width...  2.67 us
    pallas_call x1, Pallas kernels, signed_units(): pl.pallas_call(signed_kernel, out_shape=jax.ShapeDtypeStruct(gate.shape,...  0.97 us
  transfers between devices with their start and end apart: 9, of which 6 were waited for; matrix products, arithmetic and copies ran while one was open for 0% of the time, Pallas kernels for 34%

profile of v2, /device:TPU:0, one launch (start us, length us, event | category | flops | bytes accessed | tf_op | source)
XLA Modules:
  0.0 45.4 jit_solution(3503190266270470767)
XLA Ops:
  0.6 1.0 %signed_units.1.after_ref.own_ref = bf16[8,4096]{1,0:T(8,128)(2,1)S(1)} custom-call(bf16[8,4096]{1,0:T(8,128)(2,1)} %gate_hbm.1, bf16[8,4096]{1,0:T(8,128)(2,1)} %up_hbm.1, s32[1,4096]{1,0:T(1,128)} %bitcast.6), custom_call_target="tpu_custom_call" | custom-call | tf_op jit(solution)/shard_map/signed_units/pallas_call | solution.py:65
  1.6 3.0 %collective-permute-start = (bf16[8,4096]{1,0:T(8,128)(2,1)S(1)}, bf16[8,4096]{1,0:T(8,128)(2,1)S(1)}, u32[]{:S(2)}, u32[]{:S(2)}) collective-permute-start(bf16[8,4096]{1,0:T(8,128)(2,1)S(1)} %signed_units.1.after_ref.own_ref), channel_id=1, source_target_pairs={{0,2},{2,0},{4,6},{6,4},{8,10},{10,8},{12,14},{14,12},{1,3},{3,1},... | collective-permute-start | bytes 196616 | tf_op jit(solution)/shard_map/ppermute | solution.py:19
  4.6 2.6 %load_rows.4.refs_0_ = bf16[1408,2048]{1,0:T(8,128)(2,1)S(1)} custom-call(bf16[8,4096]{1,0:T(8,128)(2,1)S(1)} %signed_units.1.after_ref.own_ref, bf16[4096,4096]{1,0:T(8,128)(2,1)} %refs_2_.1), custom_call_target="tpu_custom_call" | custom-call | bytes 5767168 | tf_op jit(solution)/shard_map/load_rows/pallas_call | solution.py:189
  7.3 0.0 collective-permute-done.other_ref
  7.3 0.4 mix.1
  7.7 1.8 %collective-permute-start.1 = (bf16[8,4096]{1,0:T(8,128)(2,1)S(1)}, bf16[8,4096]{1,0:T(8,128)(2,1)S(1)}, u32[]{:S(2)}, u32[]{:S(2)}) collective-permute-start(bf16[8,4096]{1,0:T(8,128)(2,1)S(1)} %get-tuple-element.24.after_ref), channel_id=1, source_target_pairs={{0,4},{2,6},{4,0},{6,2},{8,12},{10,14},{12,8},{14,10},{1,5},{3,7},... | collective-permute-start | bytes 196616 | tf_op jit(solution)/shard_map/ppermute | solution.py:19
  9.5 2.6 %load_rows.5.refs_1_ = bf16[1408,2048]{1,0:T(8,128)(2,1)S(1)} custom-call(bf16[8,4096]{1,0:T(8,128)(2,1)S(1)} %get-tuple-element.24.after_ref, bf16[4096,4096]{1,0:T(8,128)(2,1)} %refs_2_.1), custom_call_target="tpu_custom_call" | custom-call | bytes 5767168 | tf_op jit(solution)/shard_map/load_rows/pallas_call | solution.py:189
  12.1 0.0 collective-permute-done.1.other_ref
  12.2 2.7 %collective-permute-start.2 = (bf16[8,4096]{1,0:T(8,128)(2,1)S(1)}, bf16[8,4096]{1,0:T(8,128)(2,1)S(1)}, u32[]{:S(2)}, u32[]{:S(2)}) collective-permute-start(bf16[8,4096]{1,0:T(8,128)(2,1)S(1)} %get-tuple-element.27.after_ref), channel_id=1, source_target_pairs={{0,8},{2,10},{4,12},{6,14},{8,0},{10,2},{12,4},{14,6},{1,9},{3,11}... | collective-permute-start | bytes 196616 | tf_op jit(solution)/shard_map/ppermute | solution.py:19
  14.9 2.5 %load_rows.6.refs_2_ = bf16[1280,2048]{1,0:T(8,128)(2,1)S(1)} custom-call(bf16[8,4096]{1,0:T(8,128)(2,1)S(1)} %get-tuple-element.27.after_ref, bf16[4096,4096]{1,0:T(8,128)(2,1)} %refs_2_.1), custom_call_target="tpu_custom_call" | custom-call | bytes 5242880 | tf_op jit(solution)/shard_map/load_rows/pallas_call | solution.py:189
  17.4 0.1 collective-permute-done.2.other_ref
  17.5 0.0 copy-start
  17.5 0.0 copy-start.1
  17.5 0.1 collective-permute-start.3
  17.6 1.4 %load_rows.7.refs_0_ = bf16[384,2048]{1,0:T(8,128)(2,1)S(1)} custom-call(bf16[8,4096]{1,0:T(8,128)(2,1)S(1)} %combine.3.after_ref, bf16[4096,4096]{1,0:T(8,128)(2,1)} %refs_2_.1), custom_call_target="tpu_custom_call" | custom-call | bytes 1572864 | tf_op jit(solution)/shard_map/load_rows/pallas_call | solution.py:189
  19.0 2.7 %down_other.1 = (f32[16,2048]{1,0:T(8,128)S(1)}, bf16[1408,2048]{1,0:T(8,128)(2,1)S(1)}) custom-call(bf16[16,4096]{1,0:T(8,128)(2,1)S(1)} %pad_maximum_fusion.x_ref, bf16[1408,2048]{1,0:T(8,128)(2,1)S(1)} %load_rows.4.refs_0_, bf16[1408,2048]{1,0:T(8,128)(2,1)S(1)} %load_rows.5.refs_1_, bf16[1280,2048]{1,0:T(8,128)(2,1)S(1)} %load_rows.6.refs_2_, ...), custom_call_target="tpu_custom_call" | custom-call | flops 268435456 | bytes 16777216 | tf_op jit(solution)/shard_map/down_other/pallas_call | solution.py:285
  21.7 1.6 %collective-permute-start.4 = (f32[16,2048]{1,0:T(8,128)S(1)}, f32[16,2048]{1,0:T(8,128)S(1)}, u32[]{:S(2)}, u32[]{:S(2)}) collective-permute-start(f32[16,2048]{1,0:T(8,128)S(1)} %get-tuple-element.35), channel_id=1, source_target_pairs={{0,2},{2,0},{4,6},{6,4},{8,10},{10,8},{12,14},{14,12},{1,3},{3,1},... | collective-permute-start | bytes 393224 | tf_op jit(solution)/shard_map/ppermute | solution.py:19
  23.3 4.2 %down_own.1.total_ref = f32[16,2048]{1,0:T(8,128)S(1)} custom-call(bf16[16,4096]{1,0:T(8,128)(2,1)S(1)} %pad_maximum_fusion.x_ref, bf16[384,2048]{1,0:T(8,128)(2,1)S(1)} %load_rows.7.refs_0_, bf16[1408,2048]{1,0:T(8,128)(2,1)S(1)} %get-tuple-element.34.refs_1_, bf16[4096,4096]{1,0:T(8,128)(2,1)} %refs_2_.1, s32[1,4096]{1,0:T(1,128)S(1)} %bitcast.5, ...), custom_call_target="tpu_custom_call" | custom-call | flops 268435456 | bytes 16777216 | tf_op jit(solution)/shard_map/down_own/pallas_call | solution.py:285
  27.6 0.1 collective-permute-done.4.arrived_ref
  27.7 1.7 %collective-permute-start.5 = (bf16[16,2048]{1,0:T(8,128)(2,1)S(1)}, bf16[16,2048]{1,0:T(8,128)(2,1)S(1)}, u32[]{:S(2)}, u32[]{:S(2)}) collective-permute-start(bf16[16,2048]{1,0:T(8,128)(2,1)S(1)} %get-tuple-element.37), channel_id=1, source_target_pairs={{0,4},{2,6},{4,0},{6,2},{8,12},{10,14},{12,8},{14,10},{1,5},{3,7},... | collective-permute-start | bytes 196616 | tf_op jit(solution)/shard_map/ppermute | solution.py:19
  29.4 2.7 %collective-permute-done.5.arrived_ref = bf16[16,2048]{1,0:T(8,128)(2,1)S(1)} collective-permute-done((bf16[16,2048]{1,0:T(8,128)(2,1)S(1)}, bf16[16,2048]{1,0:T(8,128)(2,1)S(1)}, u32[]{:S(2)}, u32[]{:S(2)}) %collective-permute-start.5) | collective-permute-done | bytes 65568 | tf_op jit(solution)/shard_map/ppermute | solution.py:19
  32.1 2.9 %collective-permute-start.6 = (bf16[16,2048]{1,0:T(8,128)(2,1)S(1)}, bf16[16,2048]{1,0:T(8,128)(2,1)S(1)}, u32[]{:S(2)}, u32[]{:S(2)}) collective-permute-start(bf16[16,2048]{1,0:T(8,128)(2,1)S(1)} %get-tuple-element.39), channel_id=1, source_target_pairs={{0,8},{2,10},{4,12},{6,14},{8,0},{10,2},{12,4},{14,6},{1,9},{3,11}... | collective-permute-start | bytes 196616 | tf_op jit(solution)/shard_map/ppermute | solution.py:19
  35.0 2.6 %collective-permute-done.6.arrived_ref = bf16[16,2048]{1,0:T(8,128)(2,1)S(1)} collective-permute-done((bf16[16,2048]{1,0:T(8,128)(2,1)S(1)}, bf16[16,2048]{1,0:T(8,128)(2,1)S(1)}, u32[]{:S(2)}, u32[]{:S(2)}) %collective-permute-start.6) | collective-permute-done | bytes 65568 | tf_op jit(solution)/shard_map/ppermute | solution.py:19
  37.6 1.3 %collective-permute-start.7 = (bf16[16,2048]{1,0:T(8,128)(2,1)S(1)}, bf16[16,2048]{1,0:T(8,128)(2,1)S(1)}, u32[]{:S(2)}, u32[]{:S(2)}) collective-permute-start(bf16[16,2048]{1,0:T(8,128)(2,1)S(1)} %add.19.own_ref.x_ref), channel_id=1, source_target_pairs={{0,2},{2,0},{4,6},{6,4},{8,10},{10,8},{12,14},{14,12},{1,3},{3,1},... | collective-permute-start | bytes 196616 | tf_op jit(solution)/shard_map/ppermute | solution.py:19
  39.0 1.3 %qkv_own.1.refs_0_ = f32[16,2432]{1,0:T(8,128)S(1)} custom-call(bf16[16,2048]{1,0:T(8,128)(2,1)S(1)} %add.19.own_ref.x_ref, bf16[1,4096]{1,0:T(2,128)(2,1)S(1)} %reshape.16.g_ref, bf16[4096,2304]{1,0:T(8,128)(2,1)S(1)} %bitcast.3), custom_call_target="tpu_custom_call" | custom-call | flops 150994944 | bytes 9437184 | tf_op jit(solution)/shard_map/qkv_own/pallas_call | solution.py:328
  40.3 1.6 %collective-permute-done.7.other_ref.x_ref = bf16[16,2048]{1,0:T(8,128)(2,1)S(1)} collective-permute-done((bf16[16,2048]{1,0:T(8,128)(2,1)S(1)}, bf16[16,2048]{1,0:T(8,128)(2,1)S(1)}, u32[]{:S(2)}, u32[]{:S(2)}) %collective-permute-start.7) | collective-permute-done | bytes 65568 | tf_op jit(solution)/shard_map/ppermute | solution.py:19
  41.9 1.3 %qkv_other.1 = (f32[8,2432]{1,0:T(8,128)S(1)}, f32[8,2432]{1,0:T(8,128)S(1)}) custom-call(bf16[16,2048]{1,0:T(8,128)(2,1)S(1)} %collective-permute-done.7.other_ref.x_ref, bf16[1,4096]{1,0:T(2,128)(2,1)S(1)} %reshape.16.g_ref, bf16[4096,2304]{1,0:T(8,128)(2,1)S(1)} %bitcast.3, f32[16,2432]{1,0:T(8,128)S(1)} %qkv_own.1.refs_0_), custom_call_target="tpu_custom_call" | custom-call | flops 150994944 | bytes 9437184 | tf_op jit(solution)/shard_map/qkv_other/pallas_call | solution.py:328
  43.2 0.1 collective-permute-start.8
  43.3 0.7 %take_rows.1 = bf16[2,4096]{1,0:T(2,128)(2,1)} custom-call(bf16[16,2048]{1,0:T(8,128)(2,1)S(1)} %add.19.own_ref.x_ref, bf16[16,2048]{1,0:T(8,128)(2,1)S(1)} %collective-permute-done.7.other_ref.x_ref), custom_call_target="tpu_custom_call" | custom-call | tf_op jit(solution)/shard_map/take_rows/pallas_call | solution.py:355
  44.0 0.5 %collective-permute-done.8 = f32[8,2432]{1,0:T(8,128)S(1)} collective-permute-done((f32[8,2432]{1,0:T(8,128)S(1)}, f32[8,2432]{1,0:T(8,128)S(1)}, u32[]{:S(2)}, u32[]{:S(2)}) %collective-permute-start.8) | collective-permute-done | bytes 77856 | tf_op jit(solution)/shard_map/ppermute | solution.py:19
  44.6 0.1 fusion.4
  44.7 0.7 %fusion.1 = bf16[8,2304]{1,0:T(8,128)(2,1)} fusion(f32[8,2432]{1,0:T(8,128)S(1)} %add.9, f32[2304]{0:T(1024)S(1)} %convert_multiply_fusion, f32[8]{0:T(128)S(1)} %fusion.4), kind=kLoop, calls=%fused_computation.3 | loop fusion | flops 55296 | bytes 119840 | tf_op jit(solution)/shard_map/convert_element_type | solution.py:423
  (27 shorter events, 0.2 us)
Async XLA Ops:
  1.6 5.7 %collective-permute-start = (bf16[8,4096]{1,0:T(8,128)(2,1)S(1)}, bf16[8,4096]{1,0:T(8,128)(2,1)S(1)}, u32[]{:S(2)}, u32[]{:S(2)}) collective-permute-start(bf16[8,4096]{1,0:T(8,128)(2,1)S(1)} %signed_units.1.after_ref.own_ref), channel_id=1, source_target_pairs={{0,2},{2,0},{4,6},{6,4},{8,10},{10,8},{12,14},{14,12},{1,3},{3,1},... | collective-permute-start | bytes 196616 | tf_op jit(solution)/shard_map/ppermute | solution.py:19
  7.7 4.4 %collective-permute-start.1 = (bf16[8,4096]{1,0:T(8,128)(2,1)S(1)}, bf16[8,4096]{1,0:T(8,128)(2,1)S(1)}, u32[]{:S(2)}, u32[]{:S(2)}) collective-permute-start(bf16[8,4096]{1,0:T(8,128)(2,1)S(1)} %get-tuple-element.24.after_ref), channel_id=1, source_target_pairs={{0,4},{2,6},{4,0},{6,2},{8,12},{10,14},{12,8},{14,10},{1,5},{3,7},... | collective-permute-start | bytes 196616 | tf_op jit(solution)/shard_map/ppermute | solution.py:19
  12.2 5.2 %collective-permute-start.2 = (bf16[8,4096]{1,0:T(8,128)(2,1)S(1)}, bf16[8,4096]{1,0:T(8,128)(2,1)S(1)}, u32[]{:S(2)}, u32[]{:S(2)}) collective-permute-start(bf16[8,4096]{1,0:T(8,128)(2,1)S(1)} %get-tuple-element.27.after_ref), channel_id=1, source_target_pairs={{0,8},{2,10},{4,12},{6,14},{8,0},{10,2},{12,4},{14,6},{1,9},{3,11}... | collective-permute-start | bytes 196616 | tf_op jit(solution)/shard_map/ppermute | solution.py:19
  17.5 1.6 %copy-start = (s32[4096]{0:T(1024)S(1)}, s32[4096]{0:T(1024)}, u32[]{:S(2)}) copy-start(s32[4096]{0:T(1024)} %param.13) | copy-start | bytes 49156
  17.5 1.6 %copy-start.1 = (bf16[2,4096]{1,0:T(2,128)(2,1)S(1)}, bf16[2,4096]{1,0:T(2,128)(2,1)}, u32[]{:S(2)}) copy-start(bf16[2,4096]{1,0:T(2,128)(2,1)} %refs_4_.1) | copy-start | bytes 49156
  17.5 1.5 %collective-permute-start.3 = (bf16[8,4096]{1,0:T(8,128)(2,1)S(1)}, bf16[8,4096]{1,0:T(8,128)(2,1)S(1)}, u32[]{:S(2)}, u32[]{:S(2)}) collective-permute-start(bf16[8,4096]{1,0:T(8,128)(2,1)S(1)} %combine.3.after_ref), channel_id=1, source_target_pairs={{0,1},{1,0},{2,3},{3,2},{4,5},{5,4},{6,7},{7,6},{8,9},{9,8},{10,11... | collective-permute-start | bytes 196616 | tf_op jit(solution)/shard_map/ppermute | solution.py:19
  21.7 5.9 %collective-permute-start.4 = (f32[16,2048]{1,0:T(8,128)S(1)}, f32[16,2048]{1,0:T(8,128)S(1)}, u32[]{:S(2)}, u32[]{:S(2)}) collective-permute-start(f32[16,2048]{1,0:T(8,128)S(1)} %get-tuple-element.35), channel_id=1, source_target_pairs={{0,2},{2,0},{4,6},{6,4},{8,10},{10,8},{12,14},{14,12},{1,3},{3,1},... | collective-permute-start | bytes 393224 | tf_op jit(solution)/shard_map/ppermute | solution.py:19
  27.7 4.3 %collective-permute-start.5 = (bf16[16,2048]{1,0:T(8,128)(2,1)S(1)}, bf16[16,2048]{1,0:T(8,128)(2,1)S(1)}, u32[]{:S(2)}, u32[]{:S(2)}) collective-permute-start(bf16[16,2048]{1,0:T(8,128)(2,1)S(1)} %get-tuple-element.37), channel_id=1, source_target_pairs={{0,4},{2,6},{4,0},{6,2},{8,12},{10,14},{12,8},{14,10},{1,5},{3,7},... | collective-permute-start | bytes 196616 | tf_op jit(solution)/shard_map/ppermute | solution.py:19
  32.0 6.9 %slice-start = ((s8[18874368]{0:T(1024)(128)(4,1)}), s8[4194304]{0:T(1024)(128)(4,1)S(1)}, s32[]{:S(2)}) async-start(s8[18874368]{0:T(1024)(128)(4,1)} %bitcast.2), calls=%async_computation | async-start | bytes 8388608
  32.0 6.9 %copy-start.3 = (bf16[4096]{0:T(1024)(128)(2,1)S(1)}, bf16[4096]{0:T(1024)(128)(2,1)}, u32[]{:S(2)}) copy-start(bf16[4096]{0:T(1024)(128)(2,1)} %param.15) | copy-start | bytes 24580
  32.0 6.9 %slice-start.1 = ((s8[18874368]{0:T(1024)(128)(4,1)}), s8[4194304]{0:T(1024)(128)(4,1)S(1)}, s32[]{:S(2)}) async-start(s8[18874368]{0:T(1024)(128)(4,1)} %bitcast.2), calls=%async_computation.1 | async-start | bytes 8388608
  32.0 6.9 %slice-start.2 = ((s8[18874368]{0:T(1024)(128)(4,1)}), s8[4194304]{0:T(1024)(128)(4,1)S(1)}, s32[]{:S(2)}) async-start(s8[18874368]{0:T(1024)(128)(4,1)} %bitcast.2), calls=%async_computation.2 | async-start | bytes 8388608
  32.0 6.9 %slice-start.3 = ((s8[18874368]{0:T(1024)(128)(4,1)}), s8[4194304]{0:T(1024)(128)(4,1)S(1)}, s32[]{:S(2)}) async-start(s8[18874368]{0:T(1024)(128)(4,1)} %bitcast.2), calls=%async_computation.3 | async-start | bytes 8388608
  32.0 6.9 %slice-start.4 = ((s8[18874368]{0:T(1024)(128)(4,1)}), s8[2097152]{0:T(1024)(128)(4,1)S(1)}, s32[]{:S(2)}) async-start(s8[18874368]{0:T(1024)(128)(4,1)} %bitcast.2), calls=%async_computation.4 | async-start | bytes 4194304
  32.1 5.5 %collective-permute-start.6 = (bf16[16,2048]{1,0:T(8,128)(2,1)S(1)}, bf16[16,2048]{1,0:T(8,128)(2,1)S(1)}, u32[]{:S(2)}, u32[]{:S(2)}) collective-permute-start(bf16[16,2048]{1,0:T(8,128)(2,1)S(1)} %get-tuple-element.39), channel_id=1, source_target_pairs={{0,8},{2,10},{4,12},{6,14},{8,0},{10,2},{12,4},{14,6},{1,9},{3,11}... | collective-permute-start | bytes 196616 | tf_op jit(solution)/shard_map/ppermute | solution.py:19
  37.6 4.3 %collective-permute-start.7 = (bf16[16,2048]{1,0:T(8,128)(2,1)S(1)}, bf16[16,2048]{1,0:T(8,128)(2,1)S(1)}, u32[]{:S(2)}, u32[]{:S(2)}) collective-permute-start(bf16[16,2048]{1,0:T(8,128)(2,1)S(1)} %add.19.own_ref.x_ref), channel_id=1, source_target_pairs={{0,2},{2,0},{4,6},{6,4},{8,10},{10,8},{12,14},{14,12},{1,3},{3,1},... | collective-permute-start | bytes 196616 | tf_op jit(solution)/shard_map/ppermute | solution.py:19
  40.3 3.0 %copy-start.2 = (s32[2304]{0:T(1024)S(1)}, s32[2304]{0:T(1024)}, u32[]{:S(2)}) copy-start(s32[2304]{0:T(1024)} %param.17) | copy-start | bytes 27652
  43.2 1.3 %collective-permute-start.8 = (f32[8,2432]{1,0:T(8,128)S(1)}, f32[8,2432]{1,0:T(8,128)S(1)}, u32[]{:S(2)}, u32[]{:S(2)}) collective-permute-start(f32[8,2432]{1,0:T(8,128)S(1)} %get-tuple-element.41), channel_id=1, source_target_pairs={{0,1},{1,0},{2,3},{3,2},{4,5},{5,4},{6,7},{7,6},{8,9},{9,8},{10,11... | collective-permute-start | bytes 233480 | tf_op jit(solution)/shard_map/ppermute | solution.py:19

commit v3 on v2

--- a/solution.py
+++ b/solution.py
@@ -31,8 +31,8 @@
     return pltpu.with_memory_space_constraint(array, pltpu.VMEM)
 
 
-def params(mib):
-    return pltpu.CompilerParams(vmem_limit_bytes=mib << 20)
+def params(mib, rows=16):
+    return pltpu.CompilerParams(vmem_limit_bytes=mib * max(1, rows // 16) << 20)
 
 
 def cost(flops, nbytes):
@@ -73,7 +73,8 @@
             pltpu.VMEM(signs.shape, jnp.int32),
             pltpu.SemaphoreType.DMA((3,)),
         ],
-        compiler_params=params(4),
+        compiler_params=params(2),
+        cost_estimate=cost(40_000_000_000, 64 << 20),
         name="signed_units",
     )(in_hbm(gate), in_hbm(up), in_hbm(signs))
 
@@ -93,12 +94,13 @@
     upper = bit_of("hid", 1) == 1
     own, other = own_ref[...].astype(f32), other_ref[...].astype(f32)
     stacked = jnp.concatenate([other, own], axis=0).astype(bf16)
+    count = width // lanes
+    tall = jnp.concatenate([stacked[:, j * lanes : (j + 1) * lanes] for j in range(count)], axis=0)
+    product = jnp.dot(tall, matrix, preferred_element_type=f32)
     blocks = []
-    for j in range(width // lanes):
-        product = jnp.dot(
-            stacked[:, j * lanes : (j + 1) * lanes], matrix, preferred_element_type=f32
-        )
-        theirs, mine = product[:rows], product[rows:]
+    for j in range(count):
+        theirs = product[2 * j * rows : (2 * j + 1) * rows]
+        mine = product[(2 * j + 1) * rows : (2 * j + 2) * rows]
         blocks.append(theirs + jnp.where(upper, -mine, mine))
     step = 1
     while step < len(blocks):
@@ -118,7 +120,7 @@
         out_shape=(jax.ShapeDtypeStruct(own.shape, f32), jax.ShapeDtypeStruct(own.shape, bf16)),
         in_specs=[VMEM] * 2,
         out_specs=(VMEM, VMEM),
-        compiler_params=params(4),
+        compiler_params=params(2),
         name="mix",
     )(own, other)
 
@@ -139,7 +141,7 @@
         out_shape=tuple(jax.ShapeDtypeStruct(wide.shape, t) for t in types),
         in_specs=[VMEM] * 2,
         out_specs=(VMEM,) * len(types),
-        compiler_params=params(4),
+        compiler_params=params(2),
         name="combine",
     )(wide, other)
 
@@ -157,7 +159,7 @@
         out_shape=tuple(jax.ShapeDtypeStruct(total.shape, t) for t in types),
         in_specs=[VMEM] * 2,
         out_specs=(VMEM,) * len(types),
-        compiler_params=params(4),
+        compiler_params=params(2, total.shape[0]),
         cost_estimate=cost(40_000_000_000, 0) if not last else None,
         name="add",
     )(total, arrived)
@@ -172,126 +174,53 @@
     return found
 
 
-def half_columns(weight_ref, start, count, other_half):
-    half = weight_ref.shape[1] // 2
-    side = bit_of("hid", 1)
-    if other_half:
-        side = 1 - side
-    return weight_ref.at[pl.ds(start, count), pl.ds(pl.multiple_of(side * half, half), half)]
-
-
-def load_rows(weight, start, count, other_half, after):
-    def kernel(after_ref, weight_ref, out_ref, sem):
-        copy = pltpu.make_async_copy(half_columns(weight_ref, start, count, other_half), out_ref, sem)
-        copy.start()
-        copy.wait()
-
-    return pl.pallas_call(
-        kernel,
-        out_shape=pltpu.VMEM((count, weight.shape[1] // 2), weight.dtype),
-        in_specs=[VMEM, HBM],
+def gather_rows(rows):
+    own_rows, depth = rows[0].shape
+
+    def kernel(*refs):
+        parts = [ref[...].astype(f32) for ref in refs[:-1]]
+        refs[-1][...] = jnp.concatenate(parts, axis=0).astype(bf16)
+
+    return pl.pallas_call(
+        kernel,
+        out_shape=jax.ShapeDtypeStruct((own_rows * len(rows), depth), bf16),
+        in_specs=[VMEM] * len(rows),
         out_specs=VMEM,
-        scratch_shapes=[pltpu.SemaphoreType.DMA],
-        compiler_params=params(2),
-        cost_estimate=cost(0, count * weight.shape[1]),
-        name="load_rows",
-    )(after, in_hbm(weight))
-
-
-def tie(first, second):
-    return lax.optimization_barrier((first, second))
-
-
-def down_half(rows, chunks, weight, scale, residual, own_rows, other_half, ahead):
+        compiler_params=params(2, own_rows * len(rows)),
+        name="gather_rows",
+    )(*rows)
+
+
+def down_half(rows, weight, scale, residual, own_rows, other_half, out_type):
     count, depth = rows.shape
     half = weight.shape[1] // 2
     bn = tile_of(half)
-    n_chunks = len(chunks)
-    starts = [sum(c.shape[0] for c in chunks[:i]) for i in range(n_chunks + 1)]
-    loaded = starts[-1]
-    rest = depth - loaded
-    pieces = max(p for p in (1, 2, 3, 4, 5, 6) if rest % (p * lanes) == 0) if rest else 0
-    piece = rest // max(pieces, 1)
-    first, few = ahead
-
-    def kernel(x_ref, *refs):
-        refs = list(refs)
-        chunk_refs = [refs.pop(0) for _ in range(n_chunks)]
-        w_ref, s_ref, r_ref, o_ref = (refs.pop(0) for _ in range(4))
-        if few:
-            ahead_ref = refs.pop(0)
-        if rest:
-            buf = refs.pop(0)
-        sems = refs.pop(0)
-        copies = [
-            pltpu.make_async_copy(
-                half_columns(w_ref, loaded + i * piece, piece, other_half),
-                buf.at[pl.ds(i * piece, piece)],
-                sems.at[i],
-            )
-            for i in range(pieces)
-        ]
-        if few:
-            copies.append(
-                pltpu.make_async_copy(
-                    half_columns(w_ref, first, few, not other_half), ahead_ref, sems.at[pieces]
-                )
-            )
-        for copy in copies:
-            copy.start()
+
+    def kernel(x_ref, w_ref, s_ref, r_ref, o_ref):
         side = bit_of("hid", 1)
         if other_half:
             side = 1 - side
         where = places(r_ref.shape[0], own_rows)
         index = lax.broadcasted_iota(jnp.int32, (count, bn), 0)
-        parts = [(refs_at, start, ref.shape[0]) for refs_at, (start, ref) in enumerate(zip(starts, chunk_refs))]
-        steps = [[(chunk_refs[i], start, 0, size) for i, start, size in parts]] if parts else []
-        for i in range(pieces):
-            steps.append([(buf, loaded + i * piece, i * piece, piece)])
-
-        for i, step in enumerate(steps):
-            if parts and i > 0:
-                copies[i - 1].wait()
-            elif not parts:
-                copies[i].wait()
-
-            @pl.loop(0, half // bn)
-            def _(n):
-                here = pl.ds(pl.multiple_of(n * bn, lanes), bn)
-                total = jnp.zeros((count, bn), f32) if i == 0 else o_ref[:, here]
-                for ref, x_at, at, size in step:
-                    total += jnp.dot(
-                        x_ref[:, x_at : x_at + size],
-                        ref[at : at + size, here],
-                        preferred_element_type=f32,
-                    )
-                if i == len(steps) - 1:
-                    there = pl.ds(pl.multiple_of(side * half + n * bn, lanes), bn)
-                    total = total * (s_ref[:, there].astype(f32) * 2.0 ** (-23))
-                    residual_rows = r_ref[:, there].astype(f32)
-                    for r, place in enumerate(where):
-                        total = total + jnp.where(index == place, residual_rows[r : r + 1], 0.0)
-                o_ref[:, here] = total
-
-        if few:
-            copies[-1].wait()
-
-    out_shape = [jax.ShapeDtypeStruct((count, half), f32)]
-    scratch = [pltpu.SemaphoreType.DMA((pieces + 1,))]
-    if few:
-        out_shape.append(pltpu.VMEM((few, half), weight.dtype))
-    if rest:
-        scratch.insert(0, pltpu.VMEM((rest, half), bf16))
-    return pl.pallas_call(
-        kernel,
-        out_shape=tuple(out_shape),
-        in_specs=[VMEM] * (1 + n_chunks) + [HBM, VMEM, VMEM],
-        out_specs=(VMEM,) * len(out_shape),
-        scratch_shapes=scratch,
-        compiler_params=params(14),
+
+        for n in range(half // bn):
+            there = pl.ds(pl.multiple_of(side * half + n * bn, lanes), bn)
+            total = jnp.dot(x_ref[...], w_ref[:, there], preferred_element_type=f32)
+            total = total * (s_ref[:, there].astype(f32) * 2.0 ** (-23))
+            residual_rows = r_ref[:, there].astype(f32)
+            for r, place in enumerate(where):
+                total = total + jnp.where(index == place, residual_rows[r : r + 1], 0.0)
+            o_ref[:, n * bn : (n + 1) * bn] = total.astype(out_type)
+
+    return pl.pallas_call(
+        kernel,
+        out_shape=jax.ShapeDtypeStruct((count, half), out_type),
+        in_specs=[VMEM] * 4,
+        out_specs=VMEM,
+        compiler_params=params(14, count),
         cost_estimate=cost(2 * count * depth * half, 2 * depth * half),
         name="down_other" if other_half else "down_own",
-    )(rows, *map(in_vmem, chunks), in_hbm(weight), scale, residual)
+    )(rows, weight, scale, residual)
 
 
 def qkv_half(stream, gain, weight, before, own_rows):
@@ -331,7 +260,7 @@
         in_specs=[VMEM] * len(operands),
         out_specs=(VMEM,) * len(first_rows),
         scratch_shapes=[pltpu.VMEM((count, depth), bf16)],
-        compiler_params=params(4),
+        compiler_params=params(2, count),
         cost_estimate=cost(2 * count * depth * width, 2 * depth * width),
         name="qkv_own" if own_half else "qkv_other",
     )(*operands)
@@ -357,7 +286,7 @@
         out_shape=jax.ShapeDtypeStruct((res_rows, 2 * half), bf16),
         in_specs=[VMEM] * 2,
         out_specs=VMEM,
-        compiler_params=params(4),
+        compiler_params=params(2, count),
         name="take_rows",
     )(stream, stream_other)
 
@@ -379,15 +308,8 @@
     distances = [1 << b for b in range(hid.bit_length() - 1)]
 
     send = signed_units(gate_proj, up_proj, hadamard_signs)
-    chunks, loaded = [], 0
-    share = -(-depth // len(distances) // lanes) * lanes
     for k, distance in enumerate(distances):
         other = exchange(send, "hid", distance)
-        count = min(share, depth - loaded)
-        chunk = load_rows(down_codes, loaded, count, True, send)
-        other, chunk = tie(other, chunk)
-        chunks.append(chunk)
-        loaded += count
         last = k == len(distances) - 1
         if k == 0:
             wide, send = mix(send, other)
@@ -396,17 +318,12 @@
         else:
             (rotated,) = combine(wide, other, distance, 1.0 / math.sqrt(depth * hid))
     rows = [rotated] + [exchange(rotated, "row", j) for j in range(1, n_row)]
-    early = depth * 3 // 32 // lanes * lanes
-    own_chunk = load_rows(down_codes, 0, early, False, rotated)
-    rows[-1], own_chunk = tie(rows[-1], own_chunk)
-    rows = jnp.concatenate(rows, axis=0)
+    rows = gather_rows(rows)
 
     scale = down_scales.reshape(1, -1)
-    ahead = (early, depth * 11 // 32 // lanes * lanes)
-    theirs, next_chunk = down_half(rows, chunks, down_codes, scale, residual, own_rows, True, ahead)
+    theirs = down_half(rows, down_codes, scale, residual, own_rows, True, bf16)
     arrived = exchange(theirs, "hid", 1)
-    own_chunks = [own_chunk, next_chunk]
-    (total,) = down_half(rows, own_chunks, down_codes, scale, residual, own_rows, False, (0, 0))
+    total = down_half(rows, down_codes, scale, residual, own_rows, False, f32)
     for distance in distances[1:]:
         total, send = add(total, arrived, False, distance == 2)
         arrived = exchange(send, "hid", distance)

time: 45.7 us -> 42.9 us (0.939)
  Pallas kernels: 21.1 us -> 9.45 us
  waiting for transfers between devices: 7.46 us -> 14.4 us
  starting transfers between devices: 15.1 us -> 17.1 us
    pallas_call x6 -> x3, Pallas kernels: 16.1 us -> 4.58 us  [the longest x2 4.57 us: down_half(): pl.pallas_call(kernel, out_shape=jax.ShapeDtypeStruct((count, half), out_...]
    ppermute x9, waiting for transfers between devices: 7.46 us -> 14.4 us  [exchange(): return lax.ppermute(block, axis, [(i, i ^ distance) for i in range(count)])]
    ppermute x9, starting transfers between devices: 15.1 us -> 17.1 us  [exchange(): return lax.ppermute(block, axis, [(i, i ^ distance) for i in range(count)])]
  transfers between devices with their start and end apart: 9 -> 9, of which waited for: 6 -> 9; matrix products, arithmetic and copies ran while one was open for 0% -> 0% of each run, Pallas kernels for 34% -> 10%
where the time goes in v3:
time: 42.9 us; the launch traced here: 42.7 us
  starting transfers between devices  17.1 us (40%)
  waiting for transfers between devices  14.4 us (34%)
  Pallas kernels  9.45 us (22%)
  other arithmetic  0.84 us (2%)
  between operations  0.83 us (2%)
    ppermute x9, starting transfers between devices, exchange(): return lax.ppermute(block, axis, [(i, i ^ distance) for i in range(count)])  17.1 us
    ppermute x9, waiting for transfers between devices, exchange(): return lax.ppermute(block, axis, [(i, i ^ distance) for i in range(count)])  14.4 us
    pallas_call x2, Pallas kernels, down_half(): pl.pallas_call(kernel, out_shape=jax.ShapeDtypeStruct((count, half), out_...  4.57 us
    pallas_call x2, Pallas kernels, qkv_half(): pl.pallas_call(kernel, out_shape=tuple((jax.ShapeDtypeStruct((size, width...  2.67 us
    pallas_call x1, Pallas kernels, signed_units(): pl.pallas_call(signed_kernel, out_shape=jax.ShapeDtypeStruct(gate.shape,...  1.12 us
  transfers between devices with their start and end apart: 9, of which 9 were waited for; matrix products, arithmetic and copies ran while one was open for 0% of the time, Pallas kernels for 10%

profile of v3, /device:TPU:0, one launch (start us, length us, event | category | flops | bytes accessed | tf_op | source)
XLA Modules:
  0.0 42.7 jit_solution(14766813877757614377)
XLA Ops:
  0.6 0.0 copy-start
  0.6 0.0 copy-start.1
  0.7 0.0 copy-start.2
  0.7 1.1 %signed_units.1.own_ref = bf16[8,4096]{1,0:T(8,128)(2,1)S(1)} custom-call(bf16[8,4096]{1,0:T(8,128)(2,1)} %gate_hbm.1, bf16[8,4096]{1,0:T(8,128)(2,1)} %up_hbm.1, s32[1,4096]{1,0:T(1,128)} %bitcast.6), custom_call_target="tpu_custom_call" | custom-call | flops 40000000000 | bytes 67108864 | tf_op jit(solution)/shard_map/signed_units/pallas_call | solution.py:65
  1.8 3.0 %collective-permute-start = (bf16[8,4096]{1,0:T(8,128)(2,1)S(1)}, bf16[8,4096]{1,0:T(8,128)(2,1)S(1)}, u32[]{:S(2)}, u32[]{:S(2)}) collective-permute-start(bf16[8,4096]{1,0:T(8,128)(2,1)S(1)} %signed_units.1.own_ref), channel_id=1, source_target_pairs={{0,2},{2,0},{4,6},{6,4},{8,10},{10,8},{12,14},{14,12},{1,3},{3,1},... | collective-permute-start | bytes 196616 | tf_op jit(solution)/shard_map/ppermute | solution.py:19
  4.8 2.2 %collective-permute-done.other_ref = bf16[8,4096]{1,0:T(8,128)(2,1)S(1)} collective-permute-done((bf16[8,4096]{1,0:T(8,128)(2,1)S(1)}, bf16[8,4096]{1,0:T(8,128)(2,1)S(1)}, u32[]{:S(2)}, u32[]{:S(2)}) %collective-permute-start) | collective-permute-done | bytes 65568 | tf_op jit(solution)/shard_map/ppermute | solution.py:19
  7.0 0.2 mix.1
  7.3 2.2 %collective-permute-start.1 = (bf16[8,4096]{1,0:T(8,128)(2,1)S(1)}, bf16[8,4096]{1,0:T(8,128)(2,1)S(1)}, u32[]{:S(2)}, u32[]{:S(2)}) collective-permute-start(bf16[8,4096]{1,0:T(8,128)(2,1)S(1)} %get-tuple-element.13), channel_id=1, source_target_pairs={{0,4},{2,6},{4,0},{6,2},{8,12},{10,14},{12,8},{14,10},{1,5},{3,7},... | collective-permute-start | bytes 196616 | tf_op jit(solution)/shard_map/ppermute | solution.py:19
  9.4 2.2 %collective-permute-done.1.other_ref = bf16[8,4096]{1,0:T(8,128)(2,1)S(1)} collective-permute-done((bf16[8,4096]{1,0:T(8,128)(2,1)S(1)}, bf16[8,4096]{1,0:T(8,128)(2,1)S(1)}, u32[]{:S(2)}, u32[]{:S(2)}) %collective-permute-start.1) | collective-permute-done | bytes 65568 | tf_op jit(solution)/shard_map/ppermute | solution.py:19
  11.7 3.1 %collective-permute-start.2 = (bf16[8,4096]{1,0:T(8,128)(2,1)S(1)}, bf16[8,4096]{1,0:T(8,128)(2,1)S(1)}, u32[]{:S(2)}, u32[]{:S(2)}) collective-permute-start(bf16[8,4096]{1,0:T(8,128)(2,1)S(1)} %get-tuple-element.15), channel_id=1, source_target_pairs={{0,8},{2,10},{4,12},{6,14},{8,0},{10,2},{12,4},{14,6},{1,9},{3,11}... | collective-permute-start | bytes 196616 | tf_op jit(solution)/shard_map/ppermute | solution.py:19
  14.8 2.2 %collective-permute-done.2.other_ref = bf16[8,4096]{1,0:T(8,128)(2,1)S(1)} collective-permute-done((bf16[8,4096]{1,0:T(8,128)(2,1)S(1)}, bf16[8,4096]{1,0:T(8,128)(2,1)S(1)}, u32[]{:S(2)}, u32[]{:S(2)}) %collective-permute-start.2) | collective-permute-done | bytes 65568 | tf_op jit(solution)/shard_map/ppermute | solution.py:19
  17.1 0.1 collective-permute-start.3
  17.2 1.2 %collective-permute-done.3.refs_1_ = bf16[8,4096]{1,0:T(8,128)(2,1)S(1)} collective-permute-done((bf16[8,4096]{1,0:T(8,128)(2,1)S(1)}, bf16[8,4096]{1,0:T(8,128)(2,1)S(1)}, u32[]{:S(2)}, u32[]{:S(2)}) %collective-permute-start.3) | collective-permute-done | bytes 65568 | tf_op jit(solution)/shard_map/ppermute | solution.py:19
  18.4 0.0 copy-done
  18.5 2.3 %down_other.1 = bf16[16,2048]{1,0:T(8,128)(2,1)S(1)} custom-call(bf16[16,4096]{1,0:T(8,128)(2,1)S(1)} %gather_rows.1.x_ref, bf16[4096,4096]{1,0:T(8,128)(2,1)S(1)} %copy-done, s32[1,4096]{1,0:T(1,128)S(1)} %bitcast.4, bf16[2,4096]{1,0:T(2,128)(2,1)S(1)} %copy-done.2), custom_call_target="tpu_custom_call" | custom-call | flops 268435456 | bytes 16777216 | tf_op jit(solution)/shard_map/down_other/pallas_call | solution.py:215
  20.8 1.8 %collective-permute-start.4 = (bf16[16,2048]{1,0:T(8,128)(2,1)S(1)}, bf16[16,2048]{1,0:T(8,128)(2,1)S(1)}, u32[]{:S(2)}, u32[]{:S(2)}) collective-permute-start(bf16[16,2048]{1,0:T(8,128)(2,1)S(1)} %down_other.1), channel_id=1, source_target_pairs={{0,2},{2,0},{4,6},{6,4},{8,10},{10,8},{12,14},{14,12},{1,3},{3,1},... | collective-permute-start | bytes 196616 | tf_op jit(solution)/shard_map/ppermute | solution.py:19
  22.6 2.3 %down_own.1.total_ref = f32[16,2048]{1,0:T(8,128)S(1)} custom-call(bf16[16,4096]{1,0:T(8,128)(2,1)S(1)} %gather_rows.1.x_ref, bf16[4096,4096]{1,0:T(8,128)(2,1)S(1)} %copy-done, s32[1,4096]{1,0:T(1,128)S(1)} %bitcast.5, bf16[2,4096]{1,0:T(2,128)(2,1)S(1)} %copy-done.2), custom_call_target="tpu_custom_call" | custom-call | flops 268435456 | bytes 16777216 | tf_op jit(solution)/shard_map/down_own/pallas_call | solution.py:215
  24.9 0.2 collective-permute-done.4.arrived_ref
  25.1 2.0 %collective-permute-start.5 = (bf16[16,2048]{1,0:T(8,128)(2,1)S(1)}, bf16[16,2048]{1,0:T(8,128)(2,1)S(1)}, u32[]{:S(2)}, u32[]{:S(2)}) collective-permute-start(bf16[16,2048]{1,0:T(8,128)(2,1)S(1)} %get-tuple-element.17), channel_id=1, source_target_pairs={{0,4},{2,6},{4,0},{6,2},{8,12},{10,14},{12,8},{14,10},{1,5},{3,7},... | collective-permute-start | bytes 196616 | tf_op jit(solution)/shard_map/ppermute | solution.py:19
  27.0 2.4 %collective-permute-done.5.arrived_ref = bf16[16,2048]{1,0:T(8,128)(2,1)S(1)} collective-permute-done((bf16[16,2048]{1,0:T(8,128)(2,1)S(1)}, bf16[16,2048]{1,0:T(8,128)(2,1)S(1)}, u32[]{:S(2)}, u32[]{:S(2)}) %collective-permute-start.5) | collective-permute-done | bytes 65568 | tf_op jit(solution)/shard_map/ppermute | solution.py:19
  29.4 0.0 copy-start.3
  29.4 3.1 %collective-permute-start.6 = (bf16[16,2048]{1,0:T(8,128)(2,1)S(1)}, bf16[16,2048]{1,0:T(8,128)(2,1)S(1)}, u32[]{:S(2)}, u32[]{:S(2)}) collective-permute-start(bf16[16,2048]{1,0:T(8,128)(2,1)S(1)} %get-tuple-element.19), channel_id=1, source_target_pairs={{0,8},{2,10},{4,12},{6,14},{8,0},{10,2},{12,4},{14,6},{1,9},{3,11}... | collective-permute-start | bytes 196616 | tf_op jit(solution)/shard_map/ppermute | solution.py:19
  32.6 2.2 %collective-permute-done.6.arrived_ref = bf16[16,2048]{1,0:T(8,128)(2,1)S(1)} collective-permute-done((bf16[16,2048]{1,0:T(8,128)(2,1)S(1)}, bf16[16,2048]{1,0:T(8,128)(2,1)S(1)}, u32[]{:S(2)}, u32[]{:S(2)}) %collective-permute-start.6) | collective-permute-done | bytes 65568 | tf_op jit(solution)/shard_map/ppermute | solution.py:19
  34.8 1.7 %collective-permute-start.7 = (bf16[16,2048]{1,0:T(8,128)(2,1)S(1)}, bf16[16,2048]{1,0:T(8,128)(2,1)S(1)}, u32[]{:S(2)}, u32[]{:S(2)}) collective-permute-start(bf16[16,2048]{1,0:T(8,128)(2,1)S(1)} %add.19.own_ref.x_ref), channel_id=1, source_target_pairs={{0,2},{2,0},{4,6},{6,4},{8,10},{10,8},{12,14},{14,12},{1,3},{3,1},... | collective-permute-start | bytes 196616 | tf_op jit(solution)/shard_map/ppermute | solution.py:19
  36.7 1.3 %qkv_own.1.refs_0_ = f32[16,2432]{1,0:T(8,128)S(1)} custom-call(bf16[16,2048]{1,0:T(8,128)(2,1)S(1)} %add.19.own_ref.x_ref, bf16[1,4096]{1,0:T(2,128)(2,1)S(1)} %reshape.16.g_ref, bf16[4096,2304]{1,0:T(8,128)(2,1)S(1)} %bitcast.3), custom_call_target="tpu_custom_call" | custom-call | flops 150994944 | bytes 9437184 | tf_op jit(solution)/shard_map/qkv_own/pallas_call | solution.py:257
  38.0 1.2 %collective-permute-done.7.other_ref.x_ref = bf16[16,2048]{1,0:T(8,128)(2,1)S(1)} collective-permute-done((bf16[16,2048]{1,0:T(8,128)(2,1)S(1)}, bf16[16,2048]{1,0:T(8,128)(2,1)S(1)}, u32[]{:S(2)}, u32[]{:S(2)}) %collective-permute-start.7) | collective-permute-done | bytes 65568 | tf_op jit(solution)/shard_map/ppermute | solution.py:19
  39.2 1.3 %qkv_other.1 = (f32[8,2432]{1,0:T(8,128)S(1)}, f32[8,2432]{1,0:T(8,128)S(1)}) custom-call(bf16[16,2048]{1,0:T(8,128)(2,1)S(1)} %collective-permute-done.7.other_ref.x_ref, bf16[1,4096]{1,0:T(2,128)(2,1)S(1)} %reshape.16.g_ref, bf16[4096,2304]{1,0:T(8,128)(2,1)S(1)} %bitcast.3, f32[16,2432]{1,0:T(8,128)S(1)} %qkv_own.1.refs_0_), custom_call_target="tpu_custom_call" | custom-call | flops 150994944 | bytes 9437184 | tf_op jit(solution)/shard_map/qkv_other/pallas_call | solution.py:257
  40.5 0.1 collective-permute-start.8
  40.6 0.7 %take_rows.1 = bf16[2,4096]{1,0:T(2,128)(2,1)} custom-call(bf16[16,2048]{1,0:T(8,128)(2,1)S(1)} %add.19.own_ref.x_ref, bf16[16,2048]{1,0:T(8,128)(2,1)S(1)} %collective-permute-done.7.other_ref.x_ref), custom_call_target="tpu_custom_call" | custom-call | tf_op jit(solution)/shard_map/take_rows/pallas_call | solution.py:284
  41.3 0.5 %collective-permute-done.8 = f32[8,2432]{1,0:T(8,128)S(1)} collective-permute-done((f32[8,2432]{1,0:T(8,128)S(1)}, f32[8,2432]{1,0:T(8,128)S(1)}, u32[]{:S(2)}, u32[]{:S(2)}) %collective-permute-start.8) | collective-permute-done | bytes 77856 | tf_op jit(solution)/shard_map/ppermute | solution.py:19
  41.8 0.1 fusion.4
  42.0 0.7 %fusion.1 = bf16[8,2304]{1,0:T(8,128)(2,1)} fusion(f32[8,2432]{1,0:T(8,128)S(1)} %add.9, f32[2304]{0:T(1024)S(1)} %convert_multiply_fusion, f32[8]{0:T(128)S(1)} %fusion.4), kind=kLoop, calls=%fused_computation.2 | loop fusion | flops 55296 | bytes 119840 | tf_op jit(solution)/shard_map/convert_element_type | solution.py:340
  (25 shorter events, 0.2 us)
Async XLA Ops:
  0.6 17.8 %copy-start = (bf16[4096,4096]{1,0:T(8,128)(2,1)S(1)}, bf16[4096,4096]{1,0:T(8,128)(2,1)}, u32[]{:S(2)}) copy-start(bf16[4096,4096]{1,0:T(8,128)(2,1)} %w_ref.5) | copy-start | bytes 100663296
  0.6 17.8 %copy-start.1 = (s32[4096]{0:T(1024)S(1)}, s32[4096]{0:T(1024)}, u32[]{:S(2)}) copy-start(s32[4096]{0:T(1024)} %param.13) | copy-start | bytes 49156
  0.7 17.8 %copy-start.2 = (bf16[2,4096]{1,0:T(2,128)(2,1)S(1)}, bf16[2,4096]{1,0:T(2,128)(2,1)}, u32[]{:S(2)}) copy-start(bf16[2,4096]{1,0:T(2,128)(2,1)} %r_ref.3) | copy-start | bytes 49156
  1.8 5.2 %collective-permute-start = (bf16[8,4096]{1,0:T(8,128)(2,1)S(1)}, bf16[8,4096]{1,0:T(8,128)(2,1)S(1)}, u32[]{:S(2)}, u32[]{:S(2)}) collective-permute-start(bf16[8,4096]{1,0:T(8,128)(2,1)S(1)} %signed_units.1.own_ref), channel_id=1, source_target_pairs={{0,2},{2,0},{4,6},{6,4},{8,10},{10,8},{12,14},{14,12},{1,3},{3,1},... | collective-permute-start | bytes 196616 | tf_op jit(solution)/shard_map/ppermute | solution.py:19
  7.3 4.4 %collective-permute-start.1 = (bf16[8,4096]{1,0:T(8,128)(2,1)S(1)}, bf16[8,4096]{1,0:T(8,128)(2,1)S(1)}, u32[]{:S(2)}, u32[]{:S(2)}) collective-permute-start(bf16[8,4096]{1,0:T(8,128)(2,1)S(1)} %get-tuple-element.13), channel_id=1, source_target_pairs={{0,4},{2,6},{4,0},{6,2},{8,12},{10,14},{12,8},{14,10},{1,5},{3,7},... | collective-permute-start | bytes 196616 | tf_op jit(solution)/shard_map/ppermute | solution.py:19
  11.7 5.3 %collective-permute-start.2 = (bf16[8,4096]{1,0:T(8,128)(2,1)S(1)}, bf16[8,4096]{1,0:T(8,128)(2,1)S(1)}, u32[]{:S(2)}, u32[]{:S(2)}) collective-permute-start(bf16[8,4096]{1,0:T(8,128)(2,1)S(1)} %get-tuple-element.15), channel_id=1, source_target_pairs={{0,8},{2,10},{4,12},{6,14},{8,0},{10,2},{12,4},{14,6},{1,9},{3,11}... | collective-permute-start | bytes 196616 | tf_op jit(solution)/shard_map/ppermute | solution.py:19
  17.1 1.3 %collective-permute-start.3 = (bf16[8,4096]{1,0:T(8,128)(2,1)S(1)}, bf16[8,4096]{1,0:T(8,128)(2,1)S(1)}, u32[]{:S(2)}, u32[]{:S(2)}) collective-permute-start(bf16[8,4096]{1,0:T(8,128)(2,1)S(1)} %combine.3.refs_0_), channel_id=1, source_target_pairs={{0,1},{1,0},{2,3},{3,2},{4,5},{5,4},{6,7},{7,6},{8,9},{9,8},{10,11... | collective-permute-start | bytes 196616 | tf_op jit(solution)/shard_map/ppermute | solution.py:19
  20.8 4.3 %collective-permute-start.4 = (bf16[16,2048]{1,0:T(8,128)(2,1)S(1)}, bf16[16,2048]{1,0:T(8,128)(2,1)S(1)}, u32[]{:S(2)}, u32[]{:S(2)}) collective-permute-start(bf16[16,2048]{1,0:T(8,128)(2,1)S(1)} %down_other.1), channel_id=1, source_target_pairs={{0,2},{2,0},{4,6},{6,4},{8,10},{10,8},{12,14},{14,12},{1,3},{3,1},... | collective-permute-start | bytes 196616 | tf_op jit(solution)/shard_map/ppermute | solution.py:19
  25.1 11.6 %slice-start = ((s8[18874368]{0:T(1024)(128)(4,1)}), s8[4194304]{0:T(1024)(128)(4,1)S(1)}, s32[]{:S(2)}) async-start(s8[18874368]{0:T(1024)(128)(4,1)} %bitcast.2), calls=%async_computation | async-start | bytes 8388608
  25.1 11.6 %slice-start.1 = ((s8[18874368]{0:T(1024)(128)(4,1)}), s8[4194304]{0:T(1024)(128)(4,1)S(1)}, s32[]{:S(2)}) async-start(s8[18874368]{0:T(1024)(128)(4,1)} %bitcast.2), calls=%async_computation.1 | async-start | bytes 8388608
  25.1 11.6 %slice-start.2 = ((s8[18874368]{0:T(1024)(128)(4,1)}), s8[4194304]{0:T(1024)(128)(4,1)S(1)}, s32[]{:S(2)}) async-start(s8[18874368]{0:T(1024)(128)(4,1)} %bitcast.2), calls=%async_computation.2 | async-start | bytes 8388608
  25.1 4.3 %collective-permute-start.5 = (bf16[16,2048]{1,0:T(8,128)(2,1)S(1)}, bf16[16,2048]{1,0:T(8,128)(2,1)S(1)}, u32[]{:S(2)}, u32[]{:S(2)}) collective-permute-start(bf16[16,2048]{1,0:T(8,128)(2,1)S(1)} %get-tuple-element.17), channel_id=1, source_target_pairs={{0,4},{2,6},{4,0},{6,2},{8,12},{10,14},{12,8},{14,10},{1,5},{3,7},... | collective-permute-start | bytes 196616 | tf_op jit(solution)/shard_map/ppermute | solution.py:19
  29.4 7.2 %copy-start.4 = (bf16[4096]{0:T(1024)(128)(2,1)S(1)}, bf16[4096]{0:T(1024)(128)(2,1)}, u32[]{:S(2)}) copy-start(bf16[4096]{0:T(1024)(128)(2,1)} %param.15) | copy-start | bytes 24580
  29.4 7.2 %slice-start.3 = ((s8[18874368]{0:T(1024)(128)(4,1)}), s8[4194304]{0:T(1024)(128)(4,1)S(1)}, s32[]{:S(2)}) async-start(s8[18874368]{0:T(1024)(128)(4,1)} %bitcast.2), calls=%async_computation.3 | async-start | bytes 8388608
  29.4 7.2 %slice-start.4 = ((s8[18874368]{0:T(1024)(128)(4,1)}), s8[2097152]{0:T(1024)(128)(4,1)S(1)}, s32[]{:S(2)}) async-start(s8[18874368]{0:T(1024)(128)(4,1)} %bitcast.2), calls=%async_computation.4 | async-start | bytes 4194304
  29.4 11.1 %copy-start.3 = (s32[2304]{0:T(1024)S(1)}, s32[2304]{0:T(1024)}, u32[]{:S(2)}) copy-start(s32[2304]{0:T(1024)} %param.17) | copy-start | bytes 27652
  29.4 5.4 %collective-permute-start.6 = (bf16[16,2048]{1,0:T(8,128)(2,1)S(1)}, bf16[16,2048]{1,0:T(8,128)(2,1)S(1)}, u32[]{:S(2)}, u32[]{:S(2)}) collective-permute-start(bf16[16,2048]{1,0:T(8,128)(2,1)S(1)} %get-tuple-element.19), channel_id=1, source_target_pairs={{0,8},{2,10},{4,12},{6,14},{8,0},{10,2},{12,4},{14,6},{1,9},{3,11}... | collective-permute-start | bytes 196616 | tf_op jit(solution)/shard_map/ppermute | solution.py:19
  34.8 4.3 %collective-permute-start.7 = (bf16[16,2048]{1,0:T(8,128)(2,1)S(1)}, bf16[16,2048]{1,0:T(8,128)(2,1)S(1)}, u32[]{:S(2)}, u32[]{:S(2)}) collective-permute-start(bf16[16,2048]{1,0:T(8,128)(2,1)S(1)} %add.19.own_ref.x_ref), channel_id=1, source_target_pairs={{0,2},{2,0},{4,6},{6,4},{8,10},{10,8},{12,14},{14,12},{1,3},{3,1},... | collective-permute-start | bytes 196616 | tf_op jit(solution)/shard_map/ppermute | solution.py:19
  40.5 1.3 %collective-permute-start.8 = (f32[8,2432]{1,0:T(8,128)S(1)}, f32[8,2432]{1,0:T(8,128)S(1)}, u32[]{:S(2)}, u32[]{:S(2)}) collective-permute-start(f32[8,2432]{1,0:T(8,128)S(1)} %get-tuple-element.21), channel_id=1, source_target_pairs={{0,1},{1,0},{2,3},{3,2},{4,5},{5,4},{6,7},{7,6},{8,9},{9,8},{10,11... | collective-permute-start | bytes 233480 | tf_op jit(solution)/shard_map/ppermute | solution.py:19

commit v4 on v3

--- a/solution.py
+++ b/solution.py
@@ -74,7 +74,6 @@
             pltpu.SemaphoreType.DMA((3,)),
         ],
         compiler_params=params(2),
-        cost_estimate=cost(40_000_000_000, 64 << 20),
         name="signed_units",
     )(in_hbm(gate), in_hbm(up), in_hbm(signs))
 
@@ -121,6 +120,7 @@
         in_specs=[VMEM] * 2,
         out_specs=(VMEM, VMEM),
         compiler_params=params(2),
+        cost_estimate=cost(400_000_000_000, 0),
         name="mix",
     )(own, other)
 
@@ -289,6 +289,29 @@
         compiler_params=params(2, count),
         name="take_rows",
     )(stream, stream_other)
+
+
+def finish(mine, arrived, scales, features):
+    rows, wide = mine.shape
+    width = wide - lanes
+
+    def kernel(*refs):
+        mine_ref, scale_ref, out_ref = refs[0], refs[-2], refs[-1]
+        total = mine_ref[...]
+        for ref in refs[1:-2]:
+            total = total + ref[...]
+        inverse = lax.rsqrt(total[:, width : width + 1] / features + epsilon)
+        output_scale = scale_ref[...].astype(f32) * 2.0 ** (-22)
+        out_ref[...] = (total[:, :width] * inverse * output_scale).astype(bf16)
+
+    return pl.pallas_call(
+        kernel,
+        out_shape=jax.ShapeDtypeStruct((rows, width), bf16),
+        in_specs=[VMEM] * (2 + len(arrived)),
+        out_specs=VMEM,
+        compiler_params=params(2 * (1 + len(arrived))),
+        name="finish",
+    )(mine, *arrived, scales)
 
 
 def body(
@@ -333,11 +356,8 @@
     gain = norm_gain.reshape(1, -1)
     (part,) = qkv_half(stream, gain, qkv_codes, None, own_rows)
     mine, rest = qkv_half(stream_other, gain, qkv_codes, part, own_rows)
-    for j in range(1, n_row):
-        mine = mine + exchange(rest[(j - 1) * own_rows : j * own_rows], "row", j)
-    width = qkv_codes.shape[1]
-    inverse = lax.rsqrt(mine[:, width : width + 1] / (features * n_row) + epsilon)
-    joined_qkv = (mine[:, :width] * inverse * (qkv_scales.astype(f32) * 2.0 ** (-22))[None, :]).astype(bf16)
+    arrived = [exchange(rest[(j - 1) * own_rows : j * own_rows], "row", j) for j in range(1, n_row)]
+    joined_qkv = finish(mine, arrived, qkv_scales.reshape(1, -1), features * n_row)
     return (take_rows(stream, stream_other, res_rows, own_rows), joined_qkv)
 
 

time: 42.9 us -> 42.5 us (level)
  other arithmetic: 0.84 us -> 0.01 us
  Pallas kernels: 9.45 us -> 10 us
    pallas_call x0 -> x1, Pallas kernels: none -> 0.7 us  [finish(): pl.pallas_call(kernel, out_shape=jax.ShapeDtypeStruct((rows, width), bf16...]
    convert_element_type x1 -> x0, other arithmetic: 0.7 us -> none  [body(): (mine[:, :width] * inverse * (qkv_scales.astype(f32) * 2.0 ** (-22))[None...]
where the time goes in v4:
time: 42.5 us; the launch traced here: 42.4 us
  starting transfers between devices  17.1 us (40%)
  waiting for transfers between devices  14.4 us (34%)
  Pallas kernels  10 us (24%)
  between operations  0.81 us (2%)
    ppermute x9, starting transfers between devices, exchange(): return lax.ppermute(block, axis, [(i, i ^ distance) for i in range(count)])  17.1 us
    ppermute x9, waiting for transfers between devices, exchange(): return lax.ppermute(block, axis, [(i, i ^ distance) for i in range(count)])  14.4 us
    pallas_call x2, Pallas kernels, down_half(): pl.pallas_call(kernel, out_shape=jax.ShapeDtypeStruct((count, half), out_...  4.57 us
    pallas_call x2, Pallas kernels, qkv_half(): pl.pallas_call(kernel, out_shape=tuple((jax.ShapeDtypeStruct((size, width...  2.67 us
    pallas_call x1, Pallas kernels, signed_units(): pl.pallas_call(signed_kernel, out_shape=jax.ShapeDtypeStruct(gate.shape,...  0.97 us
  transfers between devices with their start and end apart: 9, of which 9 were waited for; matrix products, arithmetic and copies ran while one was open for 0% of the time, Pallas kernels for 10%

profile of v4, /device:TPU:0, one launch (start us, length us, event | category | flops | bytes accessed | tf_op | source)
XLA Modules:
  0.0 42.4 jit_solution(7776058806988390348)
XLA Ops:
  0.6 1.0 %signed_units.1.own_ref = bf16[8,4096]{1,0:T(8,128)(2,1)S(1)} custom-call(bf16[8,4096]{1,0:T(8,128)(2,1)} %gate_hbm.1, bf16[8,4096]{1,0:T(8,128)(2,1)} %up_hbm.1, s32[1,4096]{1,0:T(1,128)} %bitcast.6), custom_call_target="tpu_custom_call" | custom-call | tf_op jit(solution)/shard_map/signed_units/pallas_call | solution.py:65
  1.6 3.0 %collective-permute-start = (bf16[8,4096]{1,0:T(8,128)(2,1)S(1)}, bf16[8,4096]{1,0:T(8,128)(2,1)S(1)}, u32[]{:S(2)}, u32[]{:S(2)}) collective-permute-start(bf16[8,4096]{1,0:T(8,128)(2,1)S(1)} %signed_units.1.own_ref), channel_id=1, source_target_pairs={{0,2},{2,0},{4,6},{6,4},{8,10},{10,8},{12,14},{14,12},{1,3},{3,1},... | collective-permute-start | bytes 196616 | tf_op jit(solution)/shard_map/ppermute | solution.py:19
  4.6 2.2 %collective-permute-done.other_ref = bf16[8,4096]{1,0:T(8,128)(2,1)S(1)} collective-permute-done((bf16[8,4096]{1,0:T(8,128)(2,1)S(1)}, bf16[8,4096]{1,0:T(8,128)(2,1)S(1)}, u32[]{:S(2)}, u32[]{:S(2)}) %collective-permute-start) | collective-permute-done | bytes 65568 | tf_op jit(solution)/shard_map/ppermute | solution.py:19
  6.9 0.2 mix.1
  7.1 2.2 %collective-permute-start.1 = (bf16[8,4096]{1,0:T(8,128)(2,1)S(1)}, bf16[8,4096]{1,0:T(8,128)(2,1)S(1)}, u32[]{:S(2)}, u32[]{:S(2)}) collective-permute-start(bf16[8,4096]{1,0:T(8,128)(2,1)S(1)} %get-tuple-element.13), channel_id=1, source_target_pairs={{0,4},{2,6},{4,0},{6,2},{8,12},{10,14},{12,8},{14,10},{1,5},{3,7},... | collective-permute-start | bytes 196616 | tf_op jit(solution)/shard_map/ppermute | solution.py:19
  9.2 2.2 %collective-permute-done.1.other_ref = bf16[8,4096]{1,0:T(8,128)(2,1)S(1)} collective-permute-done((bf16[8,4096]{1,0:T(8,128)(2,1)S(1)}, bf16[8,4096]{1,0:T(8,128)(2,1)S(1)}, u32[]{:S(2)}, u32[]{:S(2)}) %collective-permute-start.1) | collective-permute-done | bytes 65568 | tf_op jit(solution)/shard_map/ppermute | solution.py:19
  11.5 3.1 %collective-permute-start.2 = (bf16[8,4096]{1,0:T(8,128)(2,1)S(1)}, bf16[8,4096]{1,0:T(8,128)(2,1)S(1)}, u32[]{:S(2)}, u32[]{:S(2)}) collective-permute-start(bf16[8,4096]{1,0:T(8,128)(2,1)S(1)} %get-tuple-element.15), channel_id=1, source_target_pairs={{0,8},{2,10},{4,12},{6,14},{8,0},{10,2},{12,4},{14,6},{1,9},{3,11}... | collective-permute-start | bytes 196616 | tf_op jit(solution)/shard_map/ppermute | solution.py:19
  14.6 2.2 %collective-permute-done.2.other_ref = bf16[8,4096]{1,0:T(8,128)(2,1)S(1)} collective-permute-done((bf16[8,4096]{1,0:T(8,128)(2,1)S(1)}, bf16[8,4096]{1,0:T(8,128)(2,1)S(1)}, u32[]{:S(2)}, u32[]{:S(2)}) %collective-permute-start.2) | collective-permute-done | bytes 65568 | tf_op jit(solution)/shard_map/ppermute | solution.py:19
  16.9 0.1 collective-permute-start.3
  17.0 1.2 %collective-permute-done.3.refs_1_ = bf16[8,4096]{1,0:T(8,128)(2,1)S(1)} collective-permute-done((bf16[8,4096]{1,0:T(8,128)(2,1)S(1)}, bf16[8,4096]{1,0:T(8,128)(2,1)S(1)}, u32[]{:S(2)}, u32[]{:S(2)}) %collective-permute-start.3) | collective-permute-done | bytes 65568 | tf_op jit(solution)/shard_map/ppermute | solution.py:19
  18.3 0.0 copy-done
  18.3 0.0 copy-done.1
  18.3 0.0 copy-done.2
  18.3 2.3 %down_other.1 = bf16[16,2048]{1,0:T(8,128)(2,1)S(1)} custom-call(bf16[16,4096]{1,0:T(8,128)(2,1)S(1)} %gather_rows.1.x_ref, bf16[4096,4096]{1,0:T(8,128)(2,1)S(1)} %copy-done, s32[1,4096]{1,0:T(1,128)S(1)} %bitcast.4, bf16[2,4096]{1,0:T(2,128)(2,1)S(1)} %copy-done.2), custom_call_target="tpu_custom_call" | custom-call | flops 268435456 | bytes 16777216 | tf_op jit(solution)/shard_map/down_other/pallas_call | solution.py:215
  20.6 1.8 %collective-permute-start.4 = (bf16[16,2048]{1,0:T(8,128)(2,1)S(1)}, bf16[16,2048]{1,0:T(8,128)(2,1)S(1)}, u32[]{:S(2)}, u32[]{:S(2)}) collective-permute-start(bf16[16,2048]{1,0:T(8,128)(2,1)S(1)} %down_other.1), channel_id=1, source_target_pairs={{0,2},{2,0},{4,6},{6,4},{8,10},{10,8},{12,14},{14,12},{1,3},{3,1},... | collective-permute-start | bytes 196616 | tf_op jit(solution)/shard_map/ppermute | solution.py:19
  22.4 2.3 %down_own.1.total_ref = f32[16,2048]{1,0:T(8,128)S(1)} custom-call(bf16[16,4096]{1,0:T(8,128)(2,1)S(1)} %gather_rows.1.x_ref, bf16[4096,4096]{1,0:T(8,128)(2,1)S(1)} %copy-done, s32[1,4096]{1,0:T(1,128)S(1)} %bitcast.5, bf16[2,4096]{1,0:T(2,128)(2,1)S(1)} %copy-done.2), custom_call_target="tpu_custom_call" | custom-call | flops 268435456 | bytes 16777216 | tf_op jit(solution)/shard_map/down_own/pallas_call | solution.py:215
  24.7 0.2 collective-permute-done.4.arrived_ref
  24.9 2.0 %collective-permute-start.5 = (bf16[16,2048]{1,0:T(8,128)(2,1)S(1)}, bf16[16,2048]{1,0:T(8,128)(2,1)S(1)}, u32[]{:S(2)}, u32[]{:S(2)}) collective-permute-start(bf16[16,2048]{1,0:T(8,128)(2,1)S(1)} %get-tuple-element.17), channel_id=1, source_target_pairs={{0,4},{2,6},{4,0},{6,2},{8,12},{10,14},{12,8},{14,10},{1,5},{3,7},... | collective-permute-start | bytes 196616 | tf_op jit(solution)/shard_map/ppermute | solution.py:19
  26.9 2.4 %collective-permute-done.5.arrived_ref = bf16[16,2048]{1,0:T(8,128)(2,1)S(1)} collective-permute-done((bf16[16,2048]{1,0:T(8,128)(2,1)S(1)}, bf16[16,2048]{1,0:T(8,128)(2,1)S(1)}, u32[]{:S(2)}, u32[]{:S(2)}) %collective-permute-start.5) | collective-permute-done | bytes 65568 | tf_op jit(solution)/shard_map/ppermute | solution.py:19
  29.3 0.0 copy-start.3
  29.3 3.1 %collective-permute-start.6 = (bf16[16,2048]{1,0:T(8,128)(2,1)S(1)}, bf16[16,2048]{1,0:T(8,128)(2,1)S(1)}, u32[]{:S(2)}, u32[]{:S(2)}) collective-permute-start(bf16[16,2048]{1,0:T(8,128)(2,1)S(1)} %get-tuple-element.19), channel_id=1, source_target_pairs={{0,8},{2,10},{4,12},{6,14},{8,0},{10,2},{12,4},{14,6},{1,9},{3,11}... | collective-permute-start | bytes 196616 | tf_op jit(solution)/shard_map/ppermute | solution.py:19
  32.4 2.2 %collective-permute-done.6.arrived_ref = bf16[16,2048]{1,0:T(8,128)(2,1)S(1)} collective-permute-done((bf16[16,2048]{1,0:T(8,128)(2,1)S(1)}, bf16[16,2048]{1,0:T(8,128)(2,1)S(1)}, u32[]{:S(2)}, u32[]{:S(2)}) %collective-permute-start.6) | collective-permute-done | bytes 65568 | tf_op jit(solution)/shard_map/ppermute | solution.py:19
  34.7 1.7 %collective-permute-start.7 = (bf16[16,2048]{1,0:T(8,128)(2,1)S(1)}, bf16[16,2048]{1,0:T(8,128)(2,1)S(1)}, u32[]{:S(2)}, u32[]{:S(2)}) collective-permute-start(bf16[16,2048]{1,0:T(8,128)(2,1)S(1)} %add.5.own_ref.x_ref), channel_id=1, source_target_pairs={{0,2},{2,0},{4,6},{6,4},{8,10},{10,8},{12,14},{14,12},{1,3},{3,1},... | collective-permute-start | bytes 196616 | tf_op jit(solution)/shard_map/ppermute | solution.py:19
  36.4 0.0 copy-done.4
  36.4 0.0 slice-done
  36.5 1.3 %qkv_own.1.refs_0_ = f32[16,2432]{1,0:T(8,128)S(1)} custom-call(bf16[16,2048]{1,0:T(8,128)(2,1)S(1)} %add.5.own_ref.x_ref, bf16[1,4096]{1,0:T(2,128)(2,1)S(1)} %reshape.18.g_ref, bf16[4096,2304]{1,0:T(8,128)(2,1)S(1)} %bitcast.3), custom_call_target="tpu_custom_call" | custom-call | flops 150994944 | bytes 9437184 | tf_op jit(solution)/shard_map/qkv_own/pallas_call | solution.py:257
  37.8 1.2 %collective-permute-done.7.other_ref.x_ref = bf16[16,2048]{1,0:T(8,128)(2,1)S(1)} collective-permute-done((bf16[16,2048]{1,0:T(8,128)(2,1)S(1)}, bf16[16,2048]{1,0:T(8,128)(2,1)S(1)}, u32[]{:S(2)}, u32[]{:S(2)}) %collective-permute-start.7) | collective-permute-done | bytes 65568 | tf_op jit(solution)/shard_map/ppermute | solution.py:19
  39.0 1.3 %qkv_other.1 = (f32[8,2432]{1,0:T(8,128)S(1)}, f32[8,2432]{1,0:T(8,128)S(1)}) custom-call(bf16[16,2048]{1,0:T(8,128)(2,1)S(1)} %collective-permute-done.7.other_ref.x_ref, bf16[1,4096]{1,0:T(2,128)(2,1)S(1)} %reshape.18.g_ref, bf16[4096,2304]{1,0:T(8,128)(2,1)S(1)} %bitcast.3, f32[16,2432]{1,0:T(8,128)S(1)} %qkv_own.1.refs_0_), custom_call_target="tpu_custom_call" | custom-call | flops 150994944 | bytes 9437184 | tf_op jit(solution)/shard_map/qkv_other/pallas_call | solution.py:257
  40.3 0.1 collective-permute-start.8
  40.4 0.7 %take_rows.1 = bf16[2,4096]{1,0:T(2,128)(2,1)} custom-call(bf16[16,2048]{1,0:T(8,128)(2,1)S(1)} %add.5.own_ref.x_ref, bf16[16,2048]{1,0:T(8,128)(2,1)S(1)} %collective-permute-done.7.other_ref.x_ref), custom_call_target="tpu_custom_call" | custom-call | tf_op jit(solution)/shard_map/take_rows/pallas_call | solution.py:284
  41.2 0.5 %collective-permute-done.8.refs_1_ = f32[8,2432]{1,0:T(8,128)S(1)} collective-permute-done((f32[8,2432]{1,0:T(8,128)S(1)}, f32[8,2432]{1,0:T(8,128)S(1)}, u32[]{:S(2)}, u32[]{:S(2)}) %collective-permute-start.8) | collective-permute-done | bytes 77856 | tf_op jit(solution)/shard_map/ppermute | solution.py:19
  41.7 0.7 %finish.1 = bf16[8,2304]{1,0:T(8,128)(2,1)} custom-call(f32[8,2432]{1,0:T(8,128)S(1)} %get-tuple-element.20.refs_0_, f32[8,2432]{1,0:T(8,128)S(1)} %collective-permute-done.8.refs_1_, s32[1,2304]{1,0:T(1,128)S(1)} %reshape.19.refs_2_), custom_call_target="tpu_custom_call" | custom-call | tf_op jit(solution)/shard_map/finish/pallas_call | solution.py:307
  (23 shorter events, 0.2 us)
Async XLA Ops:
  1.6 5.2 %collective-permute-start = (bf16[8,4096]{1,0:T(8,128)(2,1)S(1)}, bf16[8,4096]{1,0:T(8,128)(2,1)S(1)}, u32[]{:S(2)}, u32[]{:S(2)}) collective-permute-start(bf16[8,4096]{1,0:T(8,128)(2,1)S(1)} %signed_units.1.own_ref), channel_id=1, source_target_pairs={{0,2},{2,0},{4,6},{6,4},{8,10},{10,8},{12,14},{14,12},{1,3},{3,1},... | collective-permute-start | bytes 196616 | tf_op jit(solution)/shard_map/ppermute | solution.py:19
  6.9 11.4 %copy-start = (bf16[4096,4096]{1,0:T(8,128)(2,1)S(1)}, bf16[4096,4096]{1,0:T(8,128)(2,1)}, u32[]{:S(2)}) copy-start(bf16[4096,4096]{1,0:T(8,128)(2,1)} %w_ref.5) | copy-start | bytes 100663296
  6.9 11.4 %copy-start.1 = (s32[4096]{0:T(1024)S(1)}, s32[4096]{0:T(1024)}, u32[]{:S(2)}) copy-start(s32[4096]{0:T(1024)} %param.13) | copy-start | bytes 49156
  6.9 11.4 %copy-start.2 = (bf16[2,4096]{1,0:T(2,128)(2,1)S(1)}, bf16[2,4096]{1,0:T(2,128)(2,1)}, u32[]{:S(2)}) copy-start(bf16[2,4096]{1,0:T(2,128)(2,1)} %r_ref.3) | copy-start | bytes 49156
  7.1 4.4 %collective-permute-start.1 = (bf16[8,4096]{1,0:T(8,128)(2,1)S(1)}, bf16[8,4096]{1,0:T(8,128)(2,1)S(1)}, u32[]{:S(2)}, u32[]{:S(2)}) collective-permute-start(bf16[8,4096]{1,0:T(8,128)(2,1)S(1)} %get-tuple-element.13), channel_id=1, source_target_pairs={{0,4},{2,6},{4,0},{6,2},{8,12},{10,14},{12,8},{14,10},{1,5},{3,7},... | collective-permute-start | bytes 196616 | tf_op jit(solution)/shard_map/ppermute | solution.py:19
  11.5 5.3 %collective-permute-start.2 = (bf16[8,4096]{1,0:T(8,128)(2,1)S(1)}, bf16[8,4096]{1,0:T(8,128)(2,1)S(1)}, u32[]{:S(2)}, u32[]{:S(2)}) collective-permute-start(bf16[8,4096]{1,0:T(8,128)(2,1)S(1)} %get-tuple-element.15), channel_id=1, source_target_pairs={{0,8},{2,10},{4,12},{6,14},{8,0},{10,2},{12,4},{14,6},{1,9},{3,11}... | collective-permute-start | bytes 196616 | tf_op jit(solution)/shard_map/ppermute | solution.py:19
  16.9 1.3 %collective-permute-start.3 = (bf16[8,4096]{1,0:T(8,128)(2,1)S(1)}, bf16[8,4096]{1,0:T(8,128)(2,1)S(1)}, u32[]{:S(2)}, u32[]{:S(2)}) collective-permute-start(bf16[8,4096]{1,0:T(8,128)(2,1)S(1)} %combine.3.refs_0_), channel_id=1, source_target_pairs={{0,1},{1,0},{2,3},{3,2},{4,5},{5,4},{6,7},{7,6},{8,9},{9,8},{10,11... | collective-permute-start | bytes 196616 | tf_op jit(solution)/shard_map/ppermute | solution.py:19
  20.6 4.3 %collective-permute-start.4 = (bf16[16,2048]{1,0:T(8,128)(2,1)S(1)}, bf16[16,2048]{1,0:T(8,128)(2,1)S(1)}, u32[]{:S(2)}, u32[]{:S(2)}) collective-permute-start(bf16[16,2048]{1,0:T(8,128)(2,1)S(1)} %down_other.1), channel_id=1, source_target_pairs={{0,2},{2,0},{4,6},{6,4},{8,10},{10,8},{12,14},{14,12},{1,3},{3,1},... | collective-permute-start | bytes 196616 | tf_op jit(solution)/shard_map/ppermute | solution.py:19
  24.9 11.6 %slice-start = ((s8[18874368]{0:T(1024)(128)(4,1)}), s8[4194304]{0:T(1024)(128)(4,1)S(1)}, s32[]{:S(2)}) async-start(s8[18874368]{0:T(1024)(128)(4,1)} %bitcast.2), calls=%async_computation | async-start | bytes 8388608
  24.9 11.6 %slice-start.1 = ((s8[18874368]{0:T(1024)(128)(4,1)}), s8[4194304]{0:T(1024)(128)(4,1)S(1)}, s32[]{:S(2)}) async-start(s8[18874368]{0:T(1024)(128)(4,1)} %bitcast.2), calls=%async_computation.1 | async-start | bytes 8388608
  24.9 11.6 %slice-start.2 = ((s8[18874368]{0:T(1024)(128)(4,1)}), s8[4194304]{0:T(1024)(128)(4,1)S(1)}, s32[]{:S(2)}) async-start(s8[18874368]{0:T(1024)(128)(4,1)} %bitcast.2), calls=%async_computation.2 | async-start | bytes 8388608
  24.9 4.3 %collective-permute-start.5 = (bf16[16,2048]{1,0:T(8,128)(2,1)S(1)}, bf16[16,2048]{1,0:T(8,128)(2,1)S(1)}, u32[]{:S(2)}, u32[]{:S(2)}) collective-permute-start(bf16[16,2048]{1,0:T(8,128)(2,1)S(1)} %get-tuple-element.17), channel_id=1, source_target_pairs={{0,4},{2,6},{4,0},{6,2},{8,12},{10,14},{12,8},{14,10},{1,5},{3,7},... | collective-permute-start | bytes 196616 | tf_op jit(solution)/shard_map/ppermute | solution.py:19
  29.2 7.2 %copy-start.4 = (bf16[4096]{0:T(1024)(128)(2,1)S(1)}, bf16[4096]{0:T(1024)(128)(2,1)}, u32[]{:S(2)}) copy-start(bf16[4096]{0:T(1024)(128)(2,1)} %param.15) | copy-start | bytes 24580
  29.2 7.2 %slice-start.3 = ((s8[18874368]{0:T(1024)(128)(4,1)}), s8[4194304]{0:T(1024)(128)(4,1)S(1)}, s32[]{:S(2)}) async-start(s8[18874368]{0:T(1024)(128)(4,1)} %bitcast.2), calls=%async_computation.3 | async-start | bytes 8388608
  29.2 7.2 %slice-start.4 = ((s8[18874368]{0:T(1024)(128)(4,1)}), s8[2097152]{0:T(1024)(128)(4,1)S(1)}, s32[]{:S(2)}) async-start(s8[18874368]{0:T(1024)(128)(4,1)} %bitcast.2), calls=%async_computation.4 | async-start | bytes 4194304
  29.3 11.1 %copy-start.3 = (s32[2304]{0:T(1024)S(1)}, s32[2304]{0:T(1024)}, u32[]{:S(2)}) copy-start(s32[2304]{0:T(1024)} %param.17) | copy-start | bytes 27652
  29.3 5.4 %collective-permute-start.6 = (bf16[16,2048]{1,0:T(8,128)(2,1)S(1)}, bf16[16,2048]{1,0:T(8,128)(2,1)S(1)}, u32[]{:S(2)}, u32[]{:S(2)}) collective-permute-start(bf16[16,2048]{1,0:T(8,128)(2,1)S(1)} %get-tuple-element.19), channel_id=1, source_target_pairs={{0,8},{2,10},{4,12},{6,14},{8,0},{10,2},{12,4},{14,6},{1,9},{3,11}... | collective-permute-start | bytes 196616 | tf_op jit(solution)/shard_map/ppermute | solution.py:19
  34.7 4.3 %collective-permute-start.7 = (bf16[16,2048]{1,0:T(8,128)(2,1)S(1)}, bf16[16,2048]{1,0:T(8,128)(2,1)S(1)}, u32[]{:S(2)}, u32[]{:S(2)}) collective-permute-start(bf16[16,2048]{1,0:T(8,128)(2,1)S(1)} %add.5.own_ref.x_ref), channel_id=1, source_target_pairs={{0,2},{2,0},{4,6},{6,4},{8,10},{10,8},{12,14},{14,12},{1,3},{3,1},... | collective-permute-start | bytes 196616 | tf_op jit(solution)/shard_map/ppermute | solution.py:19
  40.3 1.3 %collective-permute-start.8 = (f32[8,2432]{1,0:T(8,128)S(1)}, f32[8,2432]{1,0:T(8,128)S(1)}, u32[]{:S(2)}, u32[]{:S(2)}) collective-permute-start(f32[8,2432]{1,0:T(8,128)S(1)} %get-tuple-element.21), channel_id=1, source_target_pairs={{0,1},{1,0},{2,3},{3,2},{4,5},{5,4},{6,7},{7,6},{8,9},{9,8},{10,11... | collective-permute-start | bytes 233480 | tf_op jit(solution)/shard_map/ppermute | solution.py:19

commit v5 on v4

--- a/solution.py
+++ b/solution.py
@@ -125,10 +125,16 @@
     )(own, other)
 
 
-def combine(wide, other, distance, factor):
-    def kernel(wide_ref, other_ref, *out_refs):
-        own, theirs = wide_ref[...], other_ref[...].astype(f32)
-        mixed = theirs + jnp.where(bit_of("hid", distance) == 1, -own, own)
+def combine(wide, others, masks, bits, factor):
+    def kernel(*refs):
+        out_refs = refs[1 + len(others) :]
+        mixed = None
+        for ref, mask in zip(refs, [0] + masks):
+            value = ref[...].astype(f32)
+            flips = [bit_of("hid", 1 << bit) for bit in bits if not mask >> bit & 1]
+            if flips:
+                value = jnp.where(sum(flips) % 2 == 1, -value, value)
+            mixed = value if mixed is None else mixed + value
         if factor is None:
             out_refs[0][...] = mixed
             out_refs[1][...] = mixed.astype(bf16)
@@ -139,16 +145,19 @@
     return pl.pallas_call(
         kernel,
         out_shape=tuple(jax.ShapeDtypeStruct(wide.shape, t) for t in types),
-        in_specs=[VMEM] * 2,
+        in_specs=[VMEM] * (1 + len(others)),
         out_specs=(VMEM,) * len(types),
         compiler_params=params(2),
         name="combine",
-    )(wide, other)
-
-
-def add(total, arrived, last, first):
-    def kernel(total_ref, arrived_ref, *out_refs):
-        value = total_ref[...] + arrived_ref[...].astype(f32)
+    )(wide, *others)
+
+
+def add(total, arrived, last, estimate):
+    def kernel(*refs):
+        out_refs = refs[1 + len(arrived) :]
+        value = refs[0][...]
+        for ref in refs[1 : 1 + len(arrived)]:
+            value = value + ref[...].astype(f32)
         if not last:
             out_refs[0][...] = value
         out_refs[-1][...] = value.astype(bf16)
@@ -157,12 +166,12 @@
     return pl.pallas_call(
         kernel,
         out_shape=tuple(jax.ShapeDtypeStruct(total.shape, t) for t in types),
-        in_specs=[VMEM] * 2,
+        in_specs=[VMEM] * (1 + len(arrived)),
         out_specs=(VMEM,) * len(types),
         compiler_params=params(2, total.shape[0]),
-        cost_estimate=cost(40_000_000_000, 0) if not last else None,
+        cost_estimate=estimate,
         name="add",
-    )(total, arrived)
+    )(total, *arrived)
 
 
 def places(res_rows, own_rows):
@@ -328,18 +337,19 @@
     hid, n_row = lax.axis_size("hid"), lax.axis_size("row")
     own_rows, depth = gate_proj.shape
     res_rows, features = residual.shape
-    distances = [1 << b for b in range(hid.bit_length() - 1)]
+    count = hid.bit_length() - 1
+    steps = [[0]] + [list(range(b, min(b + 2, count))) for b in range(1, count, 2)]
+    partners = [[m for m in range(hid - 1, 0, -1) if not m & ~sum(1 << b for b in bits)] for bits in steps]
 
     send = signed_units(gate_proj, up_proj, hadamard_signs)
-    for k, distance in enumerate(distances):
-        other = exchange(send, "hid", distance)
-        last = k == len(distances) - 1
+    for k, (bits, masks) in enumerate(zip(steps, partners)):
+        others = [exchange(send, "hid", mask) for mask in masks]
         if k == 0:
-            wide, send = mix(send, other)
-        elif not last:
-            wide, send = combine(wide, other, distance, None)
+            wide, send = mix(send, *others)
+        elif k < len(steps) - 1:
+            wide, send = combine(wide, others, masks, bits, None)
         else:
-            (rotated,) = combine(wide, other, distance, 1.0 / math.sqrt(depth * hid))
+            (rotated,) = combine(wide, others, masks, bits, 1.0 / math.sqrt(depth * hid))
     rows = [rotated] + [exchange(rotated, "row", j) for j in range(1, n_row)]
     rows = gather_rows(rows)
 
@@ -347,10 +357,11 @@
     theirs = down_half(rows, down_codes, scale, residual, own_rows, True, bf16)
     arrived = exchange(theirs, "hid", 1)
     total = down_half(rows, down_codes, scale, residual, own_rows, False, f32)
-    for distance in distances[1:]:
-        total, send = add(total, arrived, False, distance == 2)
-        arrived = exchange(send, "hid", distance)
-    (stream,) = add(total, arrived, True, False)
+    arrived = [arrived]
+    for k, masks in enumerate(partners[1:]):
+        total, send = add(total, arrived, False, cost(100_000_000_000, 0) if k == 0 else None)
+        arrived = [exchange(send, "hid", mask) for mask in masks]
+    (stream,) = add(total, arrived, True, None)
     stream_other = exchange(stream, "hid", 1)
 
     gain = norm_gain.reshape(1, -1)

time: 42.5 us -> 41.3 us (0.972)
  starting transfers between devices: 17.1 us -> 15.5 us
    ppermute x9 -> x11, starting transfers between devices: 17.1 us -> 15.5 us  [exchange(): return lax.ppermute(block, axis, [(i, i ^ distance) for i in range(count)])]
    ppermute x9 -> x11, waiting for transfers between devices: 14.4 us -> 14.8 us  [exchange(): return lax.ppermute(block, axis, [(i, i ^ distance) for i in range(count)])]
  transfers between devices with their start and end apart: 9 -> 11, of which waited for: 9 -> 9; matrix products, arithmetic and copies ran while one was open for 0% -> 0% of each run, Pallas kernels for 10% -> 11%
where the time goes in v5:
time: 41.3 us; the launch traced here: 41.1 us
  starting transfers between devices  15.5 us (38%)
  waiting for transfers between devices  14.8 us (36%)
  Pallas kernels  10 us (24%)
  between operations  0.82 us (2%)
    ppermute x11, starting transfers between devices, exchange(): return lax.ppermute(block, axis, [(i, i ^ distance) for i in range(count)])  15.5 us
    ppermute x11, waiting for transfers between devices, exchange(): return lax.ppermute(block, axis, [(i, i ^ distance) for i in range(count)])  14.8 us
    pallas_call x2, Pallas kernels, down_half(): pl.pallas_call(kernel, out_shape=jax.ShapeDtypeStruct((count, half), out_...  4.57 us
    pallas_call x2, Pallas kernels, qkv_half(): pl.pallas_call(kernel, out_shape=tuple((jax.ShapeDtypeStruct((size, width...  2.67 us
    pallas_call x1, Pallas kernels, signed_units(): pl.pallas_call(signed_kernel, out_shape=jax.ShapeDtypeStruct(gate.shape,...  0.97 us
  transfers between devices with their start and end apart: 11, of which 9 were waited for; matrix products, arithmetic and copies ran while one was open for 0% of the time, Pallas kernels for 11%

profile of v5, /device:TPU:0, one launch (start us, length us, event | category | flops | bytes accessed | tf_op | source)
XLA Modules:
  0.0 41.1 jit_solution(11971322139323139368)
XLA Ops:
  0.6 1.0 %signed_units.1.own_ref = bf16[8,4096]{1,0:T(8,128)(2,1)S(1)} custom-call(bf16[8,4096]{1,0:T(8,128)(2,1)} %gate_hbm.1, bf16[8,4096]{1,0:T(8,128)(2,1)} %up_hbm.1, s32[1,4096]{1,0:T(1,128)} %bitcast.6), custom_call_target="tpu_custom_call" | custom-call | tf_op jit(solution)/shard_map/signed_units/pallas_call | solution.py:65
  1.6 3.0 %collective-permute-start = (bf16[8,4096]{1,0:T(8,128)(2,1)S(1)}, bf16[8,4096]{1,0:T(8,128)(2,1)S(1)}, u32[]{:S(2)}, u32[]{:S(2)}) collective-permute-start(bf16[8,4096]{1,0:T(8,128)(2,1)S(1)} %signed_units.1.own_ref), channel_id=1, source_target_pairs={{0,2},{2,0},{4,6},{6,4},{8,10},{10,8},{12,14},{14,12},{1,3},{3,1},... | collective-permute-start | bytes 196616 | tf_op jit(solution)/shard_map/ppermute | solution.py:19
  4.6 2.2 %collective-permute-done.other_ref = bf16[8,4096]{1,0:T(8,128)(2,1)S(1)} collective-permute-done((bf16[8,4096]{1,0:T(8,128)(2,1)S(1)}, bf16[8,4096]{1,0:T(8,128)(2,1)S(1)}, u32[]{:S(2)}, u32[]{:S(2)}) %collective-permute-start) | collective-permute-done | bytes 65568 | tf_op jit(solution)/shard_map/ppermute | solution.py:19
  6.9 0.2 mix.1
  7.1 4.2 %collective-permute-start.1 = (bf16[8,4096]{1,0:T(8,128)(2,1)S(1)}, bf16[8,4096]{1,0:T(8,128)(2,1)S(1)}, u32[]{:S(2)}, u32[]{:S(2)}) collective-permute-start(bf16[8,4096]{1,0:T(8,128)(2,1)S(1)} %get-tuple-element.9), channel_id=1, source_target_pairs={{0,12},{2,14},{4,8},{6,10},{8,4},{10,6},{12,0},{14,2},{1,13},{3,15... | collective-permute-start | bytes 196616 | tf_op jit(solution)/shard_map/ppermute | solution.py:19
  11.3 0.6 %collective-permute-start.3 = (bf16[8,4096]{1,0:T(8,128)(2,1)S(1)}, bf16[8,4096]{1,0:T(8,128)(2,1)S(1)}, u32[]{:S(2)}, u32[]{:S(2)}) collective-permute-start(bf16[8,4096]{1,0:T(8,128)(2,1)S(1)} %get-tuple-element.9), channel_id=1, source_target_pairs={{0,4},{2,6},{4,0},{6,2},{8,12},{10,14},{12,8},{14,10},{1,5},{3,7},... | collective-permute-start | bytes 196616 | tf_op jit(solution)/shard_map/ppermute | solution.py:19
  11.9 1.8 %collective-permute-done.1.refs_1_ = bf16[8,4096]{1,0:T(8,128)(2,1)S(1)} collective-permute-done((bf16[8,4096]{1,0:T(8,128)(2,1)S(1)}, bf16[8,4096]{1,0:T(8,128)(2,1)S(1)}, u32[]{:S(2)}, u32[]{:S(2)}) %collective-permute-start.1) | collective-permute-done | bytes 65568 | tf_op jit(solution)/shard_map/ppermute | solution.py:19
  13.7 2.8 %collective-permute-done.2.refs_2_ = bf16[8,4096]{1,0:T(8,128)(2,1)S(1)} collective-permute-done((bf16[8,4096]{1,0:T(8,128)(2,1)S(1)}, bf16[8,4096]{1,0:T(8,128)(2,1)S(1)}, u32[]{:S(2)}, u32[]{:S(2)}) %collective-permute-start.2) | collective-permute-done | bytes 65568 | tf_op jit(solution)/shard_map/ppermute | solution.py:19
  16.5 0.0 collective-permute-done.3.refs_3_
  16.5 0.1 combine.1.refs_0_
  16.6 0.1 collective-permute-start.4
  16.6 1.2 %collective-permute-done.4.refs_1_ = bf16[8,4096]{1,0:T(8,128)(2,1)S(1)} collective-permute-done((bf16[8,4096]{1,0:T(8,128)(2,1)S(1)}, bf16[8,4096]{1,0:T(8,128)(2,1)S(1)}, u32[]{:S(2)}, u32[]{:S(2)}) %collective-permute-start.4) | collective-permute-done | bytes 65568 | tf_op jit(solution)/shard_map/ppermute | solution.py:19
  17.9 0.0 copy-done
  17.9 2.3 %down_other.1 = bf16[16,2048]{1,0:T(8,128)(2,1)S(1)} custom-call(bf16[16,4096]{1,0:T(8,128)(2,1)S(1)} %gather_rows.1.x_ref, bf16[4096,4096]{1,0:T(8,128)(2,1)S(1)} %copy-done, s32[1,4096]{1,0:T(1,128)S(1)} %bitcast.4, bf16[2,4096]{1,0:T(2,128)(2,1)S(1)} %copy-done.2), custom_call_target="tpu_custom_call" | custom-call | flops 268435456 | bytes 16777216 | tf_op jit(solution)/shard_map/down_other/pallas_call | solution.py:224
  20.2 1.5 %collective-permute-start.5 = (bf16[16,2048]{1,0:T(8,128)(2,1)S(1)}, bf16[16,2048]{1,0:T(8,128)(2,1)S(1)}, u32[]{:S(2)}, u32[]{:S(2)}) collective-permute-start(bf16[16,2048]{1,0:T(8,128)(2,1)S(1)} %down_other.1), channel_id=1, source_target_pairs={{0,2},{2,0},{4,6},{6,4},{8,10},{10,8},{12,14},{14,12},{1,3},{3,1},... | collective-permute-start | bytes 196616 | tf_op jit(solution)/shard_map/ppermute | solution.py:19
  21.7 2.3 %down_own.1.refs_0_ = f32[16,2048]{1,0:T(8,128)S(1)} custom-call(bf16[16,4096]{1,0:T(8,128)(2,1)S(1)} %gather_rows.1.x_ref, bf16[4096,4096]{1,0:T(8,128)(2,1)S(1)} %copy-done, s32[1,4096]{1,0:T(1,128)S(1)} %bitcast.5, bf16[2,4096]{1,0:T(2,128)(2,1)S(1)} %copy-done.2), custom_call_target="tpu_custom_call" | custom-call | flops 268435456 | bytes 16777216 | tf_op jit(solution)/shard_map/down_own/pallas_call | solution.py:224
  24.0 0.0 slice-start.1
  24.0 0.0 slice-start.2
  24.0 0.4 %collective-permute-done.5.refs_1_ = bf16[16,2048]{1,0:T(8,128)(2,1)S(1)} collective-permute-done((bf16[16,2048]{1,0:T(8,128)(2,1)S(1)}, bf16[16,2048]{1,0:T(8,128)(2,1)S(1)}, u32[]{:S(2)}, u32[]{:S(2)}) %collective-permute-start.5) | collective-permute-done | bytes 65568 | tf_op jit(solution)/shard_map/ppermute | solution.py:19
  24.5 0.0 copy-start.3
  24.5 3.7 %collective-permute-start.6 = (bf16[16,2048]{1,0:T(8,128)(2,1)S(1)}, bf16[16,2048]{1,0:T(8,128)(2,1)S(1)}, u32[]{:S(2)}, u32[]{:S(2)}) collective-permute-start(bf16[16,2048]{1,0:T(8,128)(2,1)S(1)} %get-tuple-element.11), channel_id=1, source_target_pairs={{0,12},{2,14},{4,8},{6,10},{8,4},{10,6},{12,0},{14,2},{1,13},{3,15... | collective-permute-start | bytes 196616 | tf_op jit(solution)/shard_map/ppermute | solution.py:19
  28.2 0.8 %collective-permute-start.8 = (bf16[16,2048]{1,0:T(8,128)(2,1)S(1)}, bf16[16,2048]{1,0:T(8,128)(2,1)S(1)}, u32[]{:S(2)}, u32[]{:S(2)}) collective-permute-start(bf16[16,2048]{1,0:T(8,128)(2,1)S(1)} %get-tuple-element.11), channel_id=1, source_target_pairs={{0,4},{2,6},{4,0},{6,2},{8,12},{10,14},{12,8},{14,10},{1,5},{3,7},... | collective-permute-start | bytes 196616 | tf_op jit(solution)/shard_map/ppermute | solution.py:19
  29.0 1.9 %collective-permute-done.6.refs_1_ = bf16[16,2048]{1,0:T(8,128)(2,1)S(1)} collective-permute-done((bf16[16,2048]{1,0:T(8,128)(2,1)S(1)}, bf16[16,2048]{1,0:T(8,128)(2,1)S(1)}, u32[]{:S(2)}, u32[]{:S(2)}) %collective-permute-start.6) | collective-permute-done | bytes 65568 | tf_op jit(solution)/shard_map/ppermute | solution.py:19
  30.9 2.5 %collective-permute-done.7.refs_2_ = bf16[16,2048]{1,0:T(8,128)(2,1)S(1)} collective-permute-done((bf16[16,2048]{1,0:T(8,128)(2,1)S(1)}, bf16[16,2048]{1,0:T(8,128)(2,1)S(1)}, u32[]{:S(2)}, u32[]{:S(2)}) %collective-permute-start.7) | collective-permute-done | bytes 65568 | tf_op jit(solution)/shard_map/ppermute | solution.py:19
  33.4 1.5 %collective-permute-start.9 = (bf16[16,2048]{1,0:T(8,128)(2,1)S(1)}, bf16[16,2048]{1,0:T(8,128)(2,1)S(1)}, u32[]{:S(2)}, u32[]{:S(2)}) collective-permute-start(bf16[16,2048]{1,0:T(8,128)(2,1)S(1)} %add.3.own_ref.x_ref), channel_id=1, source_target_pairs={{0,2},{2,0},{4,6},{6,4},{8,10},{10,8},{12,14},{14,12},{1,3},{3,1},... | collective-permute-start | bytes 196616 | tf_op jit(solution)/shard_map/ppermute | solution.py:19
  35.0 1.3 %qkv_own.1.refs_0_ = f32[16,2432]{1,0:T(8,128)S(1)} custom-call(bf16[16,2048]{1,0:T(8,128)(2,1)S(1)} %add.3.own_ref.x_ref, bf16[1,4096]{1,0:T(2,128)(2,1)S(1)} %reshape.18.g_ref, bf16[4096,2304]{1,0:T(8,128)(2,1)S(1)} %bitcast.3), custom_call_target="tpu_custom_call" | custom-call | flops 150994944 | bytes 9437184 | tf_op jit(solution)/shard_map/qkv_own/pallas_call | solution.py:266
  36.4 1.4 %collective-permute-done.9.other_ref.x_ref = bf16[16,2048]{1,0:T(8,128)(2,1)S(1)} collective-permute-done((bf16[16,2048]{1,0:T(8,128)(2,1)S(1)}, bf16[16,2048]{1,0:T(8,128)(2,1)S(1)}, u32[]{:S(2)}, u32[]{:S(2)}) %collective-permute-start.9) | collective-permute-done | bytes 65568 | tf_op jit(solution)/shard_map/ppermute | solution.py:19
  37.8 1.3 %qkv_other.1 = (f32[8,2432]{1,0:T(8,128)S(1)}, f32[8,2432]{1,0:T(8,128)S(1)}) custom-call(bf16[16,2048]{1,0:T(8,128)(2,1)S(1)} %collective-permute-done.9.other_ref.x_ref, bf16[1,4096]{1,0:T(2,128)(2,1)S(1)} %reshape.18.g_ref, bf16[4096,2304]{1,0:T(8,128)(2,1)S(1)} %bitcast.3, f32[16,2432]{1,0:T(8,128)S(1)} %qkv_own.1.refs_0_), custom_call_target="tpu_custom_call" | custom-call | flops 150994944 | bytes 9437184 | tf_op jit(solution)/shard_map/qkv_other/pallas_call | solution.py:266
  39.1 0.1 collective-permute-start.10
  39.2 0.7 %take_rows.1 = bf16[2,4096]{1,0:T(2,128)(2,1)} custom-call(bf16[16,2048]{1,0:T(8,128)(2,1)S(1)} %add.3.own_ref.x_ref, bf16[16,2048]{1,0:T(8,128)(2,1)S(1)} %collective-permute-done.9.other_ref.x_ref), custom_call_target="tpu_custom_call" | custom-call | tf_op jit(solution)/shard_map/take_rows/pallas_call | solution.py:293
  39.9 0.5 %collective-permute-done.10.refs_1_ = f32[8,2432]{1,0:T(8,128)S(1)} collective-permute-done((f32[8,2432]{1,0:T(8,128)S(1)}, f32[8,2432]{1,0:T(8,128)S(1)}, u32[]{:S(2)}, u32[]{:S(2)}) %collective-permute-start.10) | collective-permute-done | bytes 77856 | tf_op jit(solution)/shard_map/ppermute | solution.py:19
  40.4 0.7 %finish.1 = bf16[8,2304]{1,0:T(8,128)(2,1)} custom-call(f32[8,2432]{1,0:T(8,128)S(1)} %get-tuple-element.12.refs_0_, f32[8,2432]{1,0:T(8,128)S(1)} %collective-permute-done.10.refs_1_, s32[1,2304]{1,0:T(1,128)S(1)} %reshape.19.refs_2_), custom_call_target="tpu_custom_call" | custom-call | tf_op jit(solution)/shard_map/finish/pallas_call | solution.py:316
  (25 shorter events, 0.1 us)
Async XLA Ops:
  1.6 5.2 %collective-permute-start = (bf16[8,4096]{1,0:T(8,128)(2,1)S(1)}, bf16[8,4096]{1,0:T(8,128)(2,1)S(1)}, u32[]{:S(2)}, u32[]{:S(2)}) collective-permute-start(bf16[8,4096]{1,0:T(8,128)(2,1)S(1)} %signed_units.1.own_ref), channel_id=1, source_target_pairs={{0,2},{2,0},{4,6},{6,4},{8,10},{10,8},{12,14},{14,12},{1,3},{3,1},... | collective-permute-start | bytes 196616 | tf_op jit(solution)/shard_map/ppermute | solution.py:19
  6.9 11.0 %copy-start = (bf16[4096,4096]{1,0:T(8,128)(2,1)S(1)}, bf16[4096,4096]{1,0:T(8,128)(2,1)}, u32[]{:S(2)}) copy-start(bf16[4096,4096]{1,0:T(8,128)(2,1)} %w_ref.5) | copy-start | bytes 100663296
  6.9 11.0 %copy-start.1 = (s32[4096]{0:T(1024)S(1)}, s32[4096]{0:T(1024)}, u32[]{:S(2)}) copy-start(s32[4096]{0:T(1024)} %param.13) | copy-start | bytes 49156
  6.9 11.0 %copy-start.2 = (bf16[2,4096]{1,0:T(2,128)(2,1)S(1)}, bf16[2,4096]{1,0:T(2,128)(2,1)}, u32[]{:S(2)}) copy-start(bf16[2,4096]{1,0:T(2,128)(2,1)} %r_ref.3) | copy-start | bytes 49156
  7.1 6.6 %collective-permute-start.1 = (bf16[8,4096]{1,0:T(8,128)(2,1)S(1)}, bf16[8,4096]{1,0:T(8,128)(2,1)S(1)}, u32[]{:S(2)}, u32[]{:S(2)}) collective-permute-start(bf16[8,4096]{1,0:T(8,128)(2,1)S(1)} %get-tuple-element.9), channel_id=1, source_target_pairs={{0,12},{2,14},{4,8},{6,10},{8,4},{10,6},{12,0},{14,2},{1,13},{3,15... | collective-permute-start | bytes 196616 | tf_op jit(solution)/shard_map/ppermute | solution.py:19
  11.3 5.2 %collective-permute-start.2 = (bf16[8,4096]{1,0:T(8,128)(2,1)S(1)}, bf16[8,4096]{1,0:T(8,128)(2,1)S(1)}, u32[]{:S(2)}, u32[]{:S(2)}) collective-permute-start(bf16[8,4096]{1,0:T(8,128)(2,1)S(1)} %get-tuple-element.9), channel_id=1, source_target_pairs={{0,8},{2,10},{4,12},{6,14},{8,0},{10,2},{12,4},{14,6},{1,9},{3,11}... | collective-permute-start | bytes 196616 | tf_op jit(solution)/shard_map/ppermute | solution.py:19
  11.3 5.2 %collective-permute-start.3 = (bf16[8,4096]{1,0:T(8,128)(2,1)S(1)}, bf16[8,4096]{1,0:T(8,128)(2,1)S(1)}, u32[]{:S(2)}, u32[]{:S(2)}) collective-permute-start(bf16[8,4096]{1,0:T(8,128)(2,1)S(1)} %get-tuple-element.9), channel_id=1, source_target_pairs={{0,4},{2,6},{4,0},{6,2},{8,12},{10,14},{12,8},{14,10},{1,5},{3,7},... | collective-permute-start | bytes 196616 | tf_op jit(solution)/shard_map/ppermute | solution.py:19
  16.6 1.3 %collective-permute-start.4 = (bf16[8,4096]{1,0:T(8,128)(2,1)S(1)}, bf16[8,4096]{1,0:T(8,128)(2,1)S(1)}, u32[]{:S(2)}, u32[]{:S(2)}) collective-permute-start(bf16[8,4096]{1,0:T(8,128)(2,1)S(1)} %combine.1.refs_0_), channel_id=1, source_target_pairs={{0,1},{1,0},{2,3},{3,2},{4,5},{5,4},{6,7},{7,6},{8,9},{9,8},{10,11... | collective-permute-start | bytes 196616 | tf_op jit(solution)/shard_map/ppermute | solution.py:19
  20.2 4.3 %collective-permute-start.5 = (bf16[16,2048]{1,0:T(8,128)(2,1)S(1)}, bf16[16,2048]{1,0:T(8,128)(2,1)S(1)}, u32[]{:S(2)}, u32[]{:S(2)}) collective-permute-start(bf16[16,2048]{1,0:T(8,128)(2,1)S(1)} %down_other.1), channel_id=1, source_target_pairs={{0,2},{2,0},{4,6},{6,4},{8,10},{10,8},{12,14},{14,12},{1,3},{3,1},... | collective-permute-start | bytes 196616 | tf_op jit(solution)/shard_map/ppermute | solution.py:19
  21.7 13.3 %slice-start = ((s8[18874368]{0:T(1024)(128)(4,1)}), s8[2097152]{0:T(1024)(128)(4,1)S(1)}, s32[]{:S(2)}) async-start(s8[18874368]{0:T(1024)(128)(4,1)} %bitcast.2), calls=%async_computation | async-start | bytes 4194304
  24.0 11.0 %copy-start.4 = (bf16[4096]{0:T(1024)(128)(2,1)S(1)}, bf16[4096]{0:T(1024)(128)(2,1)}, u32[]{:S(2)}) copy-start(bf16[4096]{0:T(1024)(128)(2,1)} %param.15) | copy-start | bytes 24580
  24.0 11.0 %slice-start.1 = ((s8[18874368]{0:T(1024)(128)(4,1)}), s8[4194304]{0:T(1024)(128)(4,1)S(1)}, s32[]{:S(2)}) async-start(s8[18874368]{0:T(1024)(128)(4,1)} %bitcast.2), calls=%async_computation.1 | async-start | bytes 8388608
  24.0 11.0 %slice-start.2 = ((s8[18874368]{0:T(1024)(128)(4,1)}), s8[4194304]{0:T(1024)(128)(4,1)S(1)}, s32[]{:S(2)}) async-start(s8[18874368]{0:T(1024)(128)(4,1)} %bitcast.2), calls=%async_computation.2 | async-start | bytes 8388608
  24.0 11.0 %slice-start.3 = ((s8[18874368]{0:T(1024)(128)(4,1)}), s8[4194304]{0:T(1024)(128)(4,1)S(1)}, s32[]{:S(2)}) async-start(s8[18874368]{0:T(1024)(128)(4,1)} %bitcast.2), calls=%async_computation.3 | async-start | bytes 8388608
  24.0 11.0 %slice-start.4 = ((s8[18874368]{0:T(1024)(128)(4,1)}), s8[4194304]{0:T(1024)(128)(4,1)S(1)}, s32[]{:S(2)}) async-start(s8[18874368]{0:T(1024)(128)(4,1)} %bitcast.2), calls=%async_computation.4 | async-start | bytes 8388608
  24.5 14.6 %copy-start.3 = (s32[2304]{0:T(1024)S(1)}, s32[2304]{0:T(1024)}, u32[]{:S(2)}) copy-start(s32[2304]{0:T(1024)} %param.17) | copy-start | bytes 27652
  24.5 6.4 %collective-permute-start.6 = (bf16[16,2048]{1,0:T(8,128)(2,1)S(1)}, bf16[16,2048]{1,0:T(8,128)(2,1)S(1)}, u32[]{:S(2)}, u32[]{:S(2)}) collective-permute-start(bf16[16,2048]{1,0:T(8,128)(2,1)S(1)} %get-tuple-element.11), channel_id=1, source_target_pairs={{0,12},{2,14},{4,8},{6,10},{8,4},{10,6},{12,0},{14,2},{1,13},{3,15... | collective-permute-start | bytes 196616 | tf_op jit(solution)/shard_map/ppermute | solution.py:19
  28.2 5.2 %collective-permute-start.7 = (bf16[16,2048]{1,0:T(8,128)(2,1)S(1)}, bf16[16,2048]{1,0:T(8,128)(2,1)S(1)}, u32[]{:S(2)}, u32[]{:S(2)}) collective-permute-start(bf16[16,2048]{1,0:T(8,128)(2,1)S(1)} %get-tuple-element.11), channel_id=1, source_target_pairs={{0,8},{2,10},{4,12},{6,14},{8,0},{10,2},{12,4},{14,6},{1,9},{3,11}... | collective-permute-start | bytes 196616 | tf_op jit(solution)/shard_map/ppermute | solution.py:19
  28.2 5.2 %collective-permute-start.8 = (bf16[16,2048]{1,0:T(8,128)(2,1)S(1)}, bf16[16,2048]{1,0:T(8,128)(2,1)S(1)}, u32[]{:S(2)}, u32[]{:S(2)}) collective-permute-start(bf16[16,2048]{1,0:T(8,128)(2,1)S(1)} %get-tuple-element.11), channel_id=1, source_target_pairs={{0,4},{2,6},{4,0},{6,2},{8,12},{10,14},{12,8},{14,10},{1,5},{3,7},... | collective-permute-start | bytes 196616 | tf_op jit(solution)/shard_map/ppermute | solution.py:19
  33.4 4.3 %collective-permute-start.9 = (bf16[16,2048]{1,0:T(8,128)(2,1)S(1)}, bf16[16,2048]{1,0:T(8,128)(2,1)S(1)}, u32[]{:S(2)}, u32[]{:S(2)}) collective-permute-start(bf16[16,2048]{1,0:T(8,128)(2,1)S(1)} %add.3.own_ref.x_ref), channel_id=1, source_target_pairs={{0,2},{2,0},{4,6},{6,4},{8,10},{10,8},{12,14},{14,12},{1,3},{3,1},... | collective-permute-start | bytes 196616 | tf_op jit(solution)/shard_map/ppermute | solution.py:19
  39.1 1.3 %collective-permute-start.10 = (f32[8,2432]{1,0:T(8,128)S(1)}, f32[8,2432]{1,0:T(8,128)S(1)}, u32[]{:S(2)}, u32[]{:S(2)}) collective-permute-start(f32[8,2432]{1,0:T(8,128)S(1)} %get-tuple-element.13), channel_id=1, source_target_pairs={{0,1},{1,0},{2,3},{3,2},{4,5},{5,4},{6,7},{7,6},{8,9},{9,8},{10,11... | collective-permute-start | bytes 233480 | tf_op jit(solution)/shard_map/ppermute | solution.py:19

commit v6 on v5

--- a/solution.py
+++ b/solution.py
@@ -74,6 +74,7 @@
             pltpu.SemaphoreType.DMA((3,)),
         ],
         compiler_params=params(2),
+        cost_estimate=cost(40_000_000_000, 0),
         name="signed_units",
     )(in_hbm(gate), in_hbm(up), in_hbm(signs))
 
@@ -120,7 +121,6 @@
         in_specs=[VMEM] * 2,
         out_specs=(VMEM, VMEM),
         compiler_params=params(2),
-        cost_estimate=cost(400_000_000_000, 0),
         name="mix",
     )(own, other)
 
@@ -339,7 +339,7 @@
     res_rows, features = residual.shape
     count = hid.bit_length() - 1
     steps = [[0]] + [list(range(b, min(b + 2, count))) for b in range(1, count, 2)]
-    partners = [[m for m in range(hid - 1, 0, -1) if not m & ~sum(1 << b for b in bits)] for bits in steps]
+    partners = [[1 << b[0]] if len(b) == 1 else [1 << b[1], 1 << b[0] | 1 << b[1], 1 << b[0]] for b in steps]
 
     send = signed_units(gate_proj, up_proj, hadamard_signs)
     for k, (bits, masks) in enumerate(zip(steps, partners)):

time: 41.3 us -> 40.6 us (0.983)
  starting transfers between devices: 15.5 us -> 14.5 us
    ppermute x11, starting transfers between devices: 15.5 us -> 14.5 us  [exchange(): return lax.ppermute(block, axis, [(i, i ^ distance) for i in range(count)])]
  transfers between devices with their start and end apart: 11 -> 11, of which waited for: 9 -> 11; matrix products, arithmetic and copies ran while one was open for 0% -> 0% of each run, Pallas kernels for 11% -> 11%
where the time goes in v6:
time: 40.6 us; the launch traced here: 40.4 us
  waiting for transfers between devices  14.8 us (36%)
  starting transfers between devices  14.5 us (36%)
  Pallas kernels  10.2 us (25%)
  between operations  0.84 us (2%)
    ppermute x11, waiting for transfers between devices, exchange(): return lax.ppermute(block, axis, [(i, i ^ distance) for i in range(count)])  14.8 us
    ppermute x11, starting transfers between devices, exchange(): return lax.ppermute(block, axis, [(i, i ^ distance) for i in range(count)])  14.5 us
    pallas_call x2, Pallas kernels, down_half(): pl.pallas_call(kernel, out_shape=jax.ShapeDtypeStruct((count, half), out_...  4.57 us
    pallas_call x2, Pallas kernels, qkv_half(): pl.pallas_call(kernel, out_shape=tuple((jax.ShapeDtypeStruct((size, width...  2.67 us
    pallas_call x1, Pallas kernels, signed_units(): pl.pallas_call(signed_kernel, out_shape=jax.ShapeDtypeStruct(gate.shape,...  1.12 us
  transfers between devices with their start and end apart: 11, of which 11 were waited for; matrix products, arithmetic and copies ran while one was open for 0% of the time, Pallas kernels for 11%

profile of v6, /device:TPU:0, one launch (start us, length us, event | category | flops | bytes accessed | tf_op | source)
XLA Modules:
  0.0 40.4 jit_solution(14058054992925186127)
XLA Ops:
  0.7 1.1 %signed_units.1.own_ref = bf16[8,4096]{1,0:T(8,128)(2,1)S(1)} custom-call(bf16[8,4096]{1,0:T(8,128)(2,1)} %gate_hbm.1, bf16[8,4096]{1,0:T(8,128)(2,1)} %up_hbm.1, s32[1,4096]{1,0:T(1,128)} %bitcast.6), custom_call_target="tpu_custom_call" | custom-call | flops 40000000000 | tf_op jit(solution)/shard_map/signed_units/pallas_call | solution.py:65
  1.8 3.0 %collective-permute-start = (bf16[8,4096]{1,0:T(8,128)(2,1)S(1)}, bf16[8,4096]{1,0:T(8,128)(2,1)S(1)}, u32[]{:S(2)}, u32[]{:S(2)}) collective-permute-start(bf16[8,4096]{1,0:T(8,128)(2,1)S(1)} %signed_units.1.own_ref), channel_id=1, source_target_pairs={{0,2},{2,0},{4,6},{6,4},{8,10},{10,8},{12,14},{14,12},{1,3},{3,1},... | collective-permute-start | bytes 196616 | tf_op jit(solution)/shard_map/ppermute | solution.py:19
  4.8 2.2 %collective-permute-done.other_ref = bf16[8,4096]{1,0:T(8,128)(2,1)S(1)} collective-permute-done((bf16[8,4096]{1,0:T(8,128)(2,1)S(1)}, bf16[8,4096]{1,0:T(8,128)(2,1)S(1)}, u32[]{:S(2)}, u32[]{:S(2)}) %collective-permute-start) | collective-permute-done | bytes 65568 | tf_op jit(solution)/shard_map/ppermute | solution.py:19
  7.0 0.2 mix.1
  7.3 3.2 %collective-permute-start.1 = (bf16[8,4096]{1,0:T(8,128)(2,1)S(1)}, bf16[8,4096]{1,0:T(8,128)(2,1)S(1)}, u32[]{:S(2)}, u32[]{:S(2)}) collective-permute-start(bf16[8,4096]{1,0:T(8,128)(2,1)S(1)} %get-tuple-element.9), channel_id=1, source_target_pairs={{0,8},{2,10},{4,12},{6,14},{8,0},{10,2},{12,4},{14,6},{1,9},{3,11}... | collective-permute-start | bytes 196616 | tf_op jit(solution)/shard_map/ppermute | solution.py:19
  10.4 1.3 %collective-permute-start.2 = (bf16[8,4096]{1,0:T(8,128)(2,1)S(1)}, bf16[8,4096]{1,0:T(8,128)(2,1)S(1)}, u32[]{:S(2)}, u32[]{:S(2)}) collective-permute-start(bf16[8,4096]{1,0:T(8,128)(2,1)S(1)} %get-tuple-element.9), channel_id=1, source_target_pairs={{0,12},{2,14},{4,8},{6,10},{8,4},{10,6},{12,0},{14,2},{1,13},{3,15... | collective-permute-start | bytes 196616 | tf_op jit(solution)/shard_map/ppermute | solution.py:19
  11.8 0.2 collective-permute-start.3
  12.0 1.0 %collective-permute-done.1.refs_1_ = bf16[8,4096]{1,0:T(8,128)(2,1)S(1)} collective-permute-done((bf16[8,4096]{1,0:T(8,128)(2,1)S(1)}, bf16[8,4096]{1,0:T(8,128)(2,1)S(1)}, u32[]{:S(2)}, u32[]{:S(2)}) %collective-permute-start.1) | collective-permute-done | bytes 65568 | tf_op jit(solution)/shard_map/ppermute | solution.py:19
  13.0 3.6 %collective-permute-done.2.refs_2_ = bf16[8,4096]{1,0:T(8,128)(2,1)S(1)} collective-permute-done((bf16[8,4096]{1,0:T(8,128)(2,1)S(1)}, bf16[8,4096]{1,0:T(8,128)(2,1)S(1)}, u32[]{:S(2)}, u32[]{:S(2)}) %collective-permute-start.2) | collective-permute-done | bytes 65568 | tf_op jit(solution)/shard_map/ppermute | solution.py:19
  16.6 0.1 collective-permute-done.3.refs_3_
  16.8 0.1 combine.1.refs_0_
  16.8 0.1 collective-permute-start.4
  16.9 1.2 %collective-permute-done.4.refs_1_ = bf16[8,4096]{1,0:T(8,128)(2,1)S(1)} collective-permute-done((bf16[8,4096]{1,0:T(8,128)(2,1)S(1)}, bf16[8,4096]{1,0:T(8,128)(2,1)S(1)}, u32[]{:S(2)}, u32[]{:S(2)}) %collective-permute-start.4) | collective-permute-done | bytes 65568 | tf_op jit(solution)/shard_map/ppermute | solution.py:19
  18.2 2.3 %down_other.1 = bf16[16,2048]{1,0:T(8,128)(2,1)S(1)} custom-call(bf16[16,4096]{1,0:T(8,128)(2,1)S(1)} %gather_rows.1.x_ref, bf16[4096,4096]{1,0:T(8,128)(2,1)S(1)} %copy-done, s32[1,4096]{1,0:T(1,128)S(1)} %bitcast.4, bf16[2,4096]{1,0:T(2,128)(2,1)S(1)} %copy-done.2), custom_call_target="tpu_custom_call" | custom-call | flops 268435456 | bytes 16777216 | tf_op jit(solution)/shard_map/down_other/pallas_call | solution.py:224
  20.5 1.5 %collective-permute-start.5 = (bf16[16,2048]{1,0:T(8,128)(2,1)S(1)}, bf16[16,2048]{1,0:T(8,128)(2,1)S(1)}, u32[]{:S(2)}, u32[]{:S(2)}) collective-permute-start(bf16[16,2048]{1,0:T(8,128)(2,1)S(1)} %down_other.1), channel_id=1, source_target_pairs={{0,2},{2,0},{4,6},{6,4},{8,10},{10,8},{12,14},{14,12},{1,3},{3,1},... | collective-permute-start | bytes 196616 | tf_op jit(solution)/shard_map/ppermute | solution.py:19
  22.0 2.3 %down_own.1.refs_0_ = f32[16,2048]{1,0:T(8,128)S(1)} custom-call(bf16[16,4096]{1,0:T(8,128)(2,1)S(1)} %gather_rows.1.x_ref, bf16[4096,4096]{1,0:T(8,128)(2,1)S(1)} %copy-done, s32[1,4096]{1,0:T(1,128)S(1)} %bitcast.5, bf16[2,4096]{1,0:T(2,128)(2,1)S(1)} %copy-done.2), custom_call_target="tpu_custom_call" | custom-call | flops 268435456 | bytes 16777216 | tf_op jit(solution)/shard_map/down_own/pallas_call | solution.py:224
  24.3 0.5 %collective-permute-done.5.refs_1_ = bf16[16,2048]{1,0:T(8,128)(2,1)S(1)} collective-permute-done((bf16[16,2048]{1,0:T(8,128)(2,1)S(1)}, bf16[16,2048]{1,0:T(8,128)(2,1)S(1)}, u32[]{:S(2)}, u32[]{:S(2)}) %collective-permute-start.5) | collective-permute-done | bytes 65568 | tf_op jit(solution)/shard_map/ppermute | solution.py:19
  24.8 0.0 copy-start.3
  24.8 1.5 %collective-permute-start.6 = (bf16[16,2048]{1,0:T(8,128)(2,1)S(1)}, bf16[16,2048]{1,0:T(8,128)(2,1)S(1)}, u32[]{:S(2)}, u32[]{:S(2)}) collective-permute-start(bf16[16,2048]{1,0:T(8,128)(2,1)S(1)} %get-tuple-element.11), channel_id=1, source_target_pairs={{0,8},{2,10},{4,12},{6,14},{8,0},{10,2},{12,4},{14,6},{1,9},{3,11}... | collective-permute-start | bytes 196616 | tf_op jit(solution)/shard_map/ppermute | solution.py:19
  26.4 0.9 %collective-permute-start.7 = (bf16[16,2048]{1,0:T(8,128)(2,1)S(1)}, bf16[16,2048]{1,0:T(8,128)(2,1)S(1)}, u32[]{:S(2)}, u32[]{:S(2)}) collective-permute-start(bf16[16,2048]{1,0:T(8,128)(2,1)S(1)} %get-tuple-element.11), channel_id=1, source_target_pairs={{0,12},{2,14},{4,8},{6,10},{8,4},{10,6},{12,0},{14,2},{1,13},{3,15... | collective-permute-start | bytes 196616 | tf_op jit(solution)/shard_map/ppermute | solution.py:19
  27.2 1.1 %collective-permute-start.8 = (bf16[16,2048]{1,0:T(8,128)(2,1)S(1)}, bf16[16,2048]{1,0:T(8,128)(2,1)S(1)}, u32[]{:S(2)}, u32[]{:S(2)}) collective-permute-start(bf16[16,2048]{1,0:T(8,128)(2,1)S(1)} %get-tuple-element.11), channel_id=1, source_target_pairs={{0,4},{2,6},{4,0},{6,2},{8,12},{10,14},{12,8},{14,10},{1,5},{3,7},... | collective-permute-start | bytes 196616 | tf_op jit(solution)/shard_map/ppermute | solution.py:19
  28.4 3.4 %collective-permute-done.6.refs_1_ = bf16[16,2048]{1,0:T(8,128)(2,1)S(1)} collective-permute-done((bf16[16,2048]{1,0:T(8,128)(2,1)S(1)}, bf16[16,2048]{1,0:T(8,128)(2,1)S(1)}, u32[]{:S(2)}, u32[]{:S(2)}) %collective-permute-start.6) | collective-permute-done | bytes 65568 | tf_op jit(solution)/shard_map/ppermute | solution.py:19
  31.7 0.8 %collective-permute-done.7.refs_2_ = bf16[16,2048]{1,0:T(8,128)(2,1)S(1)} collective-permute-done((bf16[16,2048]{1,0:T(8,128)(2,1)S(1)}, bf16[16,2048]{1,0:T(8,128)(2,1)S(1)}, u32[]{:S(2)}, u32[]{:S(2)}) %collective-permute-start.7) | collective-permute-done | bytes 65568 | tf_op jit(solution)/shard_map/ppermute | solution.py:19
  32.6 0.1 collective-permute-done.8.refs_3_
  32.7 1.6 %collective-permute-start.9 = (bf16[16,2048]{1,0:T(8,128)(2,1)S(1)}, bf16[16,2048]{1,0:T(8,128)(2,1)S(1)}, u32[]{:S(2)}, u32[]{:S(2)}) collective-permute-start(bf16[16,2048]{1,0:T(8,128)(2,1)S(1)} %add.3.own_ref.x_ref), channel_id=1, source_target_pairs={{0,2},{2,0},{4,6},{6,4},{8,10},{10,8},{12,14},{14,12},{1,3},{3,1},... | collective-permute-start | bytes 196616 | tf_op jit(solution)/shard_map/ppermute | solution.py:19
  34.3 1.3 %qkv_own.1.refs_0_ = f32[16,2432]{1,0:T(8,128)S(1)} custom-call(bf16[16,2048]{1,0:T(8,128)(2,1)S(1)} %add.3.own_ref.x_ref, bf16[1,4096]{1,0:T(2,128)(2,1)S(1)} %reshape.18.g_ref, bf16[4096,2304]{1,0:T(8,128)(2,1)S(1)} %bitcast.3), custom_call_target="tpu_custom_call" | custom-call | flops 150994944 | bytes 9437184 | tf_op jit(solution)/shard_map/qkv_own/pallas_call | solution.py:266
  35.6 1.4 %collective-permute-done.9.other_ref.x_ref = bf16[16,2048]{1,0:T(8,128)(2,1)S(1)} collective-permute-done((bf16[16,2048]{1,0:T(8,128)(2,1)S(1)}, bf16[16,2048]{1,0:T(8,128)(2,1)S(1)}, u32[]{:S(2)}, u32[]{:S(2)}) %collective-permute-start.9) | collective-permute-done | bytes 65568 | tf_op jit(solution)/shard_map/ppermute | solution.py:19
  37.0 1.3 %qkv_other.1 = (f32[8,2432]{1,0:T(8,128)S(1)}, f32[8,2432]{1,0:T(8,128)S(1)}) custom-call(bf16[16,2048]{1,0:T(8,128)(2,1)S(1)} %collective-permute-done.9.other_ref.x_ref, bf16[1,4096]{1,0:T(2,128)(2,1)S(1)} %reshape.18.g_ref, bf16[4096,2304]{1,0:T(8,128)(2,1)S(1)} %bitcast.3, f32[16,2432]{1,0:T(8,128)S(1)} %qkv_own.1.refs_0_), custom_call_target="tpu_custom_call" | custom-call | flops 150994944 | bytes 9437184 | tf_op jit(solution)/shard_map/qkv_other/pallas_call | solution.py:266
  38.3 0.1 collective-permute-start.10
  38.4 0.7 %take_rows.1 = bf16[2,4096]{1,0:T(2,128)(2,1)} custom-call(bf16[16,2048]{1,0:T(8,128)(2,1)S(1)} %add.3.own_ref.x_ref, bf16[16,2048]{1,0:T(8,128)(2,1)S(1)} %collective-permute-done.9.other_ref.x_ref), custom_call_target="tpu_custom_call" | custom-call | tf_op jit(solution)/shard_map/take_rows/pallas_call | solution.py:293
  39.2 0.5 %collective-permute-done.10.refs_1_ = f32[8,2432]{1,0:T(8,128)S(1)} collective-permute-done((f32[8,2432]{1,0:T(8,128)S(1)}, f32[8,2432]{1,0:T(8,128)S(1)}, u32[]{:S(2)}, u32[]{:S(2)}) %collective-permute-start.10) | collective-permute-done | bytes 77856 | tf_op jit(solution)/shard_map/ppermute | solution.py:19
  39.7 0.7 %finish.1 = bf16[8,2304]{1,0:T(8,128)(2,1)} custom-call(f32[8,2432]{1,0:T(8,128)S(1)} %get-tuple-element.12.refs_0_, f32[8,2432]{1,0:T(8,128)S(1)} %collective-permute-done.10.refs_1_, s32[1,2304]{1,0:T(1,128)S(1)} %reshape.19.refs_2_), custom_call_target="tpu_custom_call" | custom-call | tf_op jit(solution)/shard_map/finish/pallas_call | solution.py:316
  (25 shorter events, 0.1 us)
Async XLA Ops:
  0.6 17.6 %copy-start = (bf16[4096,4096]{1,0:T(8,128)(2,1)S(1)}, bf16[4096,4096]{1,0:T(8,128)(2,1)}, u32[]{:S(2)}) copy-start(bf16[4096,4096]{1,0:T(8,128)(2,1)} %w_ref.5) | copy-start | bytes 100663296
  0.6 17.6 %copy-start.1 = (s32[4096]{0:T(1024)S(1)}, s32[4096]{0:T(1024)}, u32[]{:S(2)}) copy-start(s32[4096]{0:T(1024)} %param.13) | copy-start | bytes 49156
  0.7 17.6 %copy-start.2 = (bf16[2,4096]{1,0:T(2,128)(2,1)S(1)}, bf16[2,4096]{1,0:T(2,128)(2,1)}, u32[]{:S(2)}) copy-start(bf16[2,4096]{1,0:T(2,128)(2,1)} %r_ref.3) | copy-start | bytes 49156
  1.8 5.2 %collective-permute-start = (bf16[8,4096]{1,0:T(8,128)(2,1)S(1)}, bf16[8,4096]{1,0:T(8,128)(2,1)S(1)}, u32[]{:S(2)}, u32[]{:S(2)}) collective-permute-start(bf16[8,4096]{1,0:T(8,128)(2,1)S(1)} %signed_units.1.own_ref), channel_id=1, source_target_pairs={{0,2},{2,0},{4,6},{6,4},{8,10},{10,8},{12,14},{14,12},{1,3},{3,1},... | collective-permute-start | bytes 196616 | tf_op jit(solution)/shard_map/ppermute | solution.py:19
  7.3 5.7 %collective-permute-start.1 = (bf16[8,4096]{1,0:T(8,128)(2,1)S(1)}, bf16[8,4096]{1,0:T(8,128)(2,1)S(1)}, u32[]{:S(2)}, u32[]{:S(2)}) collective-permute-start(bf16[8,4096]{1,0:T(8,128)(2,1)S(1)} %get-tuple-element.9), channel_id=1, source_target_pairs={{0,8},{2,10},{4,12},{6,14},{8,0},{10,2},{12,4},{14,6},{1,9},{3,11}... | collective-permute-start | bytes 196616 | tf_op jit(solution)/shard_map/ppermute | solution.py:19
  10.4 6.2 %collective-permute-start.2 = (bf16[8,4096]{1,0:T(8,128)(2,1)S(1)}, bf16[8,4096]{1,0:T(8,128)(2,1)S(1)}, u32[]{:S(2)}, u32[]{:S(2)}) collective-permute-start(bf16[8,4096]{1,0:T(8,128)(2,1)S(1)} %get-tuple-element.9), channel_id=1, source_target_pairs={{0,12},{2,14},{4,8},{6,10},{8,4},{10,6},{12,0},{14,2},{1,13},{3,15... | collective-permute-start | bytes 196616 | tf_op jit(solution)/shard_map/ppermute | solution.py:19
  11.8 5.0 %collective-permute-start.3 = (bf16[8,4096]{1,0:T(8,128)(2,1)S(1)}, bf16[8,4096]{1,0:T(8,128)(2,1)S(1)}, u32[]{:S(2)}, u32[]{:S(2)}) collective-permute-start(bf16[8,4096]{1,0:T(8,128)(2,1)S(1)} %get-tuple-element.9), channel_id=1, source_target_pairs={{0,4},{2,6},{4,0},{6,2},{8,12},{10,14},{12,8},{14,10},{1,5},{3,7},... | collective-permute-start | bytes 196616 | tf_op jit(solution)/shard_map/ppermute | solution.py:19
  16.8 1.3 %collective-permute-start.4 = (bf16[8,4096]{1,0:T(8,128)(2,1)S(1)}, bf16[8,4096]{1,0:T(8,128)(2,1)S(1)}, u32[]{:S(2)}, u32[]{:S(2)}) collective-permute-start(bf16[8,4096]{1,0:T(8,128)(2,1)S(1)} %combine.1.refs_0_), channel_id=1, source_target_pairs={{0,1},{1,0},{2,3},{3,2},{4,5},{5,4},{6,7},{7,6},{8,9},{9,8},{10,11... | collective-permute-start | bytes 196616 | tf_op jit(solution)/shard_map/ppermute | solution.py:19
  20.5 4.3 %collective-permute-start.5 = (bf16[16,2048]{1,0:T(8,128)(2,1)S(1)}, bf16[16,2048]{1,0:T(8,128)(2,1)S(1)}, u32[]{:S(2)}, u32[]{:S(2)}) collective-permute-start(bf16[16,2048]{1,0:T(8,128)(2,1)S(1)} %down_other.1), channel_id=1, source_target_pairs={{0,2},{2,0},{4,6},{6,4},{8,10},{10,8},{12,14},{14,12},{1,3},{3,1},... | collective-permute-start | bytes 196616 | tf_op jit(solution)/shard_map/ppermute | solution.py:19
  22.0 12.2 %slice-start = ((s8[18874368]{0:T(1024)(128)(4,1)}), s8[2097152]{0:T(1024)(128)(4,1)S(1)}, s32[]{:S(2)}) async-start(s8[18874368]{0:T(1024)(128)(4,1)} %bitcast.2), calls=%async_computation | async-start | bytes 4194304
  24.3 9.9 %copy-start.4 = (bf16[4096]{0:T(1024)(128)(2,1)S(1)}, bf16[4096]{0:T(1024)(128)(2,1)}, u32[]{:S(2)}) copy-start(bf16[4096]{0:T(1024)(128)(2,1)} %param.15) | copy-start | bytes 24580
  24.3 10.0 %slice-start.1 = ((s8[18874368]{0:T(1024)(128)(4,1)}), s8[4194304]{0:T(1024)(128)(4,1)S(1)}, s32[]{:S(2)}) async-start(s8[18874368]{0:T(1024)(128)(4,1)} %bitcast.2), calls=%async_computation.1 | async-start | bytes 8388608
  24.3 10.0 %slice-start.2 = ((s8[18874368]{0:T(1024)(128)(4,1)}), s8[4194304]{0:T(1024)(128)(4,1)S(1)}, s32[]{:S(2)}) async-start(s8[18874368]{0:T(1024)(128)(4,1)} %bitcast.2), calls=%async_computation.2 | async-start | bytes 8388608
  24.3 10.0 %slice-start.3 = ((s8[18874368]{0:T(1024)(128)(4,1)}), s8[4194304]{0:T(1024)(128)(4,1)S(1)}, s32[]{:S(2)}) async-start(s8[18874368]{0:T(1024)(128)(4,1)} %bitcast.2), calls=%async_computation.3 | async-start | bytes 8388608
  24.3 10.0 %slice-start.4 = ((s8[18874368]{0:T(1024)(128)(4,1)}), s8[4194304]{0:T(1024)(128)(4,1)S(1)}, s32[]{:S(2)}) async-start(s8[18874368]{0:T(1024)(128)(4,1)} %bitcast.2), calls=%async_computation.4 | async-start | bytes 8388608
  24.8 13.6 %copy-start.3 = (s32[2304]{0:T(1024)S(1)}, s32[2304]{0:T(1024)}, u32[]{:S(2)}) copy-start(s32[2304]{0:T(1024)} %param.17) | copy-start | bytes 27652
  24.8 6.9 %collective-permute-start.6 = (bf16[16,2048]{1,0:T(8,128)(2,1)S(1)}, bf16[16,2048]{1,0:T(8,128)(2,1)S(1)}, u32[]{:S(2)}, u32[]{:S(2)}) collective-permute-start(bf16[16,2048]{1,0:T(8,128)(2,1)S(1)} %get-tuple-element.11), channel_id=1, source_target_pairs={{0,8},{2,10},{4,12},{6,14},{8,0},{10,2},{12,4},{14,6},{1,9},{3,11}... | collective-permute-start | bytes 196616 | tf_op jit(solution)/shard_map/ppermute | solution.py:19
  26.4 6.2 %collective-permute-start.7 = (bf16[16,2048]{1,0:T(8,128)(2,1)S(1)}, bf16[16,2048]{1,0:T(8,128)(2,1)S(1)}, u32[]{:S(2)}, u32[]{:S(2)}) collective-permute-start(bf16[16,2048]{1,0:T(8,128)(2,1)S(1)} %get-tuple-element.11), channel_id=1, source_target_pairs={{0,12},{2,14},{4,8},{6,10},{8,4},{10,6},{12,0},{14,2},{1,13},{3,15... | collective-permute-start | bytes 196616 | tf_op jit(solution)/shard_map/ppermute | solution.py:19
  27.2 5.4 %collective-permute-start.8 = (bf16[16,2048]{1,0:T(8,128)(2,1)S(1)}, bf16[16,2048]{1,0:T(8,128)(2,1)S(1)}, u32[]{:S(2)}, u32[]{:S(2)}) collective-permute-start(bf16[16,2048]{1,0:T(8,128)(2,1)S(1)} %get-tuple-element.11), channel_id=1, source_target_pairs={{0,4},{2,6},{4,0},{6,2},{8,12},{10,14},{12,8},{14,10},{1,5},{3,7},... | collective-permute-start | bytes 196616 | tf_op jit(solution)/shard_map/ppermute | solution.py:19
  32.7 4.3 %collective-permute-start.9 = (bf16[16,2048]{1,0:T(8,128)(2,1)S(1)}, bf16[16,2048]{1,0:T(8,128)(2,1)S(1)}, u32[]{:S(2)}, u32[]{:S(2)}) collective-permute-start(bf16[16,2048]{1,0:T(8,128)(2,1)S(1)} %add.3.own_ref.x_ref), channel_id=1, source_target_pairs={{0,2},{2,0},{4,6},{6,4},{8,10},{10,8},{12,14},{14,12},{1,3},{3,1},... | collective-permute-start | bytes 196616 | tf_op jit(solution)/shard_map/ppermute | solution.py:19
  38.3 1.3 %collective-permute-start.10 = (f32[8,2432]{1,0:T(8,128)S(1)}, f32[8,2432]{1,0:T(8,128)S(1)}, u32[]{:S(2)}, u32[]{:S(2)}) collective-permute-start(f32[8,2432]{1,0:T(8,128)S(1)} %get-tuple-element.13), channel_id=1, source_target_pairs={{0,1},{1,0},{2,3},{3,2},{4,5},{5,4},{6,7},{7,6},{8,9},{9,8},{10,11... | collective-permute-start | bytes 233480 | tf_op jit(solution)/shard_map/ppermute | solution.py:19

commit v7 on v6

--- a/solution.py
+++ b/solution.py
@@ -40,7 +40,7 @@
 
 
 def tile_of(width):
-    parts = next(p for p in (1, 2, 3, 4, 6, 8, 9, 12) if width // p <= 1152 and width % (p * lanes) == 0)
+    parts = next(p for p in (1, 2, 3, 4, 6, 8, 9, 12) if width // p <= 2304 and width % (p * lanes) == 0)
     return width // parts
 
 
@@ -88,41 +88,58 @@
     return (1 - 2 * (both & 1)).astype(f32).astype(bf16)
 
 
-def mix_kernel(own_ref, other_ref, wide_ref, send_ref):
-    rows, width = own_ref.shape
-    matrix = hadamard_128()
-    upper = bit_of("hid", 1) == 1
-    own, other = own_ref[...].astype(f32), other_ref[...].astype(f32)
-    stacked = jnp.concatenate([other, own], axis=0).astype(bf16)
-    count = width // lanes
-    tall = jnp.concatenate([stacked[:, j * lanes : (j + 1) * lanes] for j in range(count)], axis=0)
+def lane_blocks(ref, matrix):
+    rows, width = ref.shape
+    wide = ref[...].astype(f32)
+    blocks = [wide[:, j * lanes : (j + 1) * lanes] for j in range(width // lanes)]
+    tall = jnp.concatenate(blocks, axis=0).astype(bf16)
     product = jnp.dot(tall, matrix, preferred_element_type=f32)
-    blocks = []
-    for j in range(count):
-        theirs = product[2 * j * rows : (2 * j + 1) * rows]
-        mine = product[(2 * j + 1) * rows : (2 * j + 2) * rows]
-        blocks.append(theirs + jnp.where(upper, -mine, mine))
-    step = 1
-    while step < len(blocks):
-        for j in range(len(blocks)):
-            if not j & step:
-                a, b = blocks[j], blocks[j | step]
-                blocks[j], blocks[j | step] = a + b, a - b
-        step *= 2
-    for j, block in enumerate(blocks):
-        wide_ref[:, j * lanes : (j + 1) * lanes] = block
-        send_ref[:, j * lanes : (j + 1) * lanes] = block.astype(bf16)
+    return [product[j * rows : (j + 1) * rows] for j in range(len(blocks))]
+
+
+def own_lanes(own):
+    def kernel(own_ref, mixed_ref, matrix_ref):
+        matrix = hadamard_128()
+        matrix_ref[...] = matrix
+        sign = (1 - 2 * bit_of("hid", 1)).astype(f32)
+        for j, block in enumerate(lane_blocks(own_ref, matrix)):
+            mixed_ref[:, j * lanes : (j + 1) * lanes] = block * sign
+
+    return pl.pallas_call(
+        kernel,
+        out_shape=(jax.ShapeDtypeStruct(own.shape, f32), jax.ShapeDtypeStruct((lanes, lanes), bf16)),
+        in_specs=[VMEM],
+        out_specs=(VMEM, VMEM),
+        compiler_params=params(2),
+        name="own_lanes",
+    )(own)
 
 
 def mix(own, other):
-    return pl.pallas_call(
-        mix_kernel,
-        out_shape=(jax.ShapeDtypeStruct(own.shape, f32), jax.ShapeDtypeStruct(own.shape, bf16)),
-        in_specs=[VMEM] * 2,
+    def kernel(mixed_ref, matrix_ref, other_ref, wide_ref, send_ref):
+        blocks = [
+            block + mixed_ref[:, j * lanes : (j + 1) * lanes]
+            for j, block in enumerate(lane_blocks(other_ref, matrix_ref[...]))
+        ]
+        step = 1
+        while step < len(blocks):
+            for j in range(len(blocks)):
+                if not j & step:
+                    a, b = blocks[j], blocks[j | step]
+                    blocks[j], blocks[j | step] = a + b, a - b
+            step *= 2
+        for j, block in enumerate(blocks):
+            wide_ref[:, j * lanes : (j + 1) * lanes] = block
+            send_ref[:, j * lanes : (j + 1) * lanes] = block.astype(bf16)
+
+    return pl.pallas_call(
+        kernel,
+        out_shape=(jax.ShapeDtypeStruct(other.shape, f32), jax.ShapeDtypeStruct(other.shape, bf16)),
+        in_specs=[VMEM] * 3,
         out_specs=(VMEM, VMEM),
         compiler_params=params(2),
         name="mix",
-    )(own, other)
+    )(*own_lanes(own), other)
 
 
 def combine(wide, others, masks, bits, factor):

time: 40.6 us -> 40.5 us (level)
  no operation moved by 1% of the time
where the time goes in v7:
time: 40.5 us; the launch traced here: 40.3 us
  waiting for transfers between devices  14.7 us (36%)
  starting transfers between devices  14.4 us (36%)
  Pallas kernels  10.3 us (25%)
  between operations  0.84 us (2%)
    ppermute x11, waiting for transfers between devices, exchange(): return lax.ppermute(block, axis, [(i, i ^ distance) for i in range(count)])  14.7 us
    ppermute x11, starting transfers between devices, exchange(): return lax.ppermute(block, axis, [(i, i ^ distance) for i in range(count)])  14.4 us
    pallas_call x2, Pallas kernels, down_half(): pl.pallas_call(kernel, out_shape=jax.ShapeDtypeStruct((count, half), out_...  4.58 us
    pallas_call x2, Pallas kernels, qkv_half(): pl.pallas_call(kernel, out_shape=tuple((jax.ShapeDtypeStruct((size, width...  2.68 us
    pallas_call x1, Pallas kernels, signed_units(): pl.pallas_call(signed_kernel, out_shape=jax.ShapeDtypeStruct(gate.shape,...  1.12 us
  transfers between devices with their start and end apart: 11, of which 11 were waited for; matrix products, arithmetic and copies ran while one was open for 0% of the time, Pallas kernels for 11%

profile of v7, /device:TPU:0, one launch (start us, length us, event | category | flops | bytes accessed | tf_op | source)
XLA Modules:
  0.0 40.3 jit_solution(12725558822594059080)
XLA Ops:
  0.7 1.1 %signed_units.1.own_ref = bf16[8,4096]{1,0:T(8,128)(2,1)S(1)} custom-call(bf16[8,4096]{1,0:T(8,128)(2,1)} %gate_hbm.1, bf16[8,4096]{1,0:T(8,128)(2,1)} %up_hbm.1, s32[1,4096]{1,0:T(1,128)} %bitcast.6), custom_call_target="tpu_custom_call" | custom-call | flops 40000000000 | tf_op jit(solution)/shard_map/signed_units/pallas_call | solution.py:65
  1.8 3.0 %collective-permute-start = (bf16[8,4096]{1,0:T(8,128)(2,1)S(1)}, bf16[8,4096]{1,0:T(8,128)(2,1)S(1)}, u32[]{:S(2)}, u32[]{:S(2)}) collective-permute-start(bf16[8,4096]{1,0:T(8,128)(2,1)S(1)} %signed_units.1.own_ref), channel_id=1, source_target_pairs={{0,2},{2,0},{4,6},{6,4},{8,10},{10,8},{12,14},{14,12},{1,3},{3,1},... | collective-permute-start | bytes 196616 | tf_op jit(solution)/shard_map/ppermute | solution.py:19
  4.8 0.2 own_lanes.1
  5.0 2.1 %collective-permute-done.other_ref = bf16[8,4096]{1,0:T(8,128)(2,1)S(1)} collective-permute-done((bf16[8,4096]{1,0:T(8,128)(2,1)S(1)}, bf16[8,4096]{1,0:T(8,128)(2,1)S(1)}, u32[]{:S(2)}, u32[]{:S(2)}) %collective-permute-start) | collective-permute-done | bytes 65568 | tf_op jit(solution)/shard_map/ppermute | solution.py:19
  7.0 0.2 mix.1
  7.2 3.2 %collective-permute-start.1 = (bf16[8,4096]{1,0:T(8,128)(2,1)S(1)}, bf16[8,4096]{1,0:T(8,128)(2,1)S(1)}, u32[]{:S(2)}, u32[]{:S(2)}) collective-permute-start(bf16[8,4096]{1,0:T(8,128)(2,1)S(1)} %get-tuple-element.13), channel_id=1, source_target_pairs={{0,8},{2,10},{4,12},{6,14},{8,0},{10,2},{12,4},{14,6},{1,9},{3,11}... | collective-permute-start | bytes 196616 | tf_op jit(solution)/shard_map/ppermute | solution.py:19
  10.4 1.3 %collective-permute-start.2 = (bf16[8,4096]{1,0:T(8,128)(2,1)S(1)}, bf16[8,4096]{1,0:T(8,128)(2,1)S(1)}, u32[]{:S(2)}, u32[]{:S(2)}) collective-permute-start(bf16[8,4096]{1,0:T(8,128)(2,1)S(1)} %get-tuple-element.13), channel_id=1, source_target_pairs={{0,12},{2,14},{4,8},{6,10},{8,4},{10,6},{12,0},{14,2},{1,13},{3,15... | collective-permute-start | bytes 196616 | tf_op jit(solution)/shard_map/ppermute | solution.py:19
  11.7 0.2 collective-permute-start.3
  12.0 1.0 %collective-permute-done.1.refs_1_ = bf16[8,4096]{1,0:T(8,128)(2,1)S(1)} collective-permute-done((bf16[8,4096]{1,0:T(8,128)(2,1)S(1)}, bf16[8,4096]{1,0:T(8,128)(2,1)S(1)}, u32[]{:S(2)}, u32[]{:S(2)}) %collective-permute-start.1) | collective-permute-done | bytes 65568 | tf_op jit(solution)/shard_map/ppermute | solution.py:19
  13.0 3.6 %collective-permute-done.2.refs_2_ = bf16[8,4096]{1,0:T(8,128)(2,1)S(1)} collective-permute-done((bf16[8,4096]{1,0:T(8,128)(2,1)S(1)}, bf16[8,4096]{1,0:T(8,128)(2,1)S(1)}, u32[]{:S(2)}, u32[]{:S(2)}) %collective-permute-start.2) | collective-permute-done | bytes 65568 | tf_op jit(solution)/shard_map/ppermute | solution.py:19
  16.6 0.1 collective-permute-done.3.refs_3_
  16.7 0.1 combine.1.refs_0_
  16.8 0.1 collective-permute-start.4
  16.9 1.2 %collective-permute-done.4.refs_1_ = bf16[8,4096]{1,0:T(8,128)(2,1)S(1)} collective-permute-done((bf16[8,4096]{1,0:T(8,128)(2,1)S(1)}, bf16[8,4096]{1,0:T(8,128)(2,1)S(1)}, u32[]{:S(2)}, u32[]{:S(2)}) %collective-permute-start.4) | collective-permute-done | bytes 65568 | tf_op jit(solution)/shard_map/ppermute | solution.py:19
  18.2 2.3 %down_other.1 = bf16[16,2048]{1,0:T(8,128)(2,1)S(1)} custom-call(bf16[16,4096]{1,0:T(8,128)(2,1)S(1)} %gather_rows.1.x_ref, bf16[4096,4096]{1,0:T(8,128)(2,1)S(1)} %copy-done, s32[1,4096]{1,0:T(1,128)S(1)} %bitcast.4, bf16[2,4096]{1,0:T(2,128)(2,1)S(1)} %copy-done.2), custom_call_target="tpu_custom_call" | custom-call | flops 268435456 | bytes 16777216 | tf_op jit(solution)/shard_map/down_other/pallas_call | solution.py:241
  20.5 1.5 %collective-permute-start.5 = (bf16[16,2048]{1,0:T(8,128)(2,1)S(1)}, bf16[16,2048]{1,0:T(8,128)(2,1)S(1)}, u32[]{:S(2)}, u32[]{:S(2)}) collective-permute-start(bf16[16,2048]{1,0:T(8,128)(2,1)S(1)} %down_other.1), channel_id=1, source_target_pairs={{0,2},{2,0},{4,6},{6,4},{8,10},{10,8},{12,14},{14,12},{1,3},{3,1},... | collective-permute-start | bytes 196616 | tf_op jit(solution)/shard_map/ppermute | solution.py:19
  22.0 2.3 %down_own.1.refs_0_ = f32[16,2048]{1,0:T(8,128)S(1)} custom-call(bf16[16,4096]{1,0:T(8,128)(2,1)S(1)} %gather_rows.1.x_ref, bf16[4096,4096]{1,0:T(8,128)(2,1)S(1)} %copy-done, s32[1,4096]{1,0:T(1,128)S(1)} %bitcast.5, bf16[2,4096]{1,0:T(2,128)(2,1)S(1)} %copy-done.2), custom_call_target="tpu_custom_call" | custom-call | flops 268435456 | bytes 16777216 | tf_op jit(solution)/shard_map/down_own/pallas_call | solution.py:241
  24.2 0.0 slice-start.1
  24.3 0.4 %collective-permute-done.5.refs_1_ = bf16[16,2048]{1,0:T(8,128)(2,1)S(1)} collective-permute-done((bf16[16,2048]{1,0:T(8,128)(2,1)S(1)}, bf16[16,2048]{1,0:T(8,128)(2,1)S(1)}, u32[]{:S(2)}, u32[]{:S(2)}) %collective-permute-start.5) | collective-permute-done | bytes 65568 | tf_op jit(solution)/shard_map/ppermute | solution.py:19
  24.8 1.5 %collective-permute-start.6 = (bf16[16,2048]{1,0:T(8,128)(2,1)S(1)}, bf16[16,2048]{1,0:T(8,128)(2,1)S(1)}, u32[]{:S(2)}, u32[]{:S(2)}) collective-permute-start(bf16[16,2048]{1,0:T(8,128)(2,1)S(1)} %get-tuple-element.15), channel_id=1, source_target_pairs={{0,8},{2,10},{4,12},{6,14},{8,0},{10,2},{12,4},{14,6},{1,9},{3,11}... | collective-permute-start | bytes 196616 | tf_op jit(solution)/shard_map/ppermute | solution.py:19
  26.3 0.9 %collective-permute-start.7 = (bf16[16,2048]{1,0:T(8,128)(2,1)S(1)}, bf16[16,2048]{1,0:T(8,128)(2,1)S(1)}, u32[]{:S(2)}, u32[]{:S(2)}) collective-permute-start(bf16[16,2048]{1,0:T(8,128)(2,1)S(1)} %get-tuple-element.15), channel_id=1, source_target_pairs={{0,12},{2,14},{4,8},{6,10},{8,4},{10,6},{12,0},{14,2},{1,13},{3,15... | collective-permute-start | bytes 196616 | tf_op jit(solution)/shard_map/ppermute | solution.py:19
  27.2 1.1 %collective-permute-start.8 = (bf16[16,2048]{1,0:T(8,128)(2,1)S(1)}, bf16[16,2048]{1,0:T(8,128)(2,1)S(1)}, u32[]{:S(2)}, u32[]{:S(2)}) collective-permute-start(bf16[16,2048]{1,0:T(8,128)(2,1)S(1)} %get-tuple-element.15), channel_id=1, source_target_pairs={{0,4},{2,6},{4,0},{6,2},{8,12},{10,14},{12,8},{14,10},{1,5},{3,7},... | collective-permute-start | bytes 196616 | tf_op jit(solution)/shard_map/ppermute | solution.py:19
  28.3 3.4 %collective-permute-done.6.refs_1_ = bf16[16,2048]{1,0:T(8,128)(2,1)S(1)} collective-permute-done((bf16[16,2048]{1,0:T(8,128)(2,1)S(1)}, bf16[16,2048]{1,0:T(8,128)(2,1)S(1)}, u32[]{:S(2)}, u32[]{:S(2)}) %collective-permute-start.6) | collective-permute-done | bytes 65568 | tf_op jit(solution)/shard_map/ppermute | solution.py:19
  31.7 0.8 %collective-permute-done.7.refs_2_ = bf16[16,2048]{1,0:T(8,128)(2,1)S(1)} collective-permute-done((bf16[16,2048]{1,0:T(8,128)(2,1)S(1)}, bf16[16,2048]{1,0:T(8,128)(2,1)S(1)}, u32[]{:S(2)}, u32[]{:S(2)}) %collective-permute-start.7) | collective-permute-done | bytes 65568 | tf_op jit(solution)/shard_map/ppermute | solution.py:19
  32.5 0.1 collective-permute-done.8.refs_3_
  32.6 1.5 %collective-permute-start.9 = (bf16[16,2048]{1,0:T(8,128)(2,1)S(1)}, bf16[16,2048]{1,0:T(8,128)(2,1)S(1)}, u32[]{:S(2)}, u32[]{:S(2)}) collective-permute-start(bf16[16,2048]{1,0:T(8,128)(2,1)S(1)} %add.3.own_ref.x_ref), channel_id=1, source_target_pairs={{0,2},{2,0},{4,6},{6,4},{8,10},{10,8},{12,14},{14,12},{1,3},{3,1},... | collective-permute-start | bytes 196616 | tf_op jit(solution)/shard_map/ppermute | solution.py:19
  34.3 1.3 %qkv_own.1.refs_0_ = f32[16,2432]{1,0:T(8,128)S(1)} custom-call(bf16[16,2048]{1,0:T(8,128)(2,1)S(1)} %add.3.own_ref.x_ref, bf16[1,4096]{1,0:T(2,128)(2,1)S(1)} %reshape.18.g_ref, bf16[4096,2304]{1,0:T(8,128)(2,1)S(1)} %bitcast.3), custom_call_target="tpu_custom_call" | custom-call | flops 150994944 | bytes 9437184 | tf_op jit(solution)/shard_map/qkv_own/pallas_call | solution.py:283
  35.6 1.4 %collective-permute-done.9.other_ref.x_ref = bf16[16,2048]{1,0:T(8,128)(2,1)S(1)} collective-permute-done((bf16[16,2048]{1,0:T(8,128)(2,1)S(1)}, bf16[16,2048]{1,0:T(8,128)(2,1)S(1)}, u32[]{:S(2)}, u32[]{:S(2)}) %collective-permute-start.9) | collective-permute-done | bytes 65568 | tf_op jit(solution)/shard_map/ppermute | solution.py:19
  37.0 1.3 %qkv_other.1 = (f32[8,2432]{1,0:T(8,128)S(1)}, f32[8,2432]{1,0:T(8,128)S(1)}) custom-call(bf16[16,2048]{1,0:T(8,128)(2,1)S(1)} %collective-permute-done.9.other_ref.x_ref, bf16[1,4096]{1,0:T(2,128)(2,1)S(1)} %reshape.18.g_ref, bf16[4096,2304]{1,0:T(8,128)(2,1)S(1)} %bitcast.3, f32[16,2432]{1,0:T(8,128)S(1)} %qkv_own.1.refs_0_), custom_call_target="tpu_custom_call" | custom-call | flops 150994944 | bytes 9437184 | tf_op jit(solution)/shard_map/qkv_other/pallas_call | solution.py:283
  38.3 0.7 %take_rows.1 = bf16[2,4096]{1,0:T(2,128)(2,1)} custom-call(bf16[16,2048]{1,0:T(8,128)(2,1)S(1)} %add.3.own_ref.x_ref, bf16[16,2048]{1,0:T(8,128)(2,1)S(1)} %collective-permute-done.9.other_ref.x_ref), custom_call_target="tpu_custom_call" | custom-call | tf_op jit(solution)/shard_map/take_rows/pallas_call | solution.py:310
  39.1 0.5 %collective-permute-done.10.refs_1_ = f32[8,2432]{1,0:T(8,128)S(1)} collective-permute-done((f32[8,2432]{1,0:T(8,128)S(1)}, f32[8,2432]{1,0:T(8,128)S(1)}, u32[]{:S(2)}, u32[]{:S(2)}) %collective-permute-start.10) | collective-permute-done | bytes 77856 | tf_op jit(solution)/shard_map/ppermute | solution.py:19
  39.6 0.7 %finish.1 = bf16[8,2304]{1,0:T(8,128)(2,1)} custom-call(f32[8,2432]{1,0:T(8,128)S(1)} %get-tuple-element.16.refs_0_, f32[8,2432]{1,0:T(8,128)S(1)} %collective-permute-done.10.refs_1_, s32[1,2304]{1,0:T(1,128)S(1)} %reshape.19.refs_2_), custom_call_target="tpu_custom_call" | custom-call | tf_op jit(solution)/shard_map/finish/pallas_call | solution.py:333
  (26 shorter events, 0.1 us)
Async XLA Ops:
  0.6 17.5 %copy-start = (bf16[4096,4096]{1,0:T(8,128)(2,1)S(1)}, bf16[4096,4096]{1,0:T(8,128)(2,1)}, u32[]{:S(2)}) copy-start(bf16[4096,4096]{1,0:T(8,128)(2,1)} %w_ref.5) | copy-start | bytes 100663296
  0.6 17.5 %copy-start.1 = (s32[4096]{0:T(1024)S(1)}, s32[4096]{0:T(1024)}, u32[]{:S(2)}) copy-start(s32[4096]{0:T(1024)} %param.13) | copy-start | bytes 49156
  0.7 17.5 %copy-start.2 = (bf16[2,4096]{1,0:T(2,128)(2,1)S(1)}, bf16[2,4096]{1,0:T(2,128)(2,1)}, u32[]{:S(2)}) copy-start(bf16[2,4096]{1,0:T(2,128)(2,1)} %r_ref.3) | copy-start | bytes 49156
  1.8 5.2 %collective-permute-start = (bf16[8,4096]{1,0:T(8,128)(2,1)S(1)}, bf16[8,4096]{1,0:T(8,128)(2,1)S(1)}, u32[]{:S(2)}, u32[]{:S(2)}) collective-permute-start(bf16[8,4096]{1,0:T(8,128)(2,1)S(1)} %signed_units.1.own_ref), channel_id=1, source_target_pairs={{0,2},{2,0},{4,6},{6,4},{8,10},{10,8},{12,14},{14,12},{1,3},{3,1},... | collective-permute-start | bytes 196616 | tf_op jit(solution)/shard_map/ppermute | solution.py:19
  7.2 5.7 %collective-permute-start.1 = (bf16[8,4096]{1,0:T(8,128)(2,1)S(1)}, bf16[8,4096]{1,0:T(8,128)(2,1)S(1)}, u32[]{:S(2)}, u32[]{:S(2)}) collective-permute-start(bf16[8,4096]{1,0:T(8,128)(2,1)S(1)} %get-tuple-element.13), channel_id=1, source_target_pairs={{0,8},{2,10},{4,12},{6,14},{8,0},{10,2},{12,4},{14,6},{1,9},{3,11}... | collective-permute-start | bytes 196616 | tf_op jit(solution)/shard_map/ppermute | solution.py:19
  10.4 6.2 %collective-permute-start.2 = (bf16[8,4096]{1,0:T(8,128)(2,1)S(1)}, bf16[8,4096]{1,0:T(8,128)(2,1)S(1)}, u32[]{:S(2)}, u32[]{:S(2)}) collective-permute-start(bf16[8,4096]{1,0:T(8,128)(2,1)S(1)} %get-tuple-element.13), channel_id=1, source_target_pairs={{0,12},{2,14},{4,8},{6,10},{8,4},{10,6},{12,0},{14,2},{1,13},{3,15... | collective-permute-start | bytes 196616 | tf_op jit(solution)/shard_map/ppermute | solution.py:19
  11.7 5.0 %collective-permute-start.3 = (bf16[8,4096]{1,0:T(8,128)(2,1)S(1)}, bf16[8,4096]{1,0:T(8,128)(2,1)S(1)}, u32[]{:S(2)}, u32[]{:S(2)}) collective-permute-start(bf16[8,4096]{1,0:T(8,128)(2,1)S(1)} %get-tuple-element.13), channel_id=1, source_target_pairs={{0,4},{2,6},{4,0},{6,2},{8,12},{10,14},{12,8},{14,10},{1,5},{3,7},... | collective-permute-start | bytes 196616 | tf_op jit(solution)/shard_map/ppermute | solution.py:19
  16.8 1.3 %collective-permute-start.4 = (bf16[8,4096]{1,0:T(8,128)(2,1)S(1)}, bf16[8,4096]{1,0:T(8,128)(2,1)S(1)}, u32[]{:S(2)}, u32[]{:S(2)}) collective-permute-start(bf16[8,4096]{1,0:T(8,128)(2,1)S(1)} %combine.1.refs_0_), channel_id=1, source_target_pairs={{0,1},{1,0},{2,3},{3,2},{4,5},{5,4},{6,7},{7,6},{8,9},{9,8},{10,11... | collective-permute-start | bytes 196616 | tf_op jit(solution)/shard_map/ppermute | solution.py:19
  20.5 4.3 %collective-permute-start.5 = (bf16[16,2048]{1,0:T(8,128)(2,1)S(1)}, bf16[16,2048]{1,0:T(8,128)(2,1)S(1)}, u32[]{:S(2)}, u32[]{:S(2)}) collective-permute-start(bf16[16,2048]{1,0:T(8,128)(2,1)S(1)} %down_other.1), channel_id=1, source_target_pairs={{0,2},{2,0},{4,6},{6,4},{8,10},{10,8},{12,14},{14,12},{1,3},{3,1},... | collective-permute-start | bytes 196616 | tf_op jit(solution)/shard_map/ppermute | solution.py:19
  22.0 12.2 %slice-start = ((s8[18874368]{0:T(1024)(128)(4,1)}), s8[2097152]{0:T(1024)(128)(4,1)S(1)}, s32[]{:S(2)}) async-start(s8[18874368]{0:T(1024)(128)(4,1)} %bitcast.2), calls=%async_computation | async-start | bytes 4194304
  24.2 9.9 %copy-start.4 = (bf16[4096]{0:T(1024)(128)(2,1)S(1)}, bf16[4096]{0:T(1024)(128)(2,1)}, u32[]{:S(2)}) copy-start(bf16[4096]{0:T(1024)(128)(2,1)} %param.15) | copy-start | bytes 24580
  24.2 10.0 %slice-start.1 = ((s8[18874368]{0:T(1024)(128)(4,1)}), s8[4194304]{0:T(1024)(128)(4,1)S(1)}, s32[]{:S(2)}) async-start(s8[18874368]{0:T(1024)(128)(4,1)} %bitcast.2), calls=%async_computation.1 | async-start | bytes 8388608
  24.3 10.0 %slice-start.2 = ((s8[18874368]{0:T(1024)(128)(4,1)}), s8[4194304]{0:T(1024)(128)(4,1)S(1)}, s32[]{:S(2)}) async-start(s8[18874368]{0:T(1024)(128)(4,1)} %bitcast.2), calls=%async_computation.2 | async-start | bytes 8388608
  24.3 10.0 %slice-start.3 = ((s8[18874368]{0:T(1024)(128)(4,1)}), s8[4194304]{0:T(1024)(128)(4,1)S(1)}, s32[]{:S(2)}) async-start(s8[18874368]{0:T(1024)(128)(4,1)} %bitcast.2), calls=%async_computation.3 | async-start | bytes 8388608
  24.3 10.0 %slice-start.4 = ((s8[18874368]{0:T(1024)(128)(4,1)}), s8[4194304]{0:T(1024)(128)(4,1)S(1)}, s32[]{:S(2)}) async-start(s8[18874368]{0:T(1024)(128)(4,1)} %bitcast.2), calls=%async_computation.4 | async-start | bytes 8388608
  24.8 13.6 %copy-start.3 = (s32[2304]{0:T(1024)S(1)}, s32[2304]{0:T(1024)}, u32[]{:S(2)}) copy-start(s32[2304]{0:T(1024)} %param.17) | copy-start | bytes 27652
  24.8 6.9 %collective-permute-start.6 = (bf16[16,2048]{1,0:T(8,128)(2,1)S(1)}, bf16[16,2048]{1,0:T(8,128)(2,1)S(1)}, u32[]{:S(2)}, u32[]{:S(2)}) collective-permute-start(bf16[16,2048]{1,0:T(8,128)(2,1)S(1)} %get-tuple-element.15), channel_id=1, source_target_pairs={{0,8},{2,10},{4,12},{6,14},{8,0},{10,2},{12,4},{14,6},{1,9},{3,11}... | collective-permute-start | bytes 196616 | tf_op jit(solution)/shard_map/ppermute | solution.py:19
  26.3 6.2 %collective-permute-start.7 = (bf16[16,2048]{1,0:T(8,128)(2,1)S(1)}, bf16[16,2048]{1,0:T(8,128)(2,1)S(1)}, u32[]{:S(2)}, u32[]{:S(2)}) collective-permute-start(bf16[16,2048]{1,0:T(8,128)(2,1)S(1)} %get-tuple-element.15), channel_id=1, source_target_pairs={{0,12},{2,14},{4,8},{6,10},{8,4},{10,6},{12,0},{14,2},{1,13},{3,15... | collective-permute-start | bytes 196616 | tf_op jit(solution)/shard_map/ppermute | solution.py:19
  27.2 5.4 %collective-permute-start.8 = (bf16[16,2048]{1,0:T(8,128)(2,1)S(1)}, bf16[16,2048]{1,0:T(8,128)(2,1)S(1)}, u32[]{:S(2)}, u32[]{:S(2)}) collective-permute-start(bf16[16,2048]{1,0:T(8,128)(2,1)S(1)} %get-tuple-element.15), channel_id=1, source_target_pairs={{0,4},{2,6},{4,0},{6,2},{8,12},{10,14},{12,8},{14,10},{1,5},{3,7},... | collective-permute-start | bytes 196616 | tf_op jit(solution)/shard_map/ppermute | solution.py:19
  32.6 4.3 %collective-permute-start.9 = (bf16[16,2048]{1,0:T(8,128)(2,1)S(1)}, bf16[16,2048]{1,0:T(8,128)(2,1)S(1)}, u32[]{:S(2)}, u32[]{:S(2)}) collective-permute-start(bf16[16,2048]{1,0:T(8,128)(2,1)S(1)} %add.3.own_ref.x_ref), channel_id=1, source_target_pairs={{0,2},{2,0},{4,6},{6,4},{8,10},{10,8},{12,14},{14,12},{1,3},{3,1},... | collective-permute-start | bytes 196616 | tf_op jit(solution)/shard_map/ppermute | solution.py:19
  38.3 1.3 %collective-permute-start.10 = (f32[8,2432]{1,0:T(8,128)S(1)}, f32[8,2432]{1,0:T(8,128)S(1)}, u32[]{:S(2)}, u32[]{:S(2)}) collective-permute-start(f32[8,2432]{1,0:T(8,128)S(1)} %get-tuple-element.17), channel_id=1, source_target_pairs={{0,1},{1,0},{2,3},{3,2},{4,5},{5,4},{6,7},{7,6},{8,9},{9,8},{10,11... | collective-permute-start | bytes 233480 | tf_op jit(solution)/shard_map/ppermute | solution.py:19

commit v8 on v7

--- a/solution.py
+++ b/solution.py
@@ -220,7 +220,7 @@
 def down_half(rows, weight, scale, residual, own_rows, other_half, out_type):
     count, depth = rows.shape
     half = weight.shape[1] // 2
-    bn = tile_of(half)
+    bn = half // 2
 
     def kernel(x_ref, w_ref, s_ref, r_ref, o_ref):
         side = bit_of("hid", 1)

time: 40.5 us -> 40.5 us (level)
  no operation moved by 1% of the time
where the time goes in v8:
time: 40.5 us; the launch traced here: 40.3 us
  waiting for transfers between devices  14.7 us (36%)
  starting transfers between devices  14.4 us (36%)
  Pallas kernels  10.3 us (25%)
  between operations  0.84 us (2%)
    ppermute x11, waiting for transfers between devices, exchange(): return lax.ppermute(block, axis, [(i, i ^ distance) for i in range(count)])  14.7 us
    ppermute x11, starting transfers between devices, exchange(): return lax.ppermute(block, axis, [(i, i ^ distance) for i in range(count)])  14.4 us
    pallas_call x2, Pallas kernels, down_half(): pl.pallas_call(kernel, out_shape=jax.ShapeDtypeStruct((count, half), out_...  4.57 us
    pallas_call x2, Pallas kernels, qkv_half(): pl.pallas_call(kernel, out_shape=tuple((jax.ShapeDtypeStruct((size, width...  2.68 us
    pallas_call x1, Pallas kernels, signed_units(): pl.pallas_call(signed_kernel, out_shape=jax.ShapeDtypeStruct(gate.shape,...  1.12 us
  transfers between devices with their start and end apart: 11, of which 11 were waited for; matrix products, arithmetic and copies ran while one was open for 0% of the time, Pallas kernels for 11%

profile of v8, /device:TPU:0, one launch (start us, length us, event | category | flops | bytes accessed | tf_op | source)
XLA Modules:
  0.0 40.3 jit_solution(3447381883053554969)
XLA Ops:
  0.7 1.1 %signed_units.1.own_ref = bf16[8,4096]{1,0:T(8,128)(2,1)S(1)} custom-call(bf16[8,4096]{1,0:T(8,128)(2,1)} %gate_hbm.1, bf16[8,4096]{1,0:T(8,128)(2,1)} %up_hbm.1, s32[1,4096]{1,0:T(1,128)} %bitcast.6), custom_call_target="tpu_custom_call" | custom-call | flops 40000000000 | tf_op jit(solution)/shard_map/signed_units/pallas_call | solution.py:65
  1.8 3.0 %collective-permute-start = (bf16[8,4096]{1,0:T(8,128)(2,1)S(1)}, bf16[8,4096]{1,0:T(8,128)(2,1)S(1)}, u32[]{:S(2)}, u32[]{:S(2)}) collective-permute-start(bf16[8,4096]{1,0:T(8,128)(2,1)S(1)} %signed_units.1.own_ref), channel_id=1, source_target_pairs={{0,2},{2,0},{4,6},{6,4},{8,10},{10,8},{12,14},{14,12},{1,3},{3,1},... | collective-permute-start | bytes 196616 | tf_op jit(solution)/shard_map/ppermute | solution.py:19
  4.8 0.2 own_lanes.1
  5.0 2.1 %collective-permute-done.other_ref = bf16[8,4096]{1,0:T(8,128)(2,1)S(1)} collective-permute-done((bf16[8,4096]{1,0:T(8,128)(2,1)S(1)}, bf16[8,4096]{1,0:T(8,128)(2,1)S(1)}, u32[]{:S(2)}, u32[]{:S(2)}) %collective-permute-start) | collective-permute-done | bytes 65568 | tf_op jit(solution)/shard_map/ppermute | solution.py:19
  7.0 0.2 mix.1
  7.2 3.2 %collective-permute-start.1 = (bf16[8,4096]{1,0:T(8,128)(2,1)S(1)}, bf16[8,4096]{1,0:T(8,128)(2,1)S(1)}, u32[]{:S(2)}, u32[]{:S(2)}) collective-permute-start(bf16[8,4096]{1,0:T(8,128)(2,1)S(1)} %get-tuple-element.13), channel_id=1, source_target_pairs={{0,8},{2,10},{4,12},{6,14},{8,0},{10,2},{12,4},{14,6},{1,9},{3,11}... | collective-permute-start | bytes 196616 | tf_op jit(solution)/shard_map/ppermute | solution.py:19
  10.4 1.3 %collective-permute-start.2 = (bf16[8,4096]{1,0:T(8,128)(2,1)S(1)}, bf16[8,4096]{1,0:T(8,128)(2,1)S(1)}, u32[]{:S(2)}, u32[]{:S(2)}) collective-permute-start(bf16[8,4096]{1,0:T(8,128)(2,1)S(1)} %get-tuple-element.13), channel_id=1, source_target_pairs={{0,12},{2,14},{4,8},{6,10},{8,4},{10,6},{12,0},{14,2},{1,13},{3,15... | collective-permute-start | bytes 196616 | tf_op jit(solution)/shard_map/ppermute | solution.py:19
  11.7 0.2 collective-permute-start.3
  12.0 1.0 %collective-permute-done.1.refs_1_ = bf16[8,4096]{1,0:T(8,128)(2,1)S(1)} collective-permute-done((bf16[8,4096]{1,0:T(8,128)(2,1)S(1)}, bf16[8,4096]{1,0:T(8,128)(2,1)S(1)}, u32[]{:S(2)}, u32[]{:S(2)}) %collective-permute-start.1) | collective-permute-done | bytes 65568 | tf_op jit(solution)/shard_map/ppermute | solution.py:19
  13.0 3.6 %collective-permute-done.2.refs_2_ = bf16[8,4096]{1,0:T(8,128)(2,1)S(1)} collective-permute-done((bf16[8,4096]{1,0:T(8,128)(2,1)S(1)}, bf16[8,4096]{1,0:T(8,128)(2,1)S(1)}, u32[]{:S(2)}, u32[]{:S(2)}) %collective-permute-start.2) | collective-permute-done | bytes 65568 | tf_op jit(solution)/shard_map/ppermute | solution.py:19
  16.6 0.1 collective-permute-done.3.refs_3_
  16.7 0.1 combine.1.refs_0_
  16.8 0.1 collective-permute-start.4
  16.9 1.2 %collective-permute-done.4.refs_1_ = bf16[8,4096]{1,0:T(8,128)(2,1)S(1)} collective-permute-done((bf16[8,4096]{1,0:T(8,128)(2,1)S(1)}, bf16[8,4096]{1,0:T(8,128)(2,1)S(1)}, u32[]{:S(2)}, u32[]{:S(2)}) %collective-permute-start.4) | collective-permute-done | bytes 65568 | tf_op jit(solution)/shard_map/ppermute | solution.py:19
  18.2 2.3 %down_other.1 = bf16[16,2048]{1,0:T(8,128)(2,1)S(1)} custom-call(bf16[16,4096]{1,0:T(8,128)(2,1)S(1)} %gather_rows.1.x_ref, bf16[4096,4096]{1,0:T(8,128)(2,1)S(1)} %copy-done, s32[1,4096]{1,0:T(1,128)S(1)} %bitcast.4, bf16[2,4096]{1,0:T(2,128)(2,1)S(1)} %copy-done.2), custom_call_target="tpu_custom_call" | custom-call | flops 268435456 | bytes 16777216 | tf_op jit(solution)/shard_map/down_other/pallas_call | solution.py:241
  20.5 1.5 %collective-permute-start.5 = (bf16[16,2048]{1,0:T(8,128)(2,1)S(1)}, bf16[16,2048]{1,0:T(8,128)(2,1)S(1)}, u32[]{:S(2)}, u32[]{:S(2)}) collective-permute-start(bf16[16,2048]{1,0:T(8,128)(2,1)S(1)} %down_other.1), channel_id=1, source_target_pairs={{0,2},{2,0},{4,6},{6,4},{8,10},{10,8},{12,14},{14,12},{1,3},{3,1},... | collective-permute-start | bytes 196616 | tf_op jit(solution)/shard_map/ppermute | solution.py:19
  22.0 2.3 %down_own.1.refs_0_ = f32[16,2048]{1,0:T(8,128)S(1)} custom-call(bf16[16,4096]{1,0:T(8,128)(2,1)S(1)} %gather_rows.1.x_ref, bf16[4096,4096]{1,0:T(8,128)(2,1)S(1)} %copy-done, s32[1,4096]{1,0:T(1,128)S(1)} %bitcast.5, bf16[2,4096]{1,0:T(2,128)(2,1)S(1)} %copy-done.2), custom_call_target="tpu_custom_call" | custom-call | flops 268435456 | bytes 16777216 | tf_op jit(solution)/shard_map/down_own/pallas_call | solution.py:241
  24.3 0.5 %collective-permute-done.5.refs_1_ = bf16[16,2048]{1,0:T(8,128)(2,1)S(1)} collective-permute-done((bf16[16,2048]{1,0:T(8,128)(2,1)S(1)}, bf16[16,2048]{1,0:T(8,128)(2,1)S(1)}, u32[]{:S(2)}, u32[]{:S(2)}) %collective-permute-start.5) | collective-permute-done | bytes 65568 | tf_op jit(solution)/shard_map/ppermute | solution.py:19
  24.8 0.0 copy-start.3
  24.8 1.5 %collective-permute-start.6 = (bf16[16,2048]{1,0:T(8,128)(2,1)S(1)}, bf16[16,2048]{1,0:T(8,128)(2,1)S(1)}, u32[]{:S(2)}, u32[]{:S(2)}) collective-permute-start(bf16[16,2048]{1,0:T(8,128)(2,1)S(1)} %get-tuple-element.15), channel_id=1, source_target_pairs={{0,8},{2,10},{4,12},{6,14},{8,0},{10,2},{12,4},{14,6},{1,9},{3,11}... | collective-permute-start | bytes 196616 | tf_op jit(solution)/shard_map/ppermute | solution.py:19
  26.3 0.9 %collective-permute-start.7 = (bf16[16,2048]{1,0:T(8,128)(2,1)S(1)}, bf16[16,2048]{1,0:T(8,128)(2,1)S(1)}, u32[]{:S(2)}, u32[]{:S(2)}) collective-permute-start(bf16[16,2048]{1,0:T(8,128)(2,1)S(1)} %get-tuple-element.15), channel_id=1, source_target_pairs={{0,12},{2,14},{4,8},{6,10},{8,4},{10,6},{12,0},{14,2},{1,13},{3,15... | collective-permute-start | bytes 196616 | tf_op jit(solution)/shard_map/ppermute | solution.py:19
  27.2 1.1 %collective-permute-start.8 = (bf16[16,2048]{1,0:T(8,128)(2,1)S(1)}, bf16[16,2048]{1,0:T(8,128)(2,1)S(1)}, u32[]{:S(2)}, u32[]{:S(2)}) collective-permute-start(bf16[16,2048]{1,0:T(8,128)(2,1)S(1)} %get-tuple-element.15), channel_id=1, source_target_pairs={{0,4},{2,6},{4,0},{6,2},{8,12},{10,14},{12,8},{14,10},{1,5},{3,7},... | collective-permute-start | bytes 196616 | tf_op jit(solution)/shard_map/ppermute | solution.py:19
  28.3 3.4 %collective-permute-done.6.refs_1_ = bf16[16,2048]{1,0:T(8,128)(2,1)S(1)} collective-permute-done((bf16[16,2048]{1,0:T(8,128)(2,1)S(1)}, bf16[16,2048]{1,0:T(8,128)(2,1)S(1)}, u32[]{:S(2)}, u32[]{:S(2)}) %collective-permute-start.6) | collective-permute-done | bytes 65568 | tf_op jit(solution)/shard_map/ppermute | solution.py:19
  31.7 0.8 %collective-permute-done.7.refs_2_ = bf16[16,2048]{1,0:T(8,128)(2,1)S(1)} collective-permute-done((bf16[16,2048]{1,0:T(8,128)(2,1)S(1)}, bf16[16,2048]{1,0:T(8,128)(2,1)S(1)}, u32[]{:S(2)}, u32[]{:S(2)}) %collective-permute-start.7) | collective-permute-done | bytes 65568 | tf_op jit(solution)/shard_map/ppermute | solution.py:19
  32.5 0.1 collective-permute-done.8.refs_3_
  32.6 1.6 %collective-permute-start.9 = (bf16[16,2048]{1,0:T(8,128)(2,1)S(1)}, bf16[16,2048]{1,0:T(8,128)(2,1)S(1)}, u32[]{:S(2)}, u32[]{:S(2)}) collective-permute-start(bf16[16,2048]{1,0:T(8,128)(2,1)S(1)} %add.3.own_ref.x_ref), channel_id=1, source_target_pairs={{0,2},{2,0},{4,6},{6,4},{8,10},{10,8},{12,14},{14,12},{1,3},{3,1},... | collective-permute-start | bytes 196616 | tf_op jit(solution)/shard_map/ppermute | solution.py:19
  34.3 1.3 %qkv_own.1.refs_0_ = f32[16,2432]{1,0:T(8,128)S(1)} custom-call(bf16[16,2048]{1,0:T(8,128)(2,1)S(1)} %add.3.own_ref.x_ref, bf16[1,4096]{1,0:T(2,128)(2,1)S(1)} %reshape.18.g_ref, bf16[4096,2304]{1,0:T(8,128)(2,1)S(1)} %bitcast.3), custom_call_target="tpu_custom_call" | custom-call | flops 150994944 | bytes 9437184 | tf_op jit(solution)/shard_map/qkv_own/pallas_call | solution.py:283
  35.6 1.4 %collective-permute-done.9.other_ref.x_ref = bf16[16,2048]{1,0:T(8,128)(2,1)S(1)} collective-permute-done((bf16[16,2048]{1,0:T(8,128)(2,1)S(1)}, bf16[16,2048]{1,0:T(8,128)(2,1)S(1)}, u32[]{:S(2)}, u32[]{:S(2)}) %collective-permute-start.9) | collective-permute-done | bytes 65568 | tf_op jit(solution)/shard_map/ppermute | solution.py:19
  37.0 1.3 %qkv_other.1 = (f32[8,2432]{1,0:T(8,128)S(1)}, f32[8,2432]{1,0:T(8,128)S(1)}) custom-call(bf16[16,2048]{1,0:T(8,128)(2,1)S(1)} %collective-permute-done.9.other_ref.x_ref, bf16[1,4096]{1,0:T(2,128)(2,1)S(1)} %reshape.18.g_ref, bf16[4096,2304]{1,0:T(8,128)(2,1)S(1)} %bitcast.3, f32[16,2432]{1,0:T(8,128)S(1)} %qkv_own.1.refs_0_), custom_call_target="tpu_custom_call" | custom-call | flops 150994944 | bytes 9437184 | tf_op jit(solution)/shard_map/qkv_other/pallas_call | solution.py:283
  38.3 0.7 %take_rows.1 = bf16[2,4096]{1,0:T(2,128)(2,1)} custom-call(bf16[16,2048]{1,0:T(8,128)(2,1)S(1)} %add.3.own_ref.x_ref, bf16[16,2048]{1,0:T(8,128)(2,1)S(1)} %collective-permute-done.9.other_ref.x_ref), custom_call_target="tpu_custom_call" | custom-call | tf_op jit(solution)/shard_map/take_rows/pallas_call | solution.py:310
  39.1 0.5 %collective-permute-done.10.refs_1_ = f32[8,2432]{1,0:T(8,128)S(1)} collective-permute-done((f32[8,2432]{1,0:T(8,128)S(1)}, f32[8,2432]{1,0:T(8,128)S(1)}, u32[]{:S(2)}, u32[]{:S(2)}) %collective-permute-start.10) | collective-permute-done | bytes 77856 | tf_op jit(solution)/shard_map/ppermute | solution.py:19
  39.6 0.7 %finish.1 = bf16[8,2304]{1,0:T(8,128)(2,1)} custom-call(f32[8,2432]{1,0:T(8,128)S(1)} %get-tuple-element.16.refs_0_, f32[8,2432]{1,0:T(8,128)S(1)} %collective-permute-done.10.refs_1_, s32[1,2304]{1,0:T(1,128)S(1)} %reshape.19.refs_2_), custom_call_target="tpu_custom_call" | custom-call | tf_op jit(solution)/shard_map/finish/pallas_call | solution.py:333
  (26 shorter events, 0.1 us)
Async XLA Ops:
  0.6 17.5 %copy-start = (bf16[4096,4096]{1,0:T(8,128)(2,1)S(1)}, bf16[4096,4096]{1,0:T(8,128)(2,1)}, u32[]{:S(2)}) copy-start(bf16[4096,4096]{1,0:T(8,128)(2,1)} %w_ref.5) | copy-start | bytes 100663296
  0.6 17.5 %copy-start.1 = (s32[4096]{0:T(1024)S(1)}, s32[4096]{0:T(1024)}, u32[]{:S(2)}) copy-start(s32[4096]{0:T(1024)} %param.13) | copy-start | bytes 49156
  0.7 17.5 %copy-start.2 = (bf16[2,4096]{1,0:T(2,128)(2,1)S(1)}, bf16[2,4096]{1,0:T(2,128)(2,1)}, u32[]{:S(2)}) copy-start(bf16[2,4096]{1,0:T(2,128)(2,1)} %r_ref.3) | copy-start | bytes 49156
  1.8 5.2 %collective-permute-start = (bf16[8,4096]{1,0:T(8,128)(2,1)S(1)}, bf16[8,4096]{1,0:T(8,128)(2,1)S(1)}, u32[]{:S(2)}, u32[]{:S(2)}) collective-permute-start(bf16[8,4096]{1,0:T(8,128)(2,1)S(1)} %signed_units.1.own_ref), channel_id=1, source_target_pairs={{0,2},{2,0},{4,6},{6,4},{8,10},{10,8},{12,14},{14,12},{1,3},{3,1},... | collective-permute-start | bytes 196616 | tf_op jit(solution)/shard_map/ppermute | solution.py:19
  7.2 5.7 %collective-permute-start.1 = (bf16[8,4096]{1,0:T(8,128)(2,1)S(1)}, bf16[8,4096]{1,0:T(8,128)(2,1)S(1)}, u32[]{:S(2)}, u32[]{:S(2)}) collective-permute-start(bf16[8,4096]{1,0:T(8,128)(2,1)S(1)} %get-tuple-element.13), channel_id=1, source_target_pairs={{0,8},{2,10},{4,12},{6,14},{8,0},{10,2},{12,4},{14,6},{1,9},{3,11}... | collective-permute-start | bytes 196616 | tf_op jit(solution)/shard_map/ppermute | solution.py:19
  10.4 6.2 %collective-permute-start.2 = (bf16[8,4096]{1,0:T(8,128)(2,1)S(1)}, bf16[8,4096]{1,0:T(8,128)(2,1)S(1)}, u32[]{:S(2)}, u32[]{:S(2)}) collective-permute-start(bf16[8,4096]{1,0:T(8,128)(2,1)S(1)} %get-tuple-element.13), channel_id=1, source_target_pairs={{0,12},{2,14},{4,8},{6,10},{8,4},{10,6},{12,0},{14,2},{1,13},{3,15... | collective-permute-start | bytes 196616 | tf_op jit(solution)/shard_map/ppermute | solution.py:19
  11.7 5.0 %collective-permute-start.3 = (bf16[8,4096]{1,0:T(8,128)(2,1)S(1)}, bf16[8,4096]{1,0:T(8,128)(2,1)S(1)}, u32[]{:S(2)}, u32[]{:S(2)}) collective-permute-start(bf16[8,4096]{1,0:T(8,128)(2,1)S(1)} %get-tuple-element.13), channel_id=1, source_target_pairs={{0,4},{2,6},{4,0},{6,2},{8,12},{10,14},{12,8},{14,10},{1,5},{3,7},... | collective-permute-start | bytes 196616 | tf_op jit(solution)/shard_map/ppermute | solution.py:19
  16.8 1.3 %collective-permute-start.4 = (bf16[8,4096]{1,0:T(8,128)(2,1)S(1)}, bf16[8,4096]{1,0:T(8,128)(2,1)S(1)}, u32[]{:S(2)}, u32[]{:S(2)}) collective-permute-start(bf16[8,4096]{1,0:T(8,128)(2,1)S(1)} %combine.1.refs_0_), channel_id=1, source_target_pairs={{0,1},{1,0},{2,3},{3,2},{4,5},{5,4},{6,7},{7,6},{8,9},{9,8},{10,11... | collective-permute-start | bytes 196616 | tf_op jit(solution)/shard_map/ppermute | solution.py:19
  20.5 4.3 %collective-permute-start.5 = (bf16[16,2048]{1,0:T(8,128)(2,1)S(1)}, bf16[16,2048]{1,0:T(8,128)(2,1)S(1)}, u32[]{:S(2)}, u32[]{:S(2)}) collective-permute-start(bf16[16,2048]{1,0:T(8,128)(2,1)S(1)} %down_other.1), channel_id=1, source_target_pairs={{0,2},{2,0},{4,6},{6,4},{8,10},{10,8},{12,14},{14,12},{1,3},{3,1},... | collective-permute-start | bytes 196616 | tf_op jit(solution)/shard_map/ppermute | solution.py:19
  22.0 12.2 %slice-start = ((s8[18874368]{0:T(1024)(128)(4,1)}), s8[2097152]{0:T(1024)(128)(4,1)S(1)}, s32[]{:S(2)}) async-start(s8[18874368]{0:T(1024)(128)(4,1)} %bitcast.2), calls=%async_computation | async-start | bytes 4194304
  24.2 9.9 %copy-start.4 = (bf16[4096]{0:T(1024)(128)(2,1)S(1)}, bf16[4096]{0:T(1024)(128)(2,1)}, u32[]{:S(2)}) copy-start(bf16[4096]{0:T(1024)(128)(2,1)} %param.15) | copy-start | bytes 24580
  24.2 10.0 %slice-start.1 = ((s8[18874368]{0:T(1024)(128)(4,1)}), s8[4194304]{0:T(1024)(128)(4,1)S(1)}, s32[]{:S(2)}) async-start(s8[18874368]{0:T(1024)(128)(4,1)} %bitcast.2), calls=%async_computation.1 | async-start | bytes 8388608
  24.3 10.0 %slice-start.2 = ((s8[18874368]{0:T(1024)(128)(4,1)}), s8[4194304]{0:T(1024)(128)(4,1)S(1)}, s32[]{:S(2)}) async-start(s8[18874368]{0:T(1024)(128)(4,1)} %bitcast.2), calls=%async_computation.2 | async-start | bytes 8388608
  24.3 10.0 %slice-start.3 = ((s8[18874368]{0:T(1024)(128)(4,1)}), s8[4194304]{0:T(1024)(128)(4,1)S(1)}, s32[]{:S(2)}) async-start(s8[18874368]{0:T(1024)(128)(4,1)} %bitcast.2), calls=%async_computation.3 | async-start | bytes 8388608
  24.3 10.0 %slice-start.4 = ((s8[18874368]{0:T(1024)(128)(4,1)}), s8[4194304]{0:T(1024)(128)(4,1)S(1)}, s32[]{:S(2)}) async-start(s8[18874368]{0:T(1024)(128)(4,1)} %bitcast.2), calls=%async_computation.4 | async-start | bytes 8388608
  24.8 13.6 %copy-start.3 = (s32[2304]{0:T(1024)S(1)}, s32[2304]{0:T(1024)}, u32[]{:S(2)}) copy-start(s32[2304]{0:T(1024)} %param.17) | copy-start | bytes 27652
  24.8 6.9 %collective-permute-start.6 = (bf16[16,2048]{1,0:T(8,128)(2,1)S(1)}, bf16[16,2048]{1,0:T(8,128)(2,1)S(1)}, u32[]{:S(2)}, u32[]{:S(2)}) collective-permute-start(bf16[16,2048]{1,0:T(8,128)(2,1)S(1)} %get-tuple-element.15), channel_id=1, source_target_pairs={{0,8},{2,10},{4,12},{6,14},{8,0},{10,2},{12,4},{14,6},{1,9},{3,11}... | collective-permute-start | bytes 196616 | tf_op jit(solution)/shard_map/ppermute | solution.py:19
  26.3 6.2 %collective-permute-start.7 = (bf16[16,2048]{1,0:T(8,128)(2,1)S(1)}, bf16[16,2048]{1,0:T(8,128)(2,1)S(1)}, u32[]{:S(2)}, u32[]{:S(2)}) collective-permute-start(bf16[16,2048]{1,0:T(8,128)(2,1)S(1)} %get-tuple-element.15), channel_id=1, source_target_pairs={{0,12},{2,14},{4,8},{6,10},{8,4},{10,6},{12,0},{14,2},{1,13},{3,15... | collective-permute-start | bytes 196616 | tf_op jit(solution)/shard_map/ppermute | solution.py:19
  27.2 5.4 %collective-permute-start.8 = (bf16[16,2048]{1,0:T(8,128)(2,1)S(1)}, bf16[16,2048]{1,0:T(8,128)(2,1)S(1)}, u32[]{:S(2)}, u32[]{:S(2)}) collective-permute-start(bf16[16,2048]{1,0:T(8,128)(2,1)S(1)} %get-tuple-element.15), channel_id=1, source_target_pairs={{0,4},{2,6},{4,0},{6,2},{8,12},{10,14},{12,8},{14,10},{1,5},{3,7},... | collective-permute-start | bytes 196616 | tf_op jit(solution)/shard_map/ppermute | solution.py:19
  32.6 4.3 %collective-permute-start.9 = (bf16[16,2048]{1,0:T(8,128)(2,1)S(1)}, bf16[16,2048]{1,0:T(8,128)(2,1)S(1)}, u32[]{:S(2)}, u32[]{:S(2)}) collective-permute-start(bf16[16,2048]{1,0:T(8,128)(2,1)S(1)} %add.3.own_ref.x_ref), channel_id=1, source_target_pairs={{0,2},{2,0},{4,6},{6,4},{8,10},{10,8},{12,14},{14,12},{1,3},{3,1},... | collective-permute-start | bytes 196616 | tf_op jit(solution)/shard_map/ppermute | solution.py:19
  38.3 1.3 %collective-permute-start.10 = (f32[8,2432]{1,0:T(8,128)S(1)}, f32[8,2432]{1,0:T(8,128)S(1)}, u32[]{:S(2)}, u32[]{:S(2)}) collective-permute-start(f32[8,2432]{1,0:T(8,128)S(1)} %get-tuple-element.17), channel_id=1, source_target_pairs={{0,1},{1,0},{2,3},{3,2},{4,5},{5,4},{6,7},{7,6},{8,9},{9,8},{10,11... | collective-permute-start | bytes 233480 | tf_op jit(solution)/shard_map/ppermute | solution.py:19
